TPU v7x, 512 devices: a whole 4x8x8 slice. The times are simulated.
512 devices in a mesh: lat: 4 (over z_hi), lon: 4 (over x), day: 32 (over z_lo, y, core).
Axes of the slice: x: 4, y: 8, z: 8 (z_hi: 4, z_lo: 2; z = z_hi * 2 + z_lo), core: 2. Of those that a mesh axis runs over, the one named last changes fastest.
Arguments:
- anomaly: float32 [256, 256, 4096], P('lat', 'lon', 'day'), may hold values from -6 to 6
- observed: int32 [256, 256, 4096], P('lat', 'lon', 'day'), may hold values 0 or 1
- ocean_mask: int32 [256, 256], P('lat', 'lon'), may hold values 0 or 1
- start_days: float32 [4096, 128], P('day'), may hold values from -0.09375 to 0.09375
Outputs:
- spatial: float32 [256, 256, 128], P('lat', 'lon')
- temporal: float32 [4096, 128], P('day')
Inputs may be any that keep to these rules, and one draw needn't show every extreme that they name: 1 marks an observed value, 0 a gap. `ocean_mask`: 1 marks ocean, 0 land.
All inputs are finite; a program needn't handle non-finite values. No bound on the sum of `observed` or of `ocean_mask` on one device may be relied on, other than what follows from the above.
Results may differ from a plain program's by a relative error of at most 0.0003.
Values sent between devices are 32-bit elements; how exact they have to be, the bound alone decides.
No kernel may reach another device: no remote copies, remote signals or barrier semaphores. Data moves between devices by JAX's collectives and lax.ppermute only.
A program may use at most 64 MiB of HBM per device.

v0:
```python
import functools
import math

import jax
import jax.numpy as jnp
from jax import lax
from jax.experimental import pallas as pl
from jax.experimental.pallas import tpu as pltpu
from jax.sharding import Mesh, PartitionSpec as P

ITERS = 2


ridge_term = 1.0
diffusion = 0.1
lat_south = 30.0
lat_span = 16.0

GAP = 1e30
YZ = ("zlo", "y")
DAY = ("zlo", "y", "core")
ALL = ("lat", "lon", "zlo", "y", "core")
LL = ("lat", "lon")
f32, bf16 = jnp.float32, jnp.bfloat16


def inverse_spd(matrix):
    size = matrix.shape[0]
    blocks = [matrix[8 * r : 8 * r + 8] for r in range(size // 8)]
    lane = lax.broadcasted_iota(jnp.int32, (1, size), 1)
    row = lax.broadcasted_iota(jnp.int32, (8, size), 0)
    for k in range(0, size, 4):
        home, off = k // 8, k % 8
        rows = [blocks[home][off + i : off + i + 1] for i in range(4)]
        d = [[jnp.broadcast_to(rows[i][:, k + j : k + j + 1], (1, size)) for j in range(4)] for i in range(4)]
        in_panel = (lane >= k) & (lane < k + 4)
        a, b, c = d[0][0], d[0][1], d[1][1]
        r = 1.0 / (a * c - b * b)
        a00, a01, a11 = c * r, -b * r, a * r
        b02, b03, b12, b13 = d[0][2], d[0][3], d[1][2], d[1][3]
        g02, g03 = a00 * b02 + a01 * b12, a00 * b03 + a01 * b13
        g12, g13 = a01 * b02 + a11 * b12, a01 * b03 + a11 * b13
        s22 = d[2][2] - (b02 * g02 + b12 * g12)
        s23 = d[2][3] - (b02 * g03 + b12 * g13)
        s33 = d[3][3] - (b03 * g03 + b13 * g13)
        r = 1.0 / (s22 * s33 - s23 * s23)
        i22, i23, i33 = s33 * r, -s23 * r, s22 * r
        h02, h03 = g02 * i22 + g03 * i23, g02 * i23 + g03 * i33
        h12, h13 = g12 * i22 + g13 * i23, g12 * i23 + g13 * i33
        q00 = a00 + (h02 * g02 + h03 * g03)
        q01 = a01 + (h02 * g12 + h03 * g13)
        q11 = a11 + (h12 * g12 + h13 * g13)
        inv = [[q00, q01, -h02, -h03], [q01, q11, -h12, -h13], [-h02, -h12, i22, i23], [-h03, -h13, i23, i33]]
        unit = [jnp.where(lane == k + j, 1.0, jnp.where(in_panel, 0.0, rows[j])) for j in range(4)]
        new = [
            (inv[i][0] * unit[0] + inv[i][1] * unit[1]) + (inv[i][2] * unit[2] + inv[i][3] * unit[3])
            for i in range(4)
        ]
        out = []
        for r8, block in enumerate(blocks):
            cols = [block[:, k + j : k + j + 1] for j in range(4)]
            keep = jnp.where(in_panel, 0.0, block)
            keep = keep - ((cols[0] * new[0] + cols[1] * new[1]) + (cols[2] * new[2] + cols[3] * new[3]))
            if r8 == home:
                for j in range(4):
                    keep = jnp.where(row == off + j, new[j], keep)
            out.append(keep)
        blocks = out
    return jnp.concatenate(blocks, axis=0)


def add_ridge(gram):
    size = gram.shape[0]
    same = lax.broadcasted_iota(jnp.int32, (size, size), 0) == lax.broadcasted_iota(jnp.int32, (size, size), 1)
    return gram + jnp.where(same, ridge_term, 0.0)


def split(value):
    one = value.astype(bf16)
    rest = value - one.astype(f32)
    two = rest.astype(bf16)
    three = (rest - two.astype(f32)).astype(bf16)
    return one, two, three


def right_side(value):
    one, two, three = split(value)
    wide = jnp.concatenate([one, two], axis=1)
    return jnp.concatenate([wide, wide], axis=0), jnp.concatenate([three, one], axis=0)


def times(parts, side):
    one, two, three = parts
    wide = jnp.dot(jnp.concatenate([one, two], axis=1), side[0], preferred_element_type=f32)
    tail = jnp.dot(jnp.concatenate([one, three], axis=1), side[1], preferred_element_type=f32)
    n = tail.shape[1]
    return wide[:, :n] + (wide[:, n:] + tail)


def dot_tn(left, right):
    return lax.dot_general(left, right, (((0,), (0,)), ((), ())), preferred_element_type=f32)


def full(left, right, dims=(((1,), (0,)), ((), ()))):
    return lax.dot_general(left, right, dims, precision=lax.Precision.HIGHEST, preferred_element_type=f32)


def put_block(core_ref, grid_ref, gram, mine_ref, other_ref):
    core = core_ref[0, 0]
    lats, lons, modes = grid_ref.shape
    spokes = mine_ref.shape[0]
    per = lats // (2 * spokes)
    cells = per * lons

    def edge(half, q):
        half_spokes = spokes // 2
        at = 8 * (q % half_spokes)
        far = q >= half_spokes
        if half == 0:
            return grid_ref[lats - 1 if far else 0, at : at + 8, :]
        return grid_ref[at : at + 8, lons - 1 if far else 0, :]

    for half in range(2):
        for which, ref in ((half, mine_ref), (1 - half, other_ref)):

            @pl.when(core == which)
            def _():
                for q in range(spokes):
                    ref[q, cells : cells + 8, :] = edge(half, q)
                    ref[q, cells + 8 : cells + 16, :] = gram[8 * q : 8 * q + 8]


def first_kernel(core_ref, anomaly_ref, observed_ref, seat_ref, days_ref, mine_ref, other_ref, coded_ref, sea_ref, grid_ref):
    core = core_ref[0, 0]
    lats, lons, days = anomaly_ref.shape
    spokes = mine_ref.shape[0]
    per = lats // (2 * spokes)
    temporal = days_ref[...]
    side = right_side(temporal)
    gram = full(temporal, temporal, (((0,), (0,)), ((), ())))
    seat = seat_ref[...]

    for half, ref in ((core, mine_ref), (1 - core, other_ref)):

        def step(q, _):
            rows = []
            for p in range(per):
                i = half * (lats // 2) + q * per + p
                sea = jnp.broadcast_to(pltpu.roll(seat, lax.rem(seat.shape[1] - i, seat.shape[1]), 1)[:, :1], (lons, days))
                sea_ref[i] = sea
                seen = observed_ref[i] != 0
                known = jnp.where(seen, sea * anomaly_ref[i], 0.0)
                coded_ref[i] = jnp.where(seen | (sea == 0.0), known, GAP)
                rows.append(known)
            out = times(split(jnp.concatenate(rows, axis=0)), side)
            ref[q, 0 : per * lons, :] = out
            for p in range(per):
                grid_ref[half * (lats // 2) + q * per + p] = out[p * lons : (p + 1) * lons]
            return _

        lax.fori_loop(0, spokes, step, 0, unroll=2)
    put_block(core_ref, grid_ref, gram, mine_ref, other_ref)


def modes_kernel(first, core_ref, weight_ref, here_ref, there_ref, days_ref, coded_ref, field_ref, *refs):
    if first:
        spatial_ref, sums_ref, around_ref, pad_ref, rim_ref, wide_ref, tail_ref = refs
    else:
        spatial_ref, sums_ref, pad_ref, rim_ref, wide_ref, tail_ref = refs
    core = core_ref[0, 0]
    lats, lons, modes = coded_ref.shape
    days = modes
    spokes = here_ref.shape[0]
    per = lats // (2 * spokes)
    cells = per * lons
    tiles = 2 if first else 1
    gram_at = cells + 8 * tiles

    for half, ref in ((core, here_ref), (1 - core, there_ref)):

        def fill(q, _):
            base = half * (lats // 2) + q * per
            for p in range(per):
                pad_ref[base + p + 1] = ref[q, p * lons : (p + 1) * lons, :]
            at = half * 2 * lons + q * 8
            for t in range(tiles):
                rim_ref[pl.ds(pl.multiple_of(t * 4 * lons + at, 8), 8), :] = ref[q, cells + 8 * t : cells + 8 * t + 8, :]
            return _

        lax.fori_loop(0, spokes, fill, 0)
    pad_ref[0] = rim_ref[lons : 2 * lons, :]
    pad_ref[lats + 1] = rim_ref[0:lons, :]
    gram = jnp.concatenate([here_ref[q, gram_at : gram_at + 8, :] for q in range(spokes)], axis=0)
    inverse_side = right_side(inverse_spd(add_ridge(gram)))
    days_side = right_side(days_ref[...].T)
    row = lax.broadcasted_iota(jnp.int32, (lons, modes), 0)
    wide_ref[...] = jnp.zeros_like(wide_ref)
    tail_ref[...] = jnp.zeros_like(tail_ref)

    def beside(value, i, kind):
        east = rim_ref[pl.ds(kind * 4 * lons + 2 * lons + i, 1), :]
        west = rim_ref[pl.ds(kind * 4 * lons + 3 * lons + i, 1), :]
        ahead = jnp.where(row == lons - 1, east, pltpu.roll(value, lons - 1, 0))
        behind = jnp.where(row == 0, west, pltpu.roll(value, 1, 0))
        return ahead + behind

    if first:

        def masks(i, _):
            sea = field_ref[i]
            north = jnp.where(i == 0, rim_ref[5 * lons : 6 * lons, :], field_ref[jnp.maximum(i - 1, 0)])
            south = jnp.where(i == lats - 1, rim_ref[4 * lons : 5 * lons, :], field_ref[jnp.minimum(i + 1, lats - 1)])
            round_ = (north + south) + weight_ref[0, i] * beside(sea, i, 1)
            around_ref[i] = jnp.where(sea == 0.0, GAP, 1.0 - diffusion * round_)
            return _

        lax.fori_loop(0, lats, masks, 0)
    around_in = around_ref if first else field_ref

    group = 4

    def step(g, _):
        smoothed = []
        for p in range(group):
            i = g * group + p
            around = around_in[i]
            raw = pad_ref[i + 1]
            near = (pad_ref[i] + pad_ref[i + 2]) + weight_ref[0, i] * beside(raw, i, 0)
            smoothed.append(jnp.where(around == GAP, 0.0, around * raw + diffusion * near))
        spatial = times(split(jnp.concatenate(smoothed, axis=0)), inverse_side)
        parts = split(spatial)
        guess = times(parts, days_side)
        filled = []
        for p in range(group):
            i = g * group + p
            spatial_ref[i] = spatial[p * lons : (p + 1) * lons]
            coded = coded_ref[i]
            filled.append(jnp.where(coded == GAP, guess[p * lons : (p + 1) * lons], coded))
        f1, f2, f3 = split(jnp.concatenate(filled, axis=0))
        s1, s2, s3 = parts
        wide_ref[...] += dot_tn(jnp.concatenate([f1, f2, s1, s2], axis=1), jnp.concatenate([s1, s2], axis=1))
        tail_ref[...] += dot_tn(
            jnp.concatenate([jnp.concatenate([f1, s1], axis=1), jnp.concatenate([f3, s3], axis=1)], axis=0),
            jnp.concatenate([s3, s1], axis=0),
        )
        return _

    lax.fori_loop(0, lats // group, step, 0)
    n = modes
    for part in range(2):
        at = 2 * part * n
        wide = wide_ref[at : at + n, :] + wide_ref[at + n : at + 2 * n, :]
        sums_ref[part * n : (part + 1) * n, :] = (wide[:, :n] + wide[:, n:]) + tail_ref[part * n : (part + 1) * n, :]


def days_kernel(core_ref, sums_ref, coded_ref, spatial_ref, mine_ref, other_ref, days_ref, grid_ref):
    core = core_ref[0, 0]
    lats, lons, modes = coded_ref.shape
    days = sums_ref.shape[0] - modes
    spokes = mine_ref.shape[0]
    per = lats // (2 * spokes)
    temporal = full(sums_ref[0:days, :], inverse_spd(add_ridge(sums_ref[days:, :])))
    days_ref[...] = temporal
    side = right_side(temporal)
    across = right_side(temporal.T)
    gram = full(temporal, temporal, (((0,), (0,)), ((), ())))

    for half, ref in ((core, mine_ref), (1 - core, other_ref)):

        def step(q, _):
            base = half * (lats // 2) + q * per
            guess = times(split(jnp.concatenate([spatial_ref[base + p] for p in range(per)], axis=0)), across)
            coded = jnp.concatenate([coded_ref[base + p] for p in range(per)], axis=0)
            out = times(split(jnp.where(coded == GAP, guess, coded)), side)
            ref[q, 0 : per * lons, :] = out
            for p in range(per):
                grid_ref[base + p] = out[p * lons : (p + 1) * lons]
            return _

        lax.fori_loop(0, spokes, step, 0, unroll=2)
    put_block(core_ref, grid_ref, gram, mine_ref, other_ref)


def last_kernel(sums_ref, days_ref):
    days = days_ref.shape[0]
    days_ref[...] = full(sums_ref[0:days, :], inverse_spd(add_ridge(sums_ref[days:, :])))


SMEM = pl.BlockSpec(memory_space=pltpu.SMEM)
VMEM = pl.BlockSpec(memory_space=pltpu.VMEM)


def call(kernel, outs, specs, scratch, name, flops, nbytes):
    return pl.pallas_call(
        kernel,
        out_shape=[jax.ShapeDtypeStruct(shape, f32) for shape in outs],
        in_specs=specs,
        out_specs=[VMEM] * len(outs),
        scratch_shapes=[pltpu.VMEM(shape, f32) for shape in scratch],
        name=name,
        cost_estimate=pl.CostEstimate(flops=flops, bytes_accessed=nbytes, transcendentals=0),
        compiler_params=pltpu.CompilerParams(vmem_limit_bytes=40 * 1024 * 1024),
    )


def first_call(core, anomaly, observed, seat, days, spokes):
    lats, lons, n = anomaly.shape
    block = (spokes, lats * lons // (2 * spokes) + 16, n)
    grid = (lats, lons, n)
    return call(first_kernel, [block, block, grid, grid], [SMEM] + [VMEM] * 4, [grid], "first_projection", 10**9, 10**7)(
        core, anomaly, observed, seat, days
    )


def modes_call(first, core, weight, here, there, days, coded, field):
    lats, lons, n = coded.shape
    grid = (lats, lons, n)
    outs = [grid, (2 * n, n)] + ([grid] if first else [])
    scratch = [(lats + 2, lons, n), ((8 if first else 4) * lons, n), (4 * n, 2 * n), (2 * n, n)]
    return call(functools.partial(modes_kernel, first), outs, [SMEM, SMEM] + [VMEM] * 5, scratch, "modes_sweep", 2 * 10**9, 10**7)(
        core, weight, here, there, days, coded, field
    )


def days_call(core, sums, coded, spatial, spokes):
    lats, lons, n = coded.shape
    block = (spokes, lats * lons // (2 * spokes) + 16, n)
    return call(days_kernel, [block, block, (sums.shape[0] - n, n)], [SMEM] + [VMEM] * 3, [(lats, lons, n)], "days_sweep", 2 * 10**9, 10**7)(
        core, sums, coded, spatial
    )


def last_call(sums):
    n = sums.shape[1]
    return call(last_kernel, [(sums.shape[0] - n, n)], [VMEM], [], "last_days", 10**7, 10**6)(sums)[0]


def lat_weights(first_row, row_count, total_rows):
    index_rows = first_row + jnp.arange(row_count, dtype=jnp.float32)
    angle = (lat_south + lat_span * (index_rows + 0.5) / total_rows) * (math.pi / 180.0)
    cosine = jnp.cos(angle)
    return 1.0 / (cosine * cosine)


def swap_core(value):
    return lax.ppermute(value, "core", [(0, 1), (1, 0)])


def halo_pairs(lats, lons, spokes):
    pairs = []
    for la in range(lats):
        for lo in range(lons):
            for q in range(spokes):
                for core in range(2):
                    step = -1 if q < spokes // 2 else 1
                    to_la, to_lo = (la + step, lo) if core == 0 else (la, lo + step)
                    if 0 <= to_la < lats and 0 <= to_lo < lons:
                        here = ((la * lons + lo) * spokes + q) * 2 + core
                        there = ((to_la * lons + to_lo) * spokes + q) * 2 + core
                        pairs.append((here, there))
    return pairs


def gather_all(value, axes, size):
    spread = jnp.broadcast_to(value[None], (size,) + value.shape)
    return lax.all_to_all(spread, axes, 0, 0, tiled=True)


def sum_cells(value):
    size = lax.axis_size("lat") * lax.axis_size("lon")
    rows = value.shape[0]
    parts = lax.all_to_all(value.reshape(size, rows // size, -1), LL, 0, 0, tiled=True)
    mine = jnp.sum(parts, axis=0)
    return gather_all(mine, LL, size).reshape(rows, -1)


def edges_of(grid):
    return jnp.concatenate([grid[0], grid[-1], grid[:, 0], grid[:, -1]], axis=0)


def on_device(anomaly, observed, ocean_mask, start_days):
    rows_lat, cols_lon, _ = anomaly.shape
    rank_count = start_days.shape[1]
    lats, lons = lax.axis_size("lat"), lax.axis_size("lon")
    spokes = lax.axis_size("zlo") * lax.axis_size("y")
    core = lax.axis_index("core")
    spoke = lax.axis_index("zlo") * lax.axis_size("y") + lax.axis_index("y")
    pairs = halo_pairs(lats, lons, spokes)
    cells = rows_lat * cols_lon // (2 * spokes)
    core_word = core.reshape(1, 1).astype(jnp.int32)
    sea_grid = ocean_mask.astype(f32)
    seat = jnp.pad(sea_grid.T, ((0, 0), (0, rank_count - rows_lat)))
    first_lat = (lax.axis_index("lat") * rows_lat).astype(f32)
    weight = lat_weights(first_lat, rows_lat, float(rows_lat * lats)).reshape(1, rows_lat)
    edge_sea = lax.dynamic_slice_in_dim(edges_of(sea_grid), (core * spokes + spoke) * 8, 8)
    edge_sea = jnp.broadcast_to(edge_sea[:, None], (8, rank_count))
    temporal = start_days
    mine, other, coded, field = first_call(core_word, anomaly, observed, seat, start_days, spokes)
    for sweep in range(ITERS):
        half = mine + swap_core(other)
        shard = jnp.sum(lax.all_to_all(half, YZ, 0, 0, tiled=True), axis=0)
        send = shard[cells : cells + 8]
        if sweep == 0:
            send = jnp.concatenate([send, edge_sea], axis=0)
        halo = lax.ppermute(send, ALL, pairs)
        shard = jnp.concatenate([shard[:cells], halo, shard[cells + 8 :]], axis=0)
        here = gather_all(shard, YZ, spokes)
        there = swap_core(here)
        out = modes_call(sweep == 0, core_word, weight, here, there, temporal, coded, field)
        spatial, sums = out[0], sum_cells(out[1])
        if sweep == 0:
            field = out[2]
        if sweep < ITERS - 1:
            mine, other, temporal = days_call(core_word, sums, coded, spatial, spokes)
        else:
            temporal = last_call(sums)
    return (spatial, temporal)


def solution(mesh):
    lats, lons, days = mesh.devices.shape
    fine = Mesh(mesh.devices.reshape(lats, lons, 2, days // 4, 2), ALL)
    in_specs = (P("lat", "lon", DAY), P("lat", "lon", DAY), P("lat", "lon"), P(DAY, None))
    out_specs = (P("lat", "lon", None), P(DAY, None))
    return jax.shard_map(
        on_device, mesh=fine, in_specs=in_specs, out_specs=out_specs, check_vma=False
    )
```

profile of v0, /device:TPU:8, one launch (start us, length us, event | category | flops | bytes accessed | tf_op | source)
XLA Modules:
  0.0 314.6 jit_solution(5713692649219091059)
XLA Ops:
  0.6 0.8 copy.7
  1.5 0.0 copy-start
  1.5 1.6 copy-done
  3.1 1.6 copy-done.1
  4.7 0.8 copy-done.2
  5.5 6.6 %first_projection.1 = (f32[16,144,128]{2,1,0:T(8,128)S(1)}, f32[16,144,128]{2,1,0:T(8,128)S(1)}, f32[64,64,128]{2,1,0:T(8,128)S(1)}, f32[64,64,128]{2,1,0:T(8,128)S(1)}) custom-call(s32[1,1]{1,0:T(1,128)} %bitcast.core_ref, f32[64,64,128]{2,1,0:T(8,128)S(1)} %copy-done, s32[64,64,128]{2,1,0:T(8,128)S(1)} %copy-done.1, f32[64,128]{1,0:T(8,128)S(1)} %pad.4.seat_ref, ...), custom_call_target="tpu_custom_call" | custom-call | flops 1000000000 | bytes 10000000 | tf_op jit(solution)/shard_map/first_projection/pallas_call | solution.py:310
  12.2 1.3 copy-done.4
  13.5 1.9 collective-permute-start
  15.4 2.8 collective-permute-done
  18.2 1.1 add.62
  19.3 9.4 %all-to-all-start = ((f32[16,144,128]{2,1,0:T(8,128)}), f32[16,144,128]{2,1,0:T(8,128)S(1)}, u32[]{:S(2)}, u32[]{:S(2)}) async-start(f32[16,144,128]{2,1,0:T(8,128)} %add.62), calls=%async_computation | async-start | bytes 2359296 | tf_op jit(solution)/shard_map/all_to_all | solution.py:401
  28.7 0.2 slice_reduce_fusion.1
  28.9 0.1 pad_maximum_fusion.3
  29.0 0.1 dynamic_slice.3
  29.1 0.1 pad.12.clone
  29.1 29.1 %all-to-all-done = f32[16,144,128]{2,1,0:T(8,128)S(1)} async-done(((f32[16,144,128]{2,1,0:T(8,128)}), f32[16,144,128]{2,1,0:T(8,128)S(1)}, u32[]{:S(2)}, u32[]{:S(2)}) %all-to-all-start) | async-done | bytes 1179680 | tf_op jit(solution)/shard_map/all_to_all | solution.py:401
  58.3 0.1 reduce_sum.36
  58.4 0.1 pad_maximum_fusion.2
  58.4 1.3 collective-permute-start.1
  59.7 6.2 %collective-permute-done.1 = f32[16,128]{1,0:T(8,128)S(1)} collective-permute-done((f32[16,128]{1,0:T(8,128)S(1)}, f32[16,128]{1,0:T(8,128)S(1)}, u32[]{:S(2)}, u32[]{:S(2)}) %collective-permute-start.1) | collective-permute-done | bytes 8224 | tf_op jit(solution)/shard_map/ppermute | solution.py:405
  65.9 0.1 broadcast_in_dim.11
  66.0 33.2 %all_to_all.40.here_ref = f32[16,152,128]{2,1,0:T(8,128)S(1)} all-to-all(f32[16,152,128]{2,1,0:T(8,128)S(1)} %broadcast_in_dim.11), channel_id=1, replica_groups=mesh['lat'=4,'lon'=4,'zlo'=2,'y'=8,'core'=2] {'zlo','y'}, dimensions={0} | all-to-all | bytes 2490368 | tf_op jit(solution)/shard_map/all_to_all | solution.py:366
  99.2 1.9 collective-permute-start.2
  101.1 0.1 multiply_divide_fusion.weight_ref
  101.2 3.0 collective-permute-done.2.there_ref
  104.2 1.6 copy-done.5
  105.7 19.5 %modes_sweep.2 = (f32[64,64,128]{2,1,0:T(8,128)S(1)}, f32[256,128]{1,0:T(8,128)S(1)}, f32[64,64,128]{2,1,0:T(8,128)S(1)}) custom-call(s32[1,1]{1,0:T(1,128)} %bitcast.core_ref, f32[1,64]{1,0:T(1,128)S(1)} %multiply_divide_fusion.weight_ref, f32[16,152,128]{2,1,0:T(8,128)S(1)} %all_to_all.40.here_ref, f32[16,152,128]{2,1,0:T(8,128)} %collective-permute-done.2.there_ref, ...), custom_call_target="tpu_custom_call" | custom-call | flops 2000000000 | bytes 10000000 | tf_op jit(solution)/shard_map/modes_sweep/pallas_call | solution.py:320
  125.3 1.3 copy-done.6
  126.6 1.3 copy-done.8
  127.9 22.9 %all_to_all.41 = f32[16,16,128]{2,1,0:T(8,128)S(1)} all-to-all(f32[16,16,128]{2,1,0:T(8,128)S(1)} %bitcast.13), channel_id=1, replica_groups=mesh['lat'=4,'lon'=4,'zlo'=2,'y'=8,'core'=2] {'lat','lon'}, dimensions={0} | all-to-all | bytes 262144 | tf_op jit(solution)/shard_map/all_to_all | solution.py:372
  150.9 13.3 %all_to_all.42 = f32[16,16,128]{2,1,0:T(8,128)S(1)} all-to-all(f32[16,16,128]{2,1,0:T(8,128)S(1)} %broadcast_in_dim.12), channel_id=1, replica_groups=mesh['lat'=4,'lon'=4,'zlo'=2,'y'=8,'core'=2] {'lat','lon'}, dimensions={0} | all-to-all | bytes 262144 | tf_op jit(solution)/shard_map/all_to_all | solution.py:366
  164.2 1.6 copy-done.9
  165.8 14.1 %days_sweep.1 = (f32[16,144,128]{2,1,0:T(8,128)S(1)}, f32[16,144,128]{2,1,0:T(8,128)S(1)}, f32[128,128]{1,0:T(8,128)S(1)}) custom-call(s32[1,1]{1,0:T(1,128)} %bitcast.core_ref, f32[256,128]{1,0:T(8,128)S(1)} %bitcast.14, f32[64,64,128]{2,1,0:T(8,128)S(1)} %get-tuple-element.16.coded_ref, f32[64,64,128]{2,1,0:T(8,128)S(1)} %copy-done.9), custom_call_target="tpu_custom_call" | custom-call | flops 2000000000 | bytes 10000000 | tf_op jit(solution)/shard_map/days_sweep/pallas_call | solution.py:328
  179.9 2.1 collective-permute-start.3
  182.0 2.6 collective-permute-done.3
  184.7 0.1 add.66
  184.8 35.1 %all_to_all.43 = f32[16,144,128]{2,1,0:T(8,128)S(1)} all-to-all(f32[16,144,128]{2,1,0:T(8,128)S(1)} %add.66), channel_id=1, replica_groups=mesh['lat'=4,'lon'=4,'zlo'=2,'y'=8,'core'=2] {'zlo','y'}, dimensions={0} | all-to-all | bytes 2359296 | tf_op jit(solution)/shard_map/all_to_all | solution.py:401
  219.9 0.1 reduce_sum.38
  220.0 1.3 collective-permute-start.4
  221.3 5.1 %collective-permute-done.4 = f32[8,128]{1,0:T(8,128)S(1)} collective-permute-done((f32[8,128]{1,0:T(8,128)S(1)}, f32[8,128]{1,0:T(8,128)S(1)}, u32[]{:S(2)}, u32[]{:S(2)}) %collective-permute-start.4) | collective-permute-done | bytes 4128 | tf_op jit(solution)/shard_map/ppermute | solution.py:405
  226.4 0.1 broadcast_in_dim.13
  226.5 31.4 %all_to_all.44.here_ref = f32[16,144,128]{2,1,0:T(8,128)S(1)} all-to-all(f32[16,144,128]{2,1,0:T(8,128)S(1)} %broadcast_in_dim.13), channel_id=1, replica_groups=mesh['lat'=4,'lon'=4,'zlo'=2,'y'=8,'core'=2] {'zlo','y'}, dimensions={0} | all-to-all | bytes 2359296 | tf_op jit(solution)/shard_map/all_to_all | solution.py:366
  257.9 1.9 collective-permute-start.5
  259.8 2.8 collective-permute-done.5.there_ref
  262.6 18.1 %modes_sweep.3 = (f32[64,64,128]{2,1,0:T(8,128)}, f32[256,128]{1,0:T(8,128)S(1)}) custom-call(s32[1,1]{1,0:T(1,128)} %bitcast.core_ref, f32[1,64]{1,0:T(1,128)S(1)} %multiply_divide_fusion.weight_ref, f32[16,144,128]{2,1,0:T(8,128)S(1)} %all_to_all.44.here_ref, f32[16,144,128]{2,1,0:T(8,128)S(1)} %collective-permute-done.5.there_ref, ...), custom_call_target="tpu_custom_call" | custom-call | flops 2000000000 | bytes 10000000 | tf_op jit(solution)/shard_map/modes_sweep/pallas_call | solution.py:320
  280.7 14.2 %all_to_all.45 = f32[16,16,128]{2,1,0:T(8,128)S(1)} all-to-all(f32[16,16,128]{2,1,0:T(8,128)S(1)} %bitcast.12), channel_id=1, replica_groups=mesh['lat'=4,'lon'=4,'zlo'=2,'y'=8,'core'=2] {'lat','lon'}, dimensions={0} | all-to-all | bytes 262144 | tf_op jit(solution)/shard_map/all_to_all | solution.py:372
  295.0 13.7 %all_to_all.46 = f32[16,16,128]{2,1,0:T(8,128)S(1)} all-to-all(f32[16,16,128]{2,1,0:T(8,128)S(1)} %broadcast_in_dim.14), channel_id=1, replica_groups=mesh['lat'=4,'lon'=4,'zlo'=2,'y'=8,'core'=2] {'lat','lon'}, dimensions={0} | all-to-all | bytes 262144 | tf_op jit(solution)/shard_map/all_to_all | solution.py:366
  308.7 5.9 %last_days.1 = f32[128,128]{1,0:T(8,128)} custom-call(f32[256,128]{1,0:T(8,128)S(1)} %bitcast.11), custom_call_target="tpu_custom_call" | custom-call | flops 10000000 | bytes 1000000 | tf_op jit(solution)/shard_map/last_days/pallas_call | solution.py:335
  (24 shorter events, 0.1 us)
Async XLA Ops:
  1.5 1.6 copy-start
  3.1 1.6 copy-start.1
  4.7 0.8 copy-start.2
  12.1 1.3 copy-start.4
  13.5 4.7 %collective-permute-start = (f32[16,144,128]{2,1,0:T(8,128)S(1)}, f32[16,144,128]{2,1,0:T(8,128)S(1)}, u32[]{:S(2)}, u32[]{:S(2)}) collective-permute-start(f32[16,144,128]{2,1,0:T(8,128)S(1)} %get-tuple-element.15), channel_id=1, source_target_pairs={{0,1},{1,0},{2,3},{3,2},{4,5},{5,4},{6,7},{7,6},{8,9},{9,8},{10,11... | collective-permute-start | bytes 3538952 | tf_op jit(solution)/shard_map/ppermute | solution.py:346
  19.3 38.9 %all-to-all-start = ((f32[16,144,128]{2,1,0:T(8,128)}), f32[16,144,128]{2,1,0:T(8,128)S(1)}, u32[]{:S(2)}, u32[]{:S(2)}) async-start(f32[16,144,128]{2,1,0:T(8,128)} %add.62), calls=%async_computation | async-start | bytes 2359296 | tf_op jit(solution)/shard_map/all_to_all | solution.py:401
  58.4 7.5 %collective-permute-start.1 = (f32[16,128]{1,0:T(8,128)S(1)}, f32[16,128]{1,0:T(8,128)S(1)}, u32[]{:S(2)}, u32[]{:S(2)}) collective-permute-start(f32[16,128]{1,0:T(8,128)S(1)} %pad_maximum_fusion.2), channel_id=1, source_target_pairs={{16,144},{17,49},{18,146},{19,51},{20,148},{21,53},{22,150},{23,55... | collective-permute-start | bytes 24584 | tf_op jit(solution)/shard_map/ppermute | solution.py:405
  66.0 38.2 %copy-start.3 = (f32[128,128]{1,0:T(8,128)S(1)}, f32[128,128]{1,0:T(8,128)}, u32[]{:S(2)}) copy-start(f32[128,128]{1,0:T(8,128)} %days_ref.3) | copy-start | bytes 196612
  99.2 5.0 %collective-permute-start.2 = (f32[16,152,128]{2,1,0:T(8,128)S(1)}, f32[16,152,128]{2,1,0:T(8,128)}, u32[]{:S(2)}, u32[]{:S(2)}) collective-permute-start(f32[16,152,128]{2,1,0:T(8,128)S(1)} %all_to_all.40.here_ref), channel_id=1, source_target_pairs={{0,1},{1,0},{2,3},{3,2},{4,5},{5,4},{6,7},{7,6},{8,9},{9,8},{10,11... | collective-permute-start | bytes 3735560 | tf_op jit(solution)/shard_map/ppermute | solution.py:346
  104.2 1.6 copy-start.5
  125.3 1.3 copy-start.6
  126.6 1.3 copy-start.8
  164.2 1.6 copy-start.9
  179.9 4.7 %collective-permute-start.3 = (f32[16,144,128]{2,1,0:T(8,128)S(1)}, f32[16,144,128]{2,1,0:T(8,128)S(1)}, u32[]{:S(2)}, u32[]{:S(2)}) collective-permute-start(f32[16,144,128]{2,1,0:T(8,128)S(1)} %get-tuple-element.21), channel_id=1, source_target_pairs={{0,1},{1,0},{2,3},{3,2},{4,5},{5,4},{6,7},{7,6},{8,9},{9,8},{10,11... | collective-permute-start | bytes 3538952 | tf_op jit(solution)/shard_map/ppermute | solution.py:346
  220.0 6.4 %collective-permute-start.4 = (f32[8,128]{1,0:T(8,128)S(1)}, f32[8,128]{1,0:T(8,128)S(1)}, u32[]{:S(2)}, u32[]{:S(2)}) collective-permute-start(f32[8,128]{1,0:T(8,128)S(1)} %get-tuple-element.28), channel_id=1, source_target_pairs={{16,144},{17,49},{18,146},{19,51},{20,148},{21,53},{22,150},{23,55... | collective-permute-start | bytes 12296 | tf_op jit(solution)/shard_map/ppermute | solution.py:405
  226.5 36.1 %copy-start.7 = (f32[64,64,128]{2,1,0:T(8,128)S(1)}, f32[64,64,128]{2,1,0:T(8,128)}, u32[]{:S(2)}) copy-start(f32[64,64,128]{2,1,0:T(8,128)} %copy-done.6) | copy-start | bytes 6291460
  257.9 4.7 %collective-permute-start.5 = (f32[16,144,128]{2,1,0:T(8,128)S(1)}, f32[16,144,128]{2,1,0:T(8,128)S(1)}, u32[]{:S(2)}, u32[]{:S(2)}) collective-permute-start(f32[16,144,128]{2,1,0:T(8,128)S(1)} %all_to_all.44.here_ref), channel_id=1, source_target_pairs={{0,1},{1,0},{2,3},{3,2},{4,5},{5,4},{6,7},{7,6},{8,9},{9,8},{10,11... | collective-permute-start | bytes 3538952 | tf_op jit(solution)/shard_map/ppermute | solution.py:346
where the time goes:
time: 316 us; the launch traced here: 315 us
  blocking collectives  164 us (52%)
  Pallas kernels  64.3 us (20%)
  waiting for transfers between devices  51.6 us (16%)
  starting transfers between devices  19.8 us (6%)
  local copies, waits for them, and re-layouts  12.5 us (4%)
    all_to_all x4, blocking collectives, gather_all(): return lax.all_to_all(spread, axes, 0, 0, tiled=True)  91.6 us
    pallas_call x2, Pallas kernels, modes_call(): call(functools.partial(modes_kernel, first), outs, [SMEM, SMEM] + [VMEM]...  37.6 us
    all_to_all x2, blocking collectives, sum_cells(): lax.all_to_all(value.reshape(size, rows // size, -1), LL, 0, 0, tiled=True)  37.2 us
    all_to_all x1, blocking collectives, on_device(): shard = jnp.sum(lax.all_to_all(half, YZ, 0, 0, tiled=True), axis=0)  35.1 us
    all_to_all x1, waiting for transfers between devices, on_device(): shard = jnp.sum(lax.all_to_all(half, YZ, 0, 0, tiled=True), axis=0)  29.1 us
    pallas_call x1, Pallas kernels, days_call(): call(days_kernel, [block, block, (sums.shape[0] - n, n)], [SMEM] + [VMEM]...  14.1 us
    unnamed x21, local copies, waits for them, and re-layouts  12 us
    ppermute x2, waiting for transfers between devices, on_device(): halo = lax.ppermute(send, ALL, pairs)  11.3 us
  transfers between devices with their start and end apart: 7, of which 7 were waited for; matrix products, arithmetic and copies ran while one was open for 0% of the time, Pallas kernels for 0%

commit v1 on v0

v1 whole, which is shorter than its diff:
```python
import functools
import math

import jax
import jax.numpy as jnp
from jax import lax
from jax.experimental import pallas as pl
from jax.experimental.pallas import tpu as pltpu
from jax.sharding import Mesh, PartitionSpec as P

ITERS = 2


ridge_term = 1.0
diffusion = 0.1
lat_south = 30.0
lat_span = 16.0

GAP = 1e30
PIECES = 8
GROUP = 16
YZ = ("zlo", "y")
DAY = ("zlo", "y", "core")
ALL = ("lat", "lon", "zlo", "y", "core")
LL = ("lat", "lon")
f32, bf16 = jnp.float32, jnp.bfloat16


def inverse_spd(matrix):
    size = matrix.shape[0]
    blocks = [matrix[8 * r : 8 * r + 8] for r in range(size // 8)]
    lane = lax.broadcasted_iota(jnp.int32, (1, size), 1)
    row = lax.broadcasted_iota(jnp.int32, (8, size), 0)
    for k in range(0, size, 4):
        home, off = k // 8, k % 8
        rows = [blocks[home][off + i : off + i + 1] for i in range(4)]
        d = [[jnp.broadcast_to(rows[i][:, k + j : k + j + 1], (1, size)) for j in range(4)] for i in range(4)]
        in_panel = (lane >= k) & (lane < k + 4)
        a, b, c = d[0][0], d[0][1], d[1][1]
        r = 1.0 / (a * c - b * b)
        a00, a01, a11 = c * r, -b * r, a * r
        b02, b03, b12, b13 = d[0][2], d[0][3], d[1][2], d[1][3]
        g02, g03 = a00 * b02 + a01 * b12, a00 * b03 + a01 * b13
        g12, g13 = a01 * b02 + a11 * b12, a01 * b03 + a11 * b13
        s22 = d[2][2] - (b02 * g02 + b12 * g12)
        s23 = d[2][3] - (b02 * g03 + b12 * g13)
        s33 = d[3][3] - (b03 * g03 + b13 * g13)
        r = 1.0 / (s22 * s33 - s23 * s23)
        i22, i23, i33 = s33 * r, -s23 * r, s22 * r
        h02, h03 = g02 * i22 + g03 * i23, g02 * i23 + g03 * i33
        h12, h13 = g12 * i22 + g13 * i23, g12 * i23 + g13 * i33
        q00 = a00 + (h02 * g02 + h03 * g03)
        q01 = a01 + (h02 * g12 + h03 * g13)
        q11 = a11 + (h12 * g12 + h13 * g13)
        inv = [[q00, q01, -h02, -h03], [q01, q11, -h12, -h13], [-h02, -h12, i22, i23], [-h03, -h13, i23, i33]]
        unit = [jnp.where(lane == k + j, 1.0, jnp.where(in_panel, 0.0, rows[j])) for j in range(4)]
        new = [
            (inv[i][0] * unit[0] + inv[i][1] * unit[1]) + (inv[i][2] * unit[2] + inv[i][3] * unit[3])
            for i in range(4)
        ]
        out = []
        for r8, block in enumerate(blocks):
            cols = [block[:, k + j : k + j + 1] for j in range(4)]
            keep = jnp.where(in_panel, 0.0, block)
            keep = keep - ((cols[0] * new[0] + cols[1] * new[1]) + (cols[2] * new[2] + cols[3] * new[3]))
            if r8 == home:
                for j in range(4):
                    keep = jnp.where(row == off + j, new[j], keep)
            out.append(keep)
        blocks = out
    return jnp.concatenate(blocks, axis=0)


def add_ridge(gram):
    size = gram.shape[0]
    same = lax.broadcasted_iota(jnp.int32, (size, size), 0) == lax.broadcasted_iota(jnp.int32, (size, size), 1)
    return gram + jnp.where(same, ridge_term, 0.0)


def split(value):
    one = value.astype(bf16)
    return jnp.concatenate([one, (value - one.astype(f32)).astype(bf16)], axis=1)


def right_side(value):
    wide = split(value)
    return jnp.concatenate([wide, wide], axis=0)


def times(parts, side):
    wide = jnp.dot(parts, side, preferred_element_type=f32)
    n = wide.shape[1] // 2
    return wide[:, :n] + wide[:, n:]


def dot_tn(left, right):
    return lax.dot_general(left, right, (((0,), (0,)), ((), ())), preferred_element_type=f32)


def full(left, right, dims=(((1,), (0,)), ((), ()))):
    return lax.dot_general(left, right, dims, precision=lax.Precision.HIGHEST, preferred_element_type=f32)


def put_block(half, grid_ref, gram_ref, ref):
    lats, lons, modes = grid_ref.shape
    spokes = ref.shape[0]
    cells = lats * lons // spokes
    line = grid_ref[half * (lats - 1)]
    for q in range(spokes):
        if q < lons // 8:
            edge = line[8 * q : 8 * q + 8]
        else:
            side, at = divmod(8 * q - lons, lats)
            edge = grid_ref[at : at + 8, side * (lons - 1), :]
        ref[q, cells : cells + 8, :] = edge
        ref[q, cells + 8 : cells + 16, :] = gram_ref[8 * q : 8 * q + 8, :]


def put_rows(ref, grid_ref, g, base, out):
    lons = grid_ref.shape[1]
    cells = ref.shape[1] - 16
    for p in range(PIECES):
        ref[g * PIECES + p, 0:cells, :] = out[p * cells : (p + 1) * cells]
    for p in range(out.shape[0] // lons):
        grid_ref[base + p] = out[p * lons : (p + 1) * lons]


def first_kernel(mine, core_ref, anomaly_ref, observed_ref, seat_ref, days_ref, ref, coded_ref, sea_ref, grid_ref, gram_ref):
    core = core_ref[0, 0]
    half = core if mine else 1 - core
    lats, lons, days = coded_ref.shape
    spokes = ref.shape[0]
    many = PIECES * lats // spokes
    temporal = days_ref[...]
    side = right_side(temporal)
    gram_ref[...] = full(temporal, temporal, (((0,), (0,)), ((), ())))
    seat = seat_ref[...]

    def step(g, _):
        rows = []
        for p in range(many):
            here = g * many + p
            i = half * lats + here
            sea = jnp.broadcast_to(pltpu.roll(seat, lax.rem(seat.shape[1] - i, seat.shape[1]), 1)[:, :1], (lons, days))
            sea_ref[here] = sea
            seen = observed_ref[i] != 0
            known = jnp.where(seen, sea * anomaly_ref[i], 0.0)
            coded_ref[here] = jnp.where(seen | (sea == 0.0), known, GAP)
            rows.append(known)
        put_rows(ref, grid_ref, g, g * many, times(split(jnp.concatenate(rows, axis=0)), side))
        return _

    lax.fori_loop(0, spokes // PIECES, step, 0)
    put_block(half, grid_ref, gram_ref, ref)


def modes_kernel(first, core_ref, weight_ref, here_ref, there_ref, days_ref, *refs):
    coded_refs, field_refs, refs = refs[0:2], refs[2:4], refs[4:]
    spatial_ref, sums_ref = refs[0:2]
    around_refs = refs[2:4] if first else field_refs
    pad_ref, rim_ref, wide_ref = refs[-3:]
    core = core_ref[0, 0]
    lats, lons, modes = spatial_ref.shape
    deep = lats // 2
    spokes = here_ref.shape[0]
    per = deep // spokes
    cells = per * lons
    tiles = 2 if first else 1
    gram_at = cells + 8 * tiles
    halves = (core, 1 - core)

    for half, ref in zip(halves, (here_ref, there_ref)):
        for q in range(spokes):
            for p in range(per):
                pad_ref[half * deep + q * per + p + 1] = ref[q, p * lons : (p + 1) * lons, :]
            if q < lons // 8:
                at = half * lons + 8 * q
            else:
                side, along = divmod(8 * q - lons, deep)
                at = 2 * lons + side * lats + half * deep + along
            for t in range(tiles):
                rim_ref[pl.ds(pl.multiple_of(t * 4 * lons + at, 8), 8), :] = ref[q, cells + 8 * t : cells + 8 * t + 8, :]
    pad_ref[0] = rim_ref[lons : 2 * lons, :]
    pad_ref[lats + 1] = rim_ref[0:lons, :]
    gram = jnp.concatenate([here_ref[q, gram_at : gram_at + 8, :] for q in range(spokes)], axis=0)
    inverse_side = right_side(inverse_spd(add_ridge(gram)))
    days_side = right_side(days_ref[...].T)
    row = lax.broadcasted_iota(jnp.int32, (lons, modes), 0)

    def beside(value, i, kind):
        east = rim_ref[pl.ds(kind * 4 * lons + 2 * lons + i, 1), :]
        west = rim_ref[pl.ds(kind * 4 * lons + 2 * lons + lats + i, 1), :]
        ahead = jnp.where(row == lons - 1, east, pltpu.roll(value, lons - 1, 0))
        behind = jnp.where(row == 0, west, pltpu.roll(value, 1, 0))
        return ahead + behind

    if first:
        for n, half in enumerate(halves):
            field_ref, beyond_ref, around_ref = field_refs[n], field_refs[1 - n], around_refs[n]

            def masks(l, _, half=half, field_ref=field_ref, beyond_ref=beyond_ref, around_ref=around_ref):
                i = half * deep + l
                sea = field_ref[l]
                above = jnp.where(half == 0, rim_ref[5 * lons : 6 * lons, :], beyond_ref[deep - 1])
                below = jnp.where(half == 0, beyond_ref[0], rim_ref[4 * lons : 5 * lons, :])
                north = jnp.where(l == 0, above, field_ref[jnp.maximum(l - 1, 0)])
                south = jnp.where(l == deep - 1, below, field_ref[jnp.minimum(l + 1, deep - 1)])
                round_ = (north + south) + weight_ref[0, i] * beside(sea, i, 1)
                around_ref[l] = jnp.where(sea == 0.0, GAP, 1.0 - diffusion * round_)
                return _

            lax.fori_loop(0, deep, masks, 0, unroll=2)

    wide_ref[...] = jnp.zeros_like(wide_ref)
    for n, half in enumerate(halves):

        def step(g, _, half=half, around_ref=around_refs[n], coded_ref=coded_refs[n]):
            smoothed = []
            for p in range(GROUP):
                l = g * GROUP + p
                i = half * deep + l
                around = around_ref[l]
                raw = pad_ref[i + 1]
                near = (pad_ref[i] + pad_ref[i + 2]) + weight_ref[0, i] * beside(raw, i, 0)
                smoothed.append(jnp.where(around == GAP, 0.0, around * raw + diffusion * near))
            spatial = times(split(jnp.concatenate(smoothed, axis=0)), inverse_side)
            parts = split(spatial)
            guess = times(parts, days_side)
            filled = []
            for p in range(GROUP):
                l = g * GROUP + p
                spatial_ref[half * deep + l] = spatial[p * lons : (p + 1) * lons]
                coded = coded_ref[l]
                filled.append(jnp.where(coded == GAP, guess[p * lons : (p + 1) * lons], coded))
            filled = split(jnp.concatenate(filled, axis=0))
            wide_ref[...] += dot_tn(jnp.concatenate([filled, parts], axis=1), parts)
            return _

        lax.fori_loop(0, deep // GROUP, step, 0)
    m = modes
    for part in range(2):
        at = 2 * part * m
        wide = wide_ref[at : at + m, :] + wide_ref[at + m : at + 2 * m, :]
        sums_ref[part * m : (part + 1) * m, :] = wide[:, :m] + wide[:, m:]


def days_kernel(mine, core_ref, sums_ref, coded_ref, spatial_ref, ref, *refs):
    core = core_ref[0, 0]
    half = core if mine else 1 - core
    grid_ref, gram_ref = refs[-2:]
    lats, lons, modes = coded_ref.shape
    spokes = ref.shape[0]
    many = PIECES * lats // spokes
    if mine:
        temporal = sums_ref[...]
    else:
        days = sums_ref.shape[0] - modes
        temporal = full(sums_ref[0:days, :], inverse_spd(add_ridge(sums_ref[days:, :])))
        refs[0][...] = temporal
    side = right_side(temporal)
    across = right_side(temporal.T)
    gram_ref[...] = full(temporal, temporal, (((0,), (0,)), ((), ())))

    def step(g, _):
        at = half * lats + g * many
        guess = times(split(jnp.concatenate([spatial_ref[at + p] for p in range(many)], axis=0)), across)
        coded = jnp.concatenate([coded_ref[g * many + p] for p in range(many)], axis=0)
        put_rows(ref, grid_ref, g, g * many, times(split(jnp.where(coded == GAP, guess, coded)), side))
        return _

    lax.fori_loop(0, spokes // PIECES, step, 0)
    put_block(half, grid_ref, gram_ref, ref)


def last_kernel(sums_ref, days_ref):
    days = days_ref.shape[0]
    days_ref[...] = full(sums_ref[0:days, :], inverse_spd(add_ridge(sums_ref[days:, :])))


SMEM = pl.BlockSpec(memory_space=pltpu.SMEM)
VMEM = pl.BlockSpec(memory_space=pltpu.VMEM)


def call(kernel, outs, specs, scratch, name, flops, nbytes):
    return pl.pallas_call(
        kernel,
        out_shape=[jax.ShapeDtypeStruct(shape, f32) for shape in outs],
        in_specs=specs,
        out_specs=[VMEM] * len(outs),
        scratch_shapes=[pltpu.VMEM(shape, f32) for shape in scratch],
        name=name,
        cost_estimate=pl.CostEstimate(flops=flops, bytes_accessed=nbytes, transcendentals=0),
        compiler_params=pltpu.CompilerParams(vmem_limit_bytes=28 * 1024 * 1024),
    )


def first_call(mine, core, anomaly, observed, seat, days, spokes):
    lats, lons, n = anomaly.shape
    block = (spokes, lats * lons // (2 * spokes) + 16, n)
    grid = (lats // 2, lons, n)
    kernel = functools.partial(first_kernel, mine)
    return call(kernel, [block, grid, grid], [SMEM] + [VMEM] * 4, [grid, (n, n)], "first_projection", 10**9, 10**7)(
        core, anomaly, observed, seat, days
    )


def modes_call(first, core, weight, here, there, days, coded, field):
    lats, lons, n = coded[0].shape
    half = (lats, lons, n)
    grid = (2 * lats, lons, n)
    outs = [grid, (2 * n, n)] + ([half, half] if first else [])
    scratch = [(2 * lats + 2, lons, n), ((8 if first else 4) * lons, n), (4 * n, 2 * n)]
    return call(functools.partial(modes_kernel, first), outs, [SMEM, SMEM] + [VMEM] * 7, scratch, "modes_sweep", 2 * 10**9, 10**7)(
        core, weight, here, there, days, *coded, *field
    )


def days_call(mine, core, sums, coded, spatial, spokes):
    lats, lons, n = coded.shape
    block = (spokes, lats * lons // spokes + 16, n)
    outs = [block] if mine else [block, (sums.shape[0] - n, n)]
    kernel = functools.partial(days_kernel, mine)
    return call(kernel, outs, [SMEM] + [VMEM] * 3, [(lats, lons, n), (n, n)], "days_sweep", 2 * 10**9, 10**7)(
        core, sums, coded, spatial
    )


def last_call(sums):
    n = sums.shape[1]
    return call(last_kernel, [(sums.shape[0] - n, n)], [VMEM], [], "last_days", 10**7, 10**6)(sums)[0]


def lat_weights(first_row, row_count, total_rows):
    index_rows = first_row + jnp.arange(row_count, dtype=jnp.float32)
    angle = (lat_south + lat_span * (index_rows + 0.5) / total_rows) * (math.pi / 180.0)
    cosine = jnp.cos(angle)
    return 1.0 / (cosine * cosine)


def swap_core(value):
    return lax.ppermute(value, "core", [(0, 1), (1, 0)])


def halo_pairs(lats, lons, spokes):
    pairs = []
    for la in range(lats):
        for lo in range(lons):
            for q in range(spokes):
                for core in range(2):
                    if q < spokes // 2:
                        to_la, to_lo = la + 2 * core - 1, lo
                    else:
                        to_la, to_lo = la, lo + (1 if q >= 3 * spokes // 4 else -1)
                    if 0 <= to_la < lats and 0 <= to_lo < lons:
                        here = ((la * lons + lo) * spokes + q) * 2 + core
                        there = ((to_la * lons + to_lo) * spokes + q) * 2 + core
                        pairs.append((here, there))
    return pairs


def gather_all(value, axes, size):
    spread = jnp.broadcast_to(value[None], (size,) + value.shape)
    return lax.all_to_all(spread, axes, 0, 0, tiled=True)


def sum_cells(value):
    size = lax.axis_size("lat") * lax.axis_size("lon")
    rows = value.shape[0]
    parts = lax.all_to_all(value.reshape(size, rows // size, -1), LL, 0, 0, tiled=True)
    mine = jnp.sum(parts, axis=0)
    return gather_all(mine, LL, size).reshape(rows, -1)


def edges_of(grid):
    middle = grid.shape[0] // 2
    up, down = grid[:middle], grid[middle:]
    return jnp.concatenate([up[0], up[:, 0], up[:, -1], down[-1], down[:, 0], down[:, -1]], axis=0)


def on_device(anomaly, observed, ocean_mask, start_days):
    rows_lat, cols_lon, _ = anomaly.shape
    rank_count = start_days.shape[1]
    lats, lons = lax.axis_size("lat"), lax.axis_size("lon")
    spokes = lax.axis_size("zlo") * lax.axis_size("y")
    core = lax.axis_index("core")
    spoke = lax.axis_index("zlo") * lax.axis_size("y") + lax.axis_index("y")
    pairs = halo_pairs(lats, lons, spokes)
    cells = rows_lat * cols_lon // (2 * spokes)
    core_word = core.reshape(1, 1).astype(jnp.int32)
    sea_grid = ocean_mask.astype(f32)
    seat = jnp.pad(sea_grid.T, ((0, 0), (0, rank_count - rows_lat)))
    first_lat = (lax.axis_index("lat") * rows_lat).astype(f32)
    weight = lat_weights(first_lat, rows_lat, float(rows_lat * lats)).reshape(1, rows_lat)
    edge_sea = lax.dynamic_slice_in_dim(edges_of(sea_grid), (core * spokes + spoke) * 8, 8)
    edge_sea = jnp.broadcast_to(edge_sea[:, None], (8, rank_count))
    temporal = start_days
    coded, field = [None, None], [None, None]
    other, coded[1], field[1] = first_call(False, core_word, anomaly, observed, seat, start_days, spokes)
    mine, coded[0], field[0] = first_call(True, core_word, anomaly, observed, seat, start_days, spokes)
    for sweep in range(ITERS):
        half = mine + swap_core(other)
        shard = jnp.sum(lax.all_to_all(half, YZ, 0, 0, tiled=True), axis=0)
        send = shard[cells : cells + 8]
        if sweep == 0:
            send = jnp.concatenate([send, edge_sea], axis=0)
        halo = lax.ppermute(send, ALL, pairs)
        shard = jnp.concatenate([shard[:cells], halo, shard[cells + 8 :]], axis=0)
        here = gather_all(shard, YZ, spokes)
        there = swap_core(here)
        out = modes_call(sweep == 0, core_word, weight, here, there, temporal, coded, field)
        spatial, sums = out[0], sum_cells(out[1])
        if sweep == 0:
            field = out[2:4]
        if sweep < ITERS - 1:
            other, temporal = days_call(False, core_word, sums, coded[1], spatial, spokes)
            (mine,) = days_call(True, core_word, temporal, coded[0], spatial, spokes)
        else:
            temporal = last_call(sums)
    return (spatial, temporal)


def solution(mesh):
    lats, lons, days = mesh.devices.shape
    fine = Mesh(mesh.devices.reshape(lats, lons, 2, days // 4, 2), ALL)
    in_specs = (P("lat", "lon", DAY), P("lat", "lon", DAY), P("lat", "lon"), P(DAY, None))
    out_specs = (P("lat", "lon", None), P(DAY, None))
    return jax.shard_map(
        on_device, mesh=fine, in_specs=in_specs, out_specs=out_specs, check_vma=False
    )
```

time: 316 us -> 299 us (0.946)
  Pallas kernels: 64.3 us -> 40.5 us
  local copies, waits for them, and re-layouts: 12.5 us -> 20.4 us
  waiting for transfers between devices: 51.6 us -> 47.4 us
    pallas_call x2, Pallas kernels: 37.6 us -> 23.3 us  [modes_call(): call(functools.partial(modes_kernel, first), outs, [SMEM, SMEM] + [VMEM]...]
    pallas_call x2 -> x4, Pallas kernels: 20.7 us -> 11.2 us  [the longest x2 8.33 us: days_call(): call(kernel, outs, [SMEM] + [VMEM] * 3, [(lats, lons, n), (n, n)], 'days_...]
    unnamed x21 -> x43, local copies, waits for them, and re-layouts: 12 us -> 19.7 us
    ppermute x4, waiting for transfers between devices: 11.2 us -> 6.86 us  [swap_core(): return lax.ppermute(value, 'core', [(0, 1), (1, 0)])]
  transfers between devices with their start and end apart: 7 -> 7, of which waited for: 7 -> 6; matrix products, arithmetic and copies ran while one was open for 0% -> 0% of each run, Pallas kernels for 0% -> 1%
where the time goes in v1:
time: 299 us; the launch traced here: 298 us
  blocking collectives  167 us (56%)
  waiting for transfers between devices  47.4 us (16%)
  Pallas kernels  40.5 us (14%)
  local copies, waits for them, and re-layouts  20.4 us (7%)
  starting transfers between devices  19.8 us (7%)
    all_to_all x4, blocking collectives, gather_all(): return lax.all_to_all(spread, axes, 0, 0, tiled=True)  94.3 us
    all_to_all x2, blocking collectives, sum_cells(): lax.all_to_all(value.reshape(size, rows // size, -1), LL, 0, 0, tiled=True)  38.3 us
    all_to_all x1, blocking collectives, on_device(): shard = jnp.sum(lax.all_to_all(half, YZ, 0, 0, tiled=True), axis=0)  34.6 us
    all_to_all x1, waiting for transfers between devices, on_device(): shard = jnp.sum(lax.all_to_all(half, YZ, 0, 0, tiled=True), axis=0)  29.1 us
    pallas_call x2, Pallas kernels, modes_call(): call(functools.partial(modes_kernel, first), outs, [SMEM, SMEM] + [VMEM]...  23.3 us
    unnamed x43, local copies, waits for them, and re-layouts  19.7 us
    ppermute x2, waiting for transfers between devices, on_device(): halo = lax.ppermute(send, ALL, pairs)  11.4 us
    all_to_all x1, starting transfers between devices, on_device(): shard = jnp.sum(lax.all_to_all(half, YZ, 0, 0, tiled=True), axis=0)  9.37 us
  transfers between devices with their start and end apart: 7, of which 6 were waited for; matrix products, arithmetic and copies ran while one was open for 0% of the time, Pallas kernels for 1%

profile of v1, /device:TPU:8, one launch (start us, length us, event | category | flops | bytes accessed | tf_op | source)
XLA Modules:
  0.0 297.8 jit_solution(9134184516367967484)
XLA Ops:
  0.6 0.8 copy.7
  1.5 1.6 copy-done
  3.1 1.6 copy-done.1
  4.7 0.8 copy-done.2
  5.5 1.4 first_projection.3
  7.0 1.0 copy-done.4
  8.0 1.0 copy-done.11
  8.9 1.9 collective-permute-start
  10.9 1.5 first_projection.2
  12.3 1.0 copy-done.8
  13.3 1.0 copy-done.13
  14.3 1.2 add.62
  15.4 9.4 %all-to-all-start = ((f32[16,144,128]{2,1,0:T(8,128)}), f32[16,144,128]{2,1,0:T(8,128)S(1)}, u32[]{:S(2)}, u32[]{:S(2)}) async-start(f32[16,144,128]{2,1,0:T(8,128)} %add.62), calls=%async_computation | async-start | bytes 2359296 | tf_op jit(solution)/shard_map/all_to_all | solution.py:402
  24.8 0.2 slice_reduce_fusion
  25.3 29.1 %all-to-all-done = f32[16,144,128]{2,1,0:T(8,128)S(1)} async-done(((f32[16,144,128]{2,1,0:T(8,128)}), f32[16,144,128]{2,1,0:T(8,128)S(1)}, u32[]{:S(2)}, u32[]{:S(2)}) %all-to-all-start) | async-done | bytes 1179680 | tf_op jit(solution)/shard_map/all_to_all | solution.py:402
  54.5 1.3 collective-permute-start.1
  55.8 6.4 %collective-permute-done.1 = f32[16,128]{1,0:T(8,128)S(1)} collective-permute-done((f32[16,128]{1,0:T(8,128)S(1)}, f32[16,128]{1,0:T(8,128)S(1)}, u32[]{:S(2)}, u32[]{:S(2)}) %collective-permute-start.1) | collective-permute-done | bytes 8224 | tf_op jit(solution)/shard_map/ppermute | solution.py:406
  62.2 0.1 broadcast_in_dim.11
  62.3 35.4 %all_to_all.40.here_ref = f32[16,152,128]{2,1,0:T(8,128)S(1)} all-to-all(f32[16,152,128]{2,1,0:T(8,128)S(1)} %broadcast_in_dim.11), channel_id=1, replica_groups=mesh['lat'=4,'lon'=4,'zlo'=2,'y'=8,'core'=2] {'zlo','y'}, dimensions={0} | all-to-all | bytes 2490368 | tf_op jit(solution)/shard_map/all_to_all | solution.py:363
  97.7 1.9 collective-permute-start.2
  99.7 2.8 collective-permute-done.2.there_ref
  102.5 1.2 copy-done.5
  103.8 1.2 copy-done.9
  105.0 1.2 copy-done.12
  106.2 1.2 copy-done.14
  107.4 12.0 %modes_sweep.2 = (f32[64,64,128]{2,1,0:T(8,128)S(1)}, f32[256,128]{1,0:T(8,128)S(1)}, f32[32,64,128]{2,1,0:T(8,128)S(1)}, f32[32,64,128]{2,1,0:T(8,128)S(1)}) custom-call(s32[1,1]{1,0:T(1,128)} %bitcast.core_ref, f32[1,64]{1,0:T(1,128)S(1)} %multiply_divide_fusion.weight_ref, f32[16,152,128]{2,1,0:T(8,128)S(1)} %all_to_all.40.here_ref, ...), custom_call_target="tpu_custom_call" | custom-call | flops 2000000000 | bytes 10000000 | tf_op jit(solution)/shard_map/modes_sweep/pallas_call | solution.py:313
  119.5 1.3 copy-done.15
  120.8 1.0 copy-done.17
  121.8 1.0 copy-done.19
  122.7 22.3 %all_to_all.41 = f32[16,16,128]{2,1,0:T(8,128)S(1)} all-to-all(f32[16,16,128]{2,1,0:T(8,128)S(1)} %bitcast.17), channel_id=1, replica_groups=mesh['lat'=4,'lon'=4,'zlo'=2,'y'=8,'core'=2] {'lat','lon'}, dimensions={0} | all-to-all | bytes 262144 | tf_op jit(solution)/shard_map/all_to_all | solution.py:369
  145.1 13.7 %all_to_all.42 = f32[16,16,128]{2,1,0:T(8,128)S(1)} all-to-all(f32[16,16,128]{2,1,0:T(8,128)S(1)} %broadcast_in_dim.12), channel_id=1, replica_groups=mesh['lat'=4,'lon'=4,'zlo'=2,'y'=8,'core'=2] {'lat','lon'}, dimensions={0} | all-to-all | bytes 262144 | tf_op jit(solution)/shard_map/all_to_all | solution.py:363
  158.9 1.2 copy-done.6
  160.1 1.6 copy-done.16
  161.7 6.9 %days_sweep.2 = (f32[16,144,128]{2,1,0:T(8,128)S(1)}, f32[128,128]{1,0:T(8,128)S(1)}) custom-call(s32[1,1]{1,0:T(1,128)} %bitcast.core_ref, f32[256,128]{1,0:T(8,128)S(1)} %bitcast.18, f32[32,64,128]{2,1,0:T(8,128)S(1)} %copy-done.6, f32[64,64,128]{2,1,0:T(8,128)S(1)} %copy-done.16), custom_call_target="tpu_custom_call" | custom-call | flops 2000000000 | bytes 10000000 | tf_op jit(solution)/shard_map/days_sweep/pallas_call | solution.py:323
  168.7 1.9 collective-permute-start.3
  170.6 1.4 days_sweep.3
  172.0 1.4 collective-permute-done.3
  173.4 0.2 add.66
  173.6 34.6 %all_to_all.43 = f32[16,144,128]{2,1,0:T(8,128)S(1)} all-to-all(f32[16,144,128]{2,1,0:T(8,128)S(1)} %add.66), channel_id=1, replica_groups=mesh['lat'=4,'lon'=4,'zlo'=2,'y'=8,'core'=2] {'zlo','y'}, dimensions={0} | all-to-all | bytes 2359296 | tf_op jit(solution)/shard_map/all_to_all | solution.py:402
  208.2 1.3 collective-permute-start.4
  209.5 5.1 %collective-permute-done.4 = f32[8,128]{1,0:T(8,128)S(1)} collective-permute-done((f32[8,128]{1,0:T(8,128)S(1)}, f32[8,128]{1,0:T(8,128)S(1)}, u32[]{:S(2)}, u32[]{:S(2)}) %collective-permute-start.4) | collective-permute-done | bytes 4128 | tf_op jit(solution)/shard_map/ppermute | solution.py:406
  214.7 31.4 %all_to_all.44.here_ref = f32[16,144,128]{2,1,0:T(8,128)S(1)} all-to-all(f32[16,144,128]{2,1,0:T(8,128)S(1)} %broadcast_in_dim.13), channel_id=1, replica_groups=mesh['lat'=4,'lon'=4,'zlo'=2,'y'=8,'core'=2] {'zlo','y'}, dimensions={0} | all-to-all | bytes 2359296 | tf_op jit(solution)/shard_map/all_to_all | solution.py:363
  246.2 2.1 collective-permute-start.5
  248.3 2.6 collective-permute-done.5.there_ref
  250.9 11.3 %modes_sweep.3 = (f32[64,64,128]{2,1,0:T(8,128)}, f32[256,128]{1,0:T(8,128)S(1)}) custom-call(s32[1,1]{1,0:T(1,128)} %bitcast.core_ref, f32[1,64]{1,0:T(1,128)S(1)} %multiply_divide_fusion.weight_ref, f32[16,144,128]{2,1,0:T(8,128)S(1)} %all_to_all.44.here_ref, f32[16,144,128]{2,1,0:T(8,128)S(1)} %collective-permute-done.5.there_ref, ...), custom_call_target="tpu_custom_call" | custom-call | flops 2000000000 | bytes 10000000 | tf_op jit(solution)/shard_map/modes_sweep/pallas_call | solution.py:313
  262.2 16.0 %all_to_all.45 = f32[16,16,128]{2,1,0:T(8,128)S(1)} all-to-all(f32[16,16,128]{2,1,0:T(8,128)S(1)} %bitcast.16), channel_id=1, replica_groups=mesh['lat'=4,'lon'=4,'zlo'=2,'y'=8,'core'=2] {'lat','lon'}, dimensions={0} | all-to-all | bytes 262144 | tf_op jit(solution)/shard_map/all_to_all | solution.py:369
  278.2 13.7 %all_to_all.46 = f32[16,16,128]{2,1,0:T(8,128)S(1)} all-to-all(f32[16,16,128]{2,1,0:T(8,128)S(1)} %broadcast_in_dim.14), channel_id=1, replica_groups=mesh['lat'=4,'lon'=4,'zlo'=2,'y'=8,'core'=2] {'lat','lon'}, dimensions={0} | all-to-all | bytes 262144 | tf_op jit(solution)/shard_map/all_to_all | solution.py:363
  291.9 5.9 %last_days.1 = f32[128,128]{1,0:T(8,128)} custom-call(f32[256,128]{1,0:T(8,128)S(1)} %bitcast.15), custom_call_target="tpu_custom_call" | custom-call | flops 10000000 | bytes 1000000 | tf_op jit(solution)/shard_map/last_days/pallas_call | solution.py:330
  (48 shorter events, 0.8 us)
Async XLA Ops:
  1.5 1.6 copy-start
  3.1 1.6 copy-start.1
  4.7 0.8 copy-start.2
  7.0 1.0 copy-start.4
  8.0 1.0 copy-start.11
  8.9 5.3 %collective-permute-start = (f32[16,144,128]{2,1,0:T(8,128)S(1)}, f32[16,144,128]{2,1,0:T(8,128)S(1)}, u32[]{:S(2)}, u32[]{:S(2)}) collective-permute-start(f32[16,144,128]{2,1,0:T(8,128)S(1)} %get-tuple-element.17), channel_id=1, source_target_pairs={{0,1},{1,0},{2,3},{3,2},{4,5},{5,4},{6,7},{7,6},{8,9},{9,8},{10,11... | collective-permute-start | bytes 3538952 | tf_op jit(solution)/shard_map/ppermute | solution.py:341
  12.3 1.0 copy-start.8
  13.3 1.0 copy-start.13
  15.4 38.9 %all-to-all-start = ((f32[16,144,128]{2,1,0:T(8,128)}), f32[16,144,128]{2,1,0:T(8,128)S(1)}, u32[]{:S(2)}, u32[]{:S(2)}) async-start(f32[16,144,128]{2,1,0:T(8,128)} %add.62), calls=%async_computation | async-start | bytes 2359296 | tf_op jit(solution)/shard_map/all_to_all | solution.py:402
  54.5 7.7 %collective-permute-start.1 = (f32[16,128]{1,0:T(8,128)S(1)}, f32[16,128]{1,0:T(8,128)S(1)}, u32[]{:S(2)}, u32[]{:S(2)}) collective-permute-start(f32[16,128]{1,0:T(8,128)S(1)} %pad_maximum_fusion.2), channel_id=1, source_target_pairs={{1,129},{3,131},{5,133},{7,135},{9,137},{11,139},{13,141},{15,143}... | collective-permute-start | bytes 24584 | tf_op jit(solution)/shard_map/ppermute | solution.py:406
  62.3 40.2 %copy-start.3 = (f32[128,128]{1,0:T(8,128)S(1)}, f32[128,128]{1,0:T(8,128)}, u32[]{:S(2)}) copy-start(f32[128,128]{1,0:T(8,128)} %days_ref.5) | copy-start | bytes 196612
  97.7 4.8 %collective-permute-start.2 = (f32[16,152,128]{2,1,0:T(8,128)S(1)}, f32[16,152,128]{2,1,0:T(8,128)S(1)}, u32[]{:S(2)}, u32[]{:S(2)}) collective-permute-start(f32[16,152,128]{2,1,0:T(8,128)S(1)} %all_to_all.40.here_ref), channel_id=1, source_target_pairs={{0,1},{1,0},{2,3},{3,2},{4,5},{5,4},{6,7},{7,6},{8,9},{9,8},{10,11... | collective-permute-start | bytes 3735560 | tf_op jit(solution)/shard_map/ppermute | solution.py:341
  102.5 1.2 copy-start.5
  103.7 1.2 copy-start.9
  105.0 1.2 copy-start.12
  106.2 1.2 copy-start.14
  119.5 1.3 copy-start.15
  120.8 1.0 copy-start.17
  121.8 1.0 copy-start.19
  158.9 1.2 copy-start.6
  160.1 1.6 copy-start.16
  161.7 8.9 %copy-start.10 = (f32[32,64,128]{2,1,0:T(8,128)S(1)}, f32[32,64,128]{2,1,0:T(8,128)}, u32[]{:S(2)}) copy-start(f32[32,64,128]{2,1,0:T(8,128)} %copy-done.8) | copy-start | bytes 3145732
  168.7 4.7 %collective-permute-start.3 = (f32[16,144,128]{2,1,0:T(8,128)S(1)}, f32[16,144,128]{2,1,0:T(8,128)S(1)}, u32[]{:S(2)}, u32[]{:S(2)}) collective-permute-start(f32[16,144,128]{2,1,0:T(8,128)S(1)} %get-tuple-element.25), channel_id=1, source_target_pairs={{0,1},{1,0},{2,3},{3,2},{4,5},{5,4},{6,7},{7,6},{8,9},{9,8},{10,11... | collective-permute-start | bytes 3538952 | tf_op jit(solution)/shard_map/ppermute | solution.py:341
  208.2 6.4 %collective-permute-start.4 = (f32[8,128]{1,0:T(8,128)S(1)}, f32[8,128]{1,0:T(8,128)S(1)}, u32[]{:S(2)}, u32[]{:S(2)}) collective-permute-start(f32[8,128]{1,0:T(8,128)S(1)} %get-tuple-element.32), channel_id=1, source_target_pairs={{1,129},{3,131},{5,133},{7,135},{9,137},{11,139},{13,141},{15,143}... | collective-permute-start | bytes 12296 | tf_op jit(solution)/shard_map/ppermute | solution.py:406
  214.6 36.3 %copy-start.20 = (f32[32,64,128]{2,1,0:T(8,128)S(1)}, f32[32,64,128]{2,1,0:T(8,128)}, u32[]{:S(2)}) copy-start(f32[32,64,128]{2,1,0:T(8,128)} %copy-done.19) | copy-start | bytes 3145732
  214.7 36.2 %copy-start.7 = (f32[32,64,128]{2,1,0:T(8,128)S(1)}, f32[32,64,128]{2,1,0:T(8,128)}, u32[]{:S(2)}) copy-start(f32[32,64,128]{2,1,0:T(8,128)} %copy-done.4) | copy-start | bytes 3145732
  214.7 36.2 %copy-start.18 = (f32[32,64,128]{2,1,0:T(8,128)S(1)}, f32[32,64,128]{2,1,0:T(8,128)}, u32[]{:S(2)}) copy-start(f32[32,64,128]{2,1,0:T(8,128)} %copy-done.17) | copy-start | bytes 3145732
  246.2 4.7 %collective-permute-start.5 = (f32[16,144,128]{2,1,0:T(8,128)S(1)}, f32[16,144,128]{2,1,0:T(8,128)S(1)}, u32[]{:S(2)}, u32[]{:S(2)}) collective-permute-start(f32[16,144,128]{2,1,0:T(8,128)S(1)} %all_to_all.44.here_ref), channel_id=1, source_target_pairs={{0,1},{1,0},{2,3},{3,2},{4,5},{5,4},{6,7},{7,6},{8,9},{9,8},{10,11... | collective-permute-start | bytes 3538952 | tf_op jit(solution)/shard_map/ppermute | solution.py:341

commit v2 on v1

--- a/solution.py
+++ b/solution.py
@@ -19,6 +19,7 @@
 GAP = 1e30
 PIECES = 8
 GROUP = 16
+ROOM = 58
 YZ = ("zlo", "y")
 DAY = ("zlo", "y", "core")
 ALL = ("lat", "lon", "zlo", "y", "core")
@@ -125,16 +126,41 @@
         grid_ref[base + p] = out[p * lons : (p + 1) * lons]
 
 
-def first_kernel(mine, core_ref, anomaly_ref, observed_ref, seat_ref, days_ref, ref, coded_ref, sea_ref, grid_ref, gram_ref):
+def fetch(pairs, sems):
+    copies = [pltpu.make_async_copy(src, dst, sems.at[n]) for n, (src, dst) in enumerate(pairs)]
+    for copy in copies:
+        copy.start()
+    return copies
+
+
+def first_kernel(
+    mine, core_ref, anomaly_hbm, observed_hbm, mask_hbm, days_hbm, ref, coded_hbm, sea_hbm,
+    grid_ref, gram_ref, anomaly_ref, observed_ref, mask_ref, days_ref, coded_ref, sea_ref, sems,
+):
     core = core_ref[0, 0]
     half = core if mine else 1 - core
     lats, lons, days = coded_ref.shape
     spokes = ref.shape[0]
     many = PIECES * lats // spokes
+    part = pl.ds(half * lats, lats)
+    copies = fetch(
+        [
+            (days_hbm, days_ref),
+            (mask_hbm, mask_ref),
+            (anomaly_hbm.at[part], anomaly_ref),
+            (observed_hbm.at[part], observed_ref),
+        ],
+        sems,
+    )
+    copies[0].wait()
     temporal = days_ref[...]
     side = right_side(temporal)
     gram_ref[...] = full(temporal, temporal, (((0,), (0,)), ((), ())))
-    seat = seat_ref[...]
+    copies[1].wait()
+    mask = mask_ref[...].astype(f32)
+    seat = jnp.concatenate([mask, jnp.zeros((days - mask.shape[0], lons), f32)], axis=0).T
+    copies[2].wait()
+    copies[3].wait()
 
     def step(g, _):
         rows = []
@@ -143,22 +169,28 @@
             i = half * lats + here
             sea = jnp.broadcast_to(pltpu.roll(seat, lax.rem(seat.shape[1] - i, seat.shape[1]), 1)[:, :1], (lons, days))
             sea_ref[here] = sea
-            seen = observed_ref[i] != 0
-            known = jnp.where(seen, sea * anomaly_ref[i], 0.0)
+            seen = observed_ref[here] != 0
+            known = jnp.where(seen, sea * anomaly_ref[here], 0.0)
             coded_ref[here] = jnp.where(seen | (sea == 0.0), known, GAP)
             rows.append(known)
         put_rows(ref, grid_ref, g, g * many, times(split(jnp.concatenate(rows, axis=0)), side))
         return _
 
     lax.fori_loop(0, spokes // PIECES, step, 0)
+    copies = fetch([(coded_ref, coded_hbm), (sea_ref, sea_hbm)], sems)
     put_block(half, grid_ref, gram_ref, ref)
-
-
-def modes_kernel(first, core_ref, weight_ref, here_ref, there_ref, days_ref, *refs):
-    coded_refs, field_refs, refs = refs[0:2], refs[2:4], refs[4:]
-    spatial_ref, sums_ref = refs[0:2]
-    around_refs = refs[2:4] if first else field_refs
-    pad_ref, rim_ref, wide_ref = refs[-3:]
+    for copy in copies:
+        copy.wait()
+
+
+def modes_kernel(first, core_ref, weight_ref, here_hbm, there_hbm, days_ref, *refs):
+    coded_hbm, field_hbm, refs = refs[0:2], refs[2:4], refs[4:]
+    spatial_hbm, sums_ref = refs[0:2]
+    around_hbm, refs = refs[2 : (4 if first else 2)], refs[(4 if first else 2) :]
+    pad_ref, rim_ref, wide_ref, spatial_ref = refs[0:4]
+    coded_refs, field_refs, refs = refs[4:6], refs[6:8], refs[8:]
+    around_refs = refs[0:2] if first else field_refs
+    gram_ref, here_ref, there_ref, in_sems, out_sems = refs[-5:]
     core = core_ref[0, 0]
     lats, lons, modes = spatial_ref.shape
     deep = lats // 2
@@ -168,6 +200,17 @@
     tiles = 2 if first else 1
     gram_at = cells + 8 * tiles
     halves = (core, 1 - core)
+    loads = fetch(
+        [(here_hbm.at[:, pl.ds(gram_at, 8)], gram_ref), (here_hbm, here_ref), (there_hbm, there_ref)]
+        + list(zip((*field_hbm, *coded_hbm), (*field_refs, *coded_refs))),
+        in_sems,
+    )
+    loads[0].wait()
+    inverse_side = right_side(inverse_spd(add_ridge(gram_ref[...].reshape(modes, modes))))
+    days_side = right_side(days_ref[...].T)
+    for copy in loads[1:]:
+        copy.wait()
+    stores = []
 
     for half, ref in zip(halves, (here_ref, there_ref)):
         for q in range(spokes):
@@ -182,9 +225,6 @@
                 rim_ref[pl.ds(pl.multiple_of(t * 4 * lons + at, 8), 8), :] = ref[q, cells + 8 * t : cells + 8 * t + 8, :]
     pad_ref[0] = rim_ref[lons : 2 * lons, :]
     pad_ref[lats + 1] = rim_ref[0:lons, :]
-    gram = jnp.concatenate([here_ref[q, gram_at : gram_at + 8, :] for q in range(spokes)], axis=0)
-    inverse_side = right_side(inverse_spd(add_ridge(gram)))
-    days_side = right_side(days_ref[...].T)
     row = lax.broadcasted_iota(jnp.int32, (lons, modes), 0)
 
     def beside(value, i, kind):
@@ -210,6 +250,7 @@
                 return _
 
             lax.fori_loop(0, deep, masks, 0, unroll=2)
+            stores += fetch([(around_ref, around_hbm[n])], out_sems.at[pl.ds(2 + n, 1)])
 
     wide_ref[...] = jnp.zeros_like(wide_ref)
     for n, half in enumerate(halves):
@@ -237,18 +278,23 @@
             return _
 
         lax.fori_loop(0, deep // GROUP, step, 0)
+        part = pl.ds(half * deep, deep)
+        stores += fetch([(spatial_ref.at[part], spatial_hbm.at[part])], out_sems.at[pl.ds(n, 1)])
     m = modes
     for part in range(2):
         at = 2 * part * m
         wide = wide_ref[at : at + m, :] + wide_ref[at + m : at + 2 * m, :]
         sums_ref[part * m : (part + 1) * m, :] = wide[:, :m] + wide[:, m:]
-
-
-def days_kernel(mine, core_ref, sums_ref, coded_ref, spatial_ref, ref, *refs):
+    for copy in stores:
+        copy.wait()
+
+
+def days_kernel(mine, core_ref, sums_ref, coded_hbm, spatial_hbm, ref, *refs):
     core = core_ref[0, 0]
     half = core if mine else 1 - core
-    grid_ref, gram_ref = refs[-2:]
+    grid_ref, gram_ref, coded_ref, spatial_ref, sems = refs[-5:]
     lats, lons, modes = coded_ref.shape
+    loads = fetch([(coded_hbm, coded_ref), (spatial_hbm.at[pl.ds(half * lats, lats)], spatial_ref)], sems)
     spokes = ref.shape[0]
     many = PIECES * lats // spokes
     if mine:
@@ -261,8 +307,11 @@
     across = right_side(temporal.T)
     gram_ref[...] = full(temporal, temporal, (((0,), (0,)), ((), ())))
 
+    for copy in loads:
+        copy.wait()
+
     def step(g, _):
-        at = half * lats + g * many
+        at = g * many
         guess = times(split(jnp.concatenate([spatial_ref[at + p] for p in range(many)], axis=0)), across)
         coded = jnp.concatenate([coded_ref[g * many + p] for p in range(many)], axis=0)
         put_rows(ref, grid_ref, g, g * many, times(split(jnp.where(coded == GAP, guess, coded)), side))
@@ -279,28 +328,34 @@
 
 SMEM = pl.BlockSpec(memory_space=pltpu.SMEM)
 VMEM = pl.BlockSpec(memory_space=pltpu.VMEM)
-
-
-def call(kernel, outs, specs, scratch, name, flops, nbytes):
+HBM = pl.BlockSpec(memory_space=pltpu.HBM)
+
+
+def call(kernel, outs, specs, scratch, name, flops, nbytes, room=60):
     return pl.pallas_call(
         kernel,
-        out_shape=[jax.ShapeDtypeStruct(shape, f32) for shape in outs],
+        out_shape=[jax.ShapeDtypeStruct(shape, f32) for shape, _ in outs],
         in_specs=specs,
-        out_specs=[VMEM] * len(outs),
-        scratch_shapes=[pltpu.VMEM(shape, f32) for shape in scratch],
+        out_specs=[place for _, place in outs],
+        scratch_shapes=[pltpu.VMEM(shape, f32) if isinstance(shape, tuple) else shape for shape in scratch],
         name=name,
         cost_estimate=pl.CostEstimate(flops=flops, bytes_accessed=nbytes, transcendentals=0),
-        compiler_params=pltpu.CompilerParams(vmem_limit_bytes=28 * 1024 * 1024),
-    )
-
-
-def first_call(mine, core, anomaly, observed, seat, days, spokes):
+        compiler_params=pltpu.CompilerParams(vmem_limit_bytes=room * 1024 * 1024),
+    )
+
+
+def copy_sems(count):
+    return pltpu.SemaphoreType.DMA((count,))
+
+
+def first_call(mine, core, anomaly, observed, mask, days, spokes):
     lats, lons, n = anomaly.shape
     block = (spokes, lats * lons // (2 * spokes) + 16, n)
     grid = (lats // 2, lons, n)
-    kernel = functools.partial(first_kernel, mine)
-    return call(kernel, [block, grid, grid], [SMEM] + [VMEM] * 4, [grid, (n, n)], "first_projection", 10**9, 10**7)(
-        core, anomaly, observed, seat, days
+    scratch = [grid, (n, n), grid, pltpu.VMEM(grid, jnp.int32), pltpu.VMEM(mask.shape, jnp.int32), (n, n), grid, grid, copy_sems(4)]
+    outs = [(block, VMEM), (grid, HBM), (grid, HBM)]
+    return call(functools.partial(first_kernel, mine), outs, [SMEM] + [HBM] * 4, scratch, "first_projection", 10**9, 10**7)(
+        core, anomaly, observed, mask, days
     )
 
 
@@ -308,9 +363,11 @@
     lats, lons, n = coded[0].shape
     half = (lats, lons, n)
     grid = (2 * lats, lons, n)
-    outs = [grid, (2 * n, n)] + ([half, half] if first else [])
-    scratch = [(2 * lats + 2, lons, n), ((8 if first else 4) * lons, n), (4 * n, 2 * n)]
-    return call(functools.partial(modes_kernel, first), outs, [SMEM, SMEM] + [VMEM] * 7, scratch, "modes_sweep", 2 * 10**9, 10**7)(
+    outs = [(grid, HBM), ((2 * n, n), VMEM)] + ([(half, HBM)] * 2 if first else [])
+    scratch = [(2 * lats + 2, lons, n), ((8 if first else 4) * lons, n), (4 * n, 2 * n), grid] + [half] * (6 if first else 4)
+    scratch += [(here.shape[0], 8, n), here.shape, here.shape, copy_sems(7), copy_sems(4)]
+    specs = [SMEM, SMEM, HBM, HBM, VMEM] + [HBM] * 4
+    return call(functools.partial(modes_kernel, first), outs, specs, scratch, "modes_sweep", 2 * 10**9, 10**7, ROOM)(
         core, weight, here, there, days, *coded, *field
     )
 
@@ -318,16 +375,17 @@
 def days_call(mine, core, sums, coded, spatial, spokes):
     lats, lons, n = coded.shape
     block = (spokes, lats * lons // spokes + 16, n)
-    outs = [block] if mine else [block, (sums.shape[0] - n, n)]
-    kernel = functools.partial(days_kernel, mine)
-    return call(kernel, outs, [SMEM] + [VMEM] * 3, [(lats, lons, n), (n, n)], "days_sweep", 2 * 10**9, 10**7)(
+    outs = [(block, VMEM)] if mine else [(block, VMEM), ((sums.shape[0] - n, n), VMEM)]
+    grid = (lats, lons, n)
+    scratch = [grid, (n, n), grid, grid, copy_sems(2)]
+    return call(functools.partial(days_kernel, mine), outs, [SMEM, VMEM, HBM, HBM], scratch, "days_sweep", 2 * 10**9, 10**7)(
         core, sums, coded, spatial
     )
 
 
 def last_call(sums):
     n = sums.shape[1]
-    return call(last_kernel, [(sums.shape[0] - n, n)], [VMEM], [], "last_days", 10**7, 10**6)(sums)[0]
+    return call(last_kernel, [((sums.shape[0] - n, n), VMEM)], [VMEM], [], "last_days", 10**7, 10**6, 16)(sums)[0]
 
 
 def lat_weights(first_row, row_count, total_rows):
@@ -388,15 +446,14 @@
     cells = rows_lat * cols_lon // (2 * spokes)
     core_word = core.reshape(1, 1).astype(jnp.int32)
     sea_grid = ocean_mask.astype(f32)
-    seat = jnp.pad(sea_grid.T, ((0, 0), (0, rank_count - rows_lat)))
     first_lat = (lax.axis_index("lat") * rows_lat).astype(f32)
     weight = lat_weights(first_lat, rows_lat, float(rows_lat * lats)).reshape(1, rows_lat)
     edge_sea = lax.dynamic_slice_in_dim(edges_of(sea_grid), (core * spokes + spoke) * 8, 8)
     edge_sea = jnp.broadcast_to(edge_sea[:, None], (8, rank_count))
     temporal = start_days
     coded, field = [None, None], [None, None]
-    other, coded[1], field[1] = first_call(False, core_word, anomaly, observed, seat, start_days, spokes)
-    mine, coded[0], field[0] = first_call(True, core_word, anomaly, observed, seat, start_days, spokes)
+    other, coded[1], field[1] = first_call(False, core_word, anomaly, observed, ocean_mask, start_days, spokes)
+    mine, coded[0], field[0] = first_call(True, core_word, anomaly, observed, ocean_mask, start_days, spokes)
     for sweep in range(ITERS):
         half = mine + swap_core(other)
         shard = jnp.sum(lax.all_to_all(half, YZ, 0, 0, tiled=True), axis=0)

time: 299 us -> 299 us (level)
  local copies, waits for them, and re-layouts: 20.4 us -> 2.77 us
  Pallas kernels: 40.5 us -> 56.6 us
  other arithmetic: 1.64 us -> 4.67 us
    unnamed x43 -> x10, local copies, waits for them, and re-layouts: 19.7 us -> 2.11 us
    pallas_call x7, Pallas kernels: 40.5 us -> 56.6 us  [the longest x2 27.2 us: modes_call(): call(functools.partial(modes_kernel, first), outs, specs, scratch, 'modes...]
  transfers between devices with their start and end apart: 7 -> 7, of which waited for: 6 -> 5; matrix products, arithmetic and copies ran while one was open for 0% -> 0% of each run, Pallas kernels for 1% -> 3%
where the time goes in v2:
time: 299 us; the launch traced here: 298 us
  blocking collectives  168 us (56%)
  Pallas kernels  56.6 us (19%)
  waiting for transfers between devices  45.4 us (15%)
  starting transfers between devices  20 us (7%)
  other arithmetic  4.67 us (2%)
    all_to_all x4, blocking collectives, gather_all(): return lax.all_to_all(spread, axes, 0, 0, tiled=True)  94.4 us
    all_to_all x2, blocking collectives, sum_cells(): lax.all_to_all(value.reshape(size, rows // size, -1), LL, 0, 0, tiled=True)  38.8 us
    all_to_all x1, blocking collectives, on_device(): shard = jnp.sum(lax.all_to_all(half, YZ, 0, 0, tiled=True), axis=0)  35 us
    all_to_all x1, waiting for transfers between devices, on_device(): shard = jnp.sum(lax.all_to_all(half, YZ, 0, 0, tiled=True), axis=0)  29.1 us
    pallas_call x2, Pallas kernels, modes_call(): call(functools.partial(modes_kernel, first), outs, specs, scratch, 'modes...  27.2 us
    pallas_call x2, Pallas kernels, days_call(): call(functools.partial(days_kernel, mine), outs, [SMEM, VMEM, HBM, HBM],...  13.5 us
    ppermute x2, waiting for transfers between devices, on_device(): halo = lax.ppermute(send, ALL, pairs)  11.4 us
    pallas_call x2, Pallas kernels, first_call(): call(functools.partial(first_kernel, mine), outs, [SMEM] + [HBM] * 4, scr...  10.1 us
  transfers between devices with their start and end apart: 7, of which 5 were waited for; matrix products, arithmetic and copies ran while one was open for 0% of the time, Pallas kernels for 3%

profile of v2, /device:TPU:8, one launch (start us, length us, event | category | flops | bytes accessed | tf_op | source)
XLA Modules:
  0.0 298.4 jit_solution(12964456876367415249)
XLA Ops:
  0.6 5.0 %first_projection.3 = (f32[16,144,128]{2,1,0:T(8,128)}, f32[32,64,128]{2,1,0:T(8,128)}, f32[32,64,128]{2,1,0:T(8,128)}) custom-call(s32[1,1]{1,0:T(1,128)} %bitcast.core_ref, f32[64,64,128]{2,1,0:T(8,128)} %anomaly_hbm.3, s32[64,64,128]{2,1,0:T(8,128)} %observed_hbm.3, s32[64,64]{1,0:T(8,128)} %mask_hbm.3, f32[128,128]{1,0:T(8,128)} %days_ref.1), custom_call_target="tpu_custom_call" | custom-call | flops 1000000000 | bytes 10000000 | tf_op jit(solution)/shard_map/first_projection/pallas_call | solution.py:357
  5.6 1.9 collective-permute-start
  7.5 5.1 %first_projection.2 = (f32[16,144,128]{2,1,0:T(8,128)}, f32[32,64,128]{2,1,0:T(8,128)}, f32[32,64,128]{2,1,0:T(8,128)}) custom-call(s32[1,1]{1,0:T(1,128)} %bitcast.core_ref, f32[64,64,128]{2,1,0:T(8,128)} %anomaly_hbm.3, s32[64,64,128]{2,1,0:T(8,128)} %observed_hbm.3, s32[64,64]{1,0:T(8,128)} %mask_hbm.3, f32[128,128]{1,0:T(8,128)} %days_ref.1), custom_call_target="tpu_custom_call" | custom-call | flops 1000000000 | bytes 10000000 | tf_op jit(solution)/shard_map/first_projection/pallas_call | solution.py:357
  12.7 0.0 collective-permute-done
  12.7 2.4 add.60
  15.1 0.0 copy-start.2
  15.1 9.5 %all-to-all-start = ((f32[16,144,128]{2,1,0:T(8,128)}), f32[16,144,128]{2,1,0:T(8,128)S(1)}, u32[]{:S(2)}, u32[]{:S(2)}) async-start(f32[16,144,128]{2,1,0:T(8,128)} %add.60), calls=%async_computation | async-start | bytes 2359296 | tf_op jit(solution)/shard_map/all_to_all | solution.py:459
  24.6 0.0 copy-done.2
  24.6 0.2 slice_reduce_fusion
  24.9 0.1 concatenate.12
  24.9 0.1 dynamic_slice.3
  25.0 0.1 pad.7.clone
  25.1 29.1 %all-to-all-done = f32[16,144,128]{2,1,0:T(8,128)S(1)} async-done(((f32[16,144,128]{2,1,0:T(8,128)}), f32[16,144,128]{2,1,0:T(8,128)S(1)}, u32[]{:S(2)}, u32[]{:S(2)}) %all-to-all-start) | async-done | bytes 1179680 | tf_op jit(solution)/shard_map/all_to_all | solution.py:459
  54.2 0.1 reduce_sum.36
  54.2 0.1 pad_maximum_fusion.2
  54.3 1.3 collective-permute-start.1
  55.6 6.4 %collective-permute-done.1 = f32[16,128]{1,0:T(8,128)S(1)} collective-permute-done((f32[16,128]{1,0:T(8,128)S(1)}, f32[16,128]{1,0:T(8,128)S(1)}, u32[]{:S(2)}, u32[]{:S(2)}) %collective-permute-start.1) | collective-permute-done | bytes 8224 | tf_op jit(solution)/shard_map/ppermute | solution.py:463
  62.0 0.1 broadcast_in_dim.11
  62.1 35.3 %all_to_all.40.here_hbm = f32[16,152,128]{2,1,0:T(8,128)S(1)} all-to-all(f32[16,152,128]{2,1,0:T(8,128)S(1)} %broadcast_in_dim.11), channel_id=1, replica_groups=mesh['lat'=4,'lon'=4,'zlo'=2,'y'=8,'core'=2] {'zlo','y'}, dimensions={0} | all-to-all | bytes 2490368 | tf_op jit(solution)/shard_map/all_to_all | solution.py:421
  97.3 0.0 copy-start
  97.3 1.9 collective-permute-start.2
  99.3 0.6 multiply_divide_fusion.weight_ref
  99.9 2.3 collective-permute-done.2.there_hbm
  102.2 0.0 copy-start.3
  102.2 0.0 copy-done
  102.2 1.1 copy-done.3
  103.2 14.2 %modes_sweep.2 = (f32[64,64,128]{2,1,0:T(8,128)}, f32[256,128]{1,0:T(8,128)}, f32[32,64,128]{2,1,0:T(8,128)}, f32[32,64,128]{2,1,0:T(8,128)}) custom-call(s32[1,1]{1,0:T(1,128)} %bitcast.core_ref, f32[1,64]{1,0:T(1,128)} %multiply_divide_fusion.weight_ref, f32[16,152,128]{2,1,0:T(8,128)} %copy-done, f32[16,152,128]{2,1,0:T(8,128)} %copy-done.3, ...), custom_call_target="tpu_custom_call" | custom-call | flops 2000000000 | bytes 10000000 | tf_op jit(solution)/shard_map/modes_sweep/pallas_call | solution.py:370
  117.5 22.6 %all_to_all.41 = f32[16,16,128]{2,1,0:T(8,128)S(1)} all-to-all(f32[16,16,128]{2,1,0:T(8,128)} %bitcast.11), channel_id=1, replica_groups=mesh['lat'=4,'lon'=4,'zlo'=2,'y'=8,'core'=2] {'lat','lon'}, dimensions={0} | all-to-all | bytes 262144 | tf_op jit(solution)/shard_map/all_to_all | solution.py:427
  140.1 13.8 %all_to_all.42 = f32[16,16,128]{2,1,0:T(8,128)} all-to-all(f32[16,16,128]{2,1,0:T(8,128)S(1)} %broadcast_in_dim.12), channel_id=1, replica_groups=mesh['lat'=4,'lon'=4,'zlo'=2,'y'=8,'core'=2] {'lat','lon'}, dimensions={0} | all-to-all | bytes 262144 | tf_op jit(solution)/shard_map/all_to_all | solution.py:421
  153.9 8.9 %days_sweep.2 = (f32[16,144,128]{2,1,0:T(8,128)}, f32[128,128]{1,0:T(8,128)}) custom-call(s32[1,1]{1,0:T(1,128)} %bitcast.core_ref, f32[256,128]{1,0:T(8,128)} %bitcast.12, f32[32,64,128]{2,1,0:T(8,128)} %get-tuple-element.19.refs_1_.coded_hbm, f32[64,64,128]{2,1,0:T(8,128)} %get-tuple-element.23.spatial_hbm), custom_call_target="tpu_custom_call" | custom-call | flops 2000000000 | bytes 10000000 | tf_op jit(solution)/shard_map/days_sweep/pallas_call | solution.py:381
  162.8 1.9 collective-permute-start.3
  164.7 4.6 %days_sweep.3 = f32[16,144,128]{2,1,0:T(8,128)} custom-call(s32[1,1]{1,0:T(1,128)} %bitcast.core_ref, f32[128,128]{1,0:T(8,128)} %get-tuple-element.24.sums_ref.days_ref, f32[32,64,128]{2,1,0:T(8,128)} %get-tuple-element.18.refs_0_.coded_hbm, f32[64,64,128]{2,1,0:T(8,128)} %get-tuple-element.23.spatial_hbm), custom_call_target="tpu_custom_call" | custom-call | flops 2000000000 | bytes 10000000 | tf_op jit(solution)/shard_map/days_sweep/pallas_call | solution.py:381
  169.3 0.0 collective-permute-done.3
  169.3 1.4 add.64
  170.7 35.0 %all_to_all.43 = f32[16,144,128]{2,1,0:T(8,128)S(1)} all-to-all(f32[16,144,128]{2,1,0:T(8,128)S(1)} %add.64), channel_id=1, replica_groups=mesh['lat'=4,'lon'=4,'zlo'=2,'y'=8,'core'=2] {'zlo','y'}, dimensions={0} | all-to-all | bytes 2359296 | tf_op jit(solution)/shard_map/all_to_all | solution.py:459
  205.7 0.1 reduce_sum.38
  205.8 1.3 collective-permute-start.4
  207.1 5.1 %collective-permute-done.4 = f32[8,128]{1,0:T(8,128)S(1)} collective-permute-done((f32[8,128]{1,0:T(8,128)S(1)}, f32[8,128]{1,0:T(8,128)S(1)}, u32[]{:S(2)}, u32[]{:S(2)}) %collective-permute-start.4) | collective-permute-done | bytes 4128 | tf_op jit(solution)/shard_map/ppermute | solution.py:463
  212.2 0.1 broadcast_in_dim.13
  212.3 31.6 %all_to_all.44.here_hbm = f32[16,144,128]{2,1,0:T(8,128)S(1)} all-to-all(f32[16,144,128]{2,1,0:T(8,128)S(1)} %broadcast_in_dim.13), channel_id=1, replica_groups=mesh['lat'=4,'lon'=4,'zlo'=2,'y'=8,'core'=2] {'zlo','y'}, dimensions={0} | all-to-all | bytes 2359296 | tf_op jit(solution)/shard_map/all_to_all | solution.py:421
  243.8 2.1 collective-permute-start.5
  246.0 2.6 collective-permute-done.5.there_hbm
  248.6 0.0 copy-done.1
  248.6 1.0 copy-done.4
  249.6 12.9 %modes_sweep.3 = (f32[64,64,128]{2,1,0:T(8,128)}, f32[256,128]{1,0:T(8,128)}) custom-call(s32[1,1]{1,0:T(1,128)} %bitcast.core_ref, f32[1,64]{1,0:T(1,128)} %multiply_divide_fusion.weight_ref, f32[16,144,128]{2,1,0:T(8,128)} %copy-done.1, f32[16,144,128]{2,1,0:T(8,128)} %copy-done.4, f32[128,128]{1,0:T(8,128)} %get-tuple-element.24.sums_ref.days_ref, ...), custom_call_target="tpu_custom_call" | custom-call | flops 2000000000 | bytes 10000000 | tf_op jit(solution)/shard_map/modes_sweep/pallas_call | solution.py:370
  262.5 16.2 %all_to_all.45 = f32[16,16,128]{2,1,0:T(8,128)S(1)} all-to-all(f32[16,16,128]{2,1,0:T(8,128)} %bitcast.10), channel_id=1, replica_groups=mesh['lat'=4,'lon'=4,'zlo'=2,'y'=8,'core'=2] {'lat','lon'}, dimensions={0} | all-to-all | bytes 262144 | tf_op jit(solution)/shard_map/all_to_all | solution.py:427
  278.8 13.7 %all_to_all.46 = f32[16,16,128]{2,1,0:T(8,128)S(1)} all-to-all(f32[16,16,128]{2,1,0:T(8,128)S(1)} %broadcast_in_dim.14), channel_id=1, replica_groups=mesh['lat'=4,'lon'=4,'zlo'=2,'y'=8,'core'=2] {'lat','lon'}, dimensions={0} | all-to-all | bytes 262144 | tf_op jit(solution)/shard_map/all_to_all | solution.py:421
  292.5 5.9 %last_days.1 = f32[128,128]{1,0:T(8,128)} custom-call(f32[256,128]{1,0:T(8,128)S(1)} %bitcast.9), custom_call_target="tpu_custom_call" | custom-call | flops 10000000 | bytes 1000000 | tf_op jit(solution)/shard_map/last_days/pallas_call | solution.py:388
  (14 shorter events, 0.1 us)
Async XLA Ops:
  5.6 7.1 %collective-permute-start = (f32[16,144,128]{2,1,0:T(8,128)}, f32[16,144,128]{2,1,0:T(8,128)S(1)}, u32[]{:S(2)}, u32[]{:S(2)}) collective-permute-start(f32[16,144,128]{2,1,0:T(8,128)} %get-tuple-element.17), channel_id=1, source_target_pairs={{0,1},{1,0},{2,3},{3,2},{4,5},{5,4},{6,7},{7,6},{8,9},{9,8},{10,11... | collective-permute-start | bytes 3538952 | tf_op jit(solution)/shard_map/ppermute | solution.py:399
  15.1 9.5 %copy-start.2 = (s32[64,64]{1,0:T(8,128)S(1)}, s32[64,64]{1,0:T(8,128)}, u32[]{:S(2)}) copy-start(s32[64,64]{1,0:T(8,128)} %mask_hbm.3) | copy-start | bytes 49156
  15.1 39.1 %all-to-all-start = ((f32[16,144,128]{2,1,0:T(8,128)}), f32[16,144,128]{2,1,0:T(8,128)S(1)}, u32[]{:S(2)}, u32[]{:S(2)}) async-start(f32[16,144,128]{2,1,0:T(8,128)} %add.60), calls=%async_computation | async-start | bytes 2359296 | tf_op jit(solution)/shard_map/all_to_all | solution.py:459
  54.3 7.7 %collective-permute-start.1 = (f32[16,128]{1,0:T(8,128)S(1)}, f32[16,128]{1,0:T(8,128)S(1)}, u32[]{:S(2)}, u32[]{:S(2)}) collective-permute-start(f32[16,128]{1,0:T(8,128)S(1)} %pad_maximum_fusion.2), channel_id=1, source_target_pairs={{1,129},{3,131},{5,133},{7,135},{9,137},{11,139},{13,141},{15,143}... | collective-permute-start | bytes 24584 | tf_op jit(solution)/shard_map/ppermute | solution.py:463
  97.3 4.8 %copy-start = (f32[16,152,128]{2,1,0:T(8,128)}, f32[16,152,128]{2,1,0:T(8,128)S(1)}, u32[]{:S(2)}) copy-start(f32[16,152,128]{2,1,0:T(8,128)S(1)} %all_to_all.40.here_hbm) | copy-start | bytes 3735556
  97.3 4.8 %collective-permute-start.2 = (f32[16,152,128]{2,1,0:T(8,128)S(1)}, f32[16,152,128]{2,1,0:T(8,128)S(1)}, u32[]{:S(2)}, u32[]{:S(2)}) collective-permute-start(f32[16,152,128]{2,1,0:T(8,128)S(1)} %all_to_all.40.here_hbm), channel_id=1, source_target_pairs={{0,1},{1,0},{2,3},{3,2},{4,5},{5,4},{6,7},{7,6},{8,9},{9,8},{10,11... | collective-permute-start | bytes 3735560 | tf_op jit(solution)/shard_map/ppermute | solution.py:399
  102.2 1.1 copy-start.3
  162.8 6.5 %collective-permute-start.3 = (f32[16,144,128]{2,1,0:T(8,128)}, f32[16,144,128]{2,1,0:T(8,128)S(1)}, u32[]{:S(2)}, u32[]{:S(2)}) collective-permute-start(f32[16,144,128]{2,1,0:T(8,128)} %get-tuple-element.25), channel_id=1, source_target_pairs={{0,1},{1,0},{2,3},{3,2},{4,5},{5,4},{6,7},{7,6},{8,9},{9,8},{10,11... | collective-permute-start | bytes 3538952 | tf_op jit(solution)/shard_map/ppermute | solution.py:399
  205.8 6.4 %collective-permute-start.4 = (f32[8,128]{1,0:T(8,128)S(1)}, f32[8,128]{1,0:T(8,128)S(1)}, u32[]{:S(2)}, u32[]{:S(2)}) collective-permute-start(f32[8,128]{1,0:T(8,128)S(1)} %get-tuple-element.34), channel_id=1, source_target_pairs={{1,129},{3,131},{5,133},{7,135},{9,137},{11,139},{13,141},{15,143}... | collective-permute-start | bytes 12296 | tf_op jit(solution)/shard_map/ppermute | solution.py:463
  243.8 4.7 %copy-start.1 = (f32[16,144,128]{2,1,0:T(8,128)}, f32[16,144,128]{2,1,0:T(8,128)S(1)}, u32[]{:S(2)}) copy-start(f32[16,144,128]{2,1,0:T(8,128)S(1)} %all_to_all.44.here_hbm) | copy-start | bytes 3538948
  243.8 4.7 %collective-permute-start.5 = (f32[16,144,128]{2,1,0:T(8,128)S(1)}, f32[16,144,128]{2,1,0:T(8,128)S(1)}, u32[]{:S(2)}, u32[]{:S(2)}) collective-permute-start(f32[16,144,128]{2,1,0:T(8,128)S(1)} %all_to_all.44.here_hbm), channel_id=1, source_target_pairs={{0,1},{1,0},{2,3},{3,2},{4,5},{5,4},{6,7},{7,6},{8,9},{9,8},{10,11... | collective-permute-start | bytes 3538952 | tf_op jit(solution)/shard_map/ppermute | solution.py:399
  248.5 1.1 copy-start.4

commit v3 on v2

--- a/solution.py
+++ b/solution.py
@@ -19,7 +19,9 @@
 GAP = 1e30
 PIECES = 8
 GROUP = 16
-ROOM = 58
+FIRST_ROOM = 57
+ROOM = 50
+SHELF = 384
 YZ = ("zlo", "y")
 DAY = ("zlo", "y", "core")
 ALL = ("lat", "lon", "zlo", "y", "core")
@@ -134,63 +136,62 @@
 
 
 def first_kernel(
-    mine, core_ref, anomaly_hbm, observed_hbm, mask_hbm, days_hbm, ref, coded_hbm, sea_hbm,
-    grid_ref, gram_ref, anomaly_ref, observed_ref, mask_ref, days_ref, coded_ref, sea_ref, sems,
+    mine, core_ref, anomaly_hbm, observed_hbm, mask_hbm, days_hbm, ref, shelf_hbm,
+    grid_ref, gram_ref, anomaly_ref, observed_ref, mask_ref, days_ref, coded_ref, sea_ref, seat_ref, sems,
 ):
     core = core_ref[0, 0]
     half = core if mine else 1 - core
     lats, lons, days = coded_ref.shape
     spokes = ref.shape[0]
     many = PIECES * lats // spokes
-    part = pl.ds(half * lats, lats)
-    copies = fetch(
-        [
-            (days_hbm, days_ref),
-            (mask_hbm, mask_ref),
-            (anomaly_hbm.at[part], anomaly_ref),
-            (observed_hbm.at[part], observed_ref),
-        ],
-        sems,
-    )
-    copies[0].wait()
+    groups = spokes // PIECES
+    small = fetch([(days_hbm, days_ref), (mask_hbm, mask_ref)], sems)
+    loads, stores = [], []
+    for g in range(groups):
+        away, near = pl.ds(half * lats + g * many, many), pl.ds(g * many, many)
+        pairs = [(anomaly_hbm.at[away], anomaly_ref.at[near]), (observed_hbm.at[away], observed_ref.at[near])]
+        loads.append(fetch(pairs, sems.at[pl.ds(2 + 2 * g, 2)]))
+    small[0].wait()
     temporal = days_ref[...]
     side = right_side(temporal)
     gram_ref[...] = full(temporal, temporal, (((0,), (0,)), ((), ())))
-    copies[1].wait()
+    small[1].wait()
     mask = mask_ref[...].astype(f32)
-    seat = jnp.concatenate([mask, jnp.zeros((days - mask.shape[0], lons), f32)], axis=0).T
-    copies[2].wait()
-    copies[3].wait()
-
-    def step(g, _):
-        rows = []
-        for p in range(many):
-            here = g * many + p
-            i = half * lats + here
-            sea = jnp.broadcast_to(pltpu.roll(seat, lax.rem(seat.shape[1] - i, seat.shape[1]), 1)[:, :1], (lons, days))
-            sea_ref[here] = sea
-            seen = observed_ref[here] != 0
-            known = jnp.where(seen, sea * anomaly_ref[here], 0.0)
-            coded_ref[here] = jnp.where(seen | (sea == 0.0), known, GAP)
-            rows.append(known)
-        put_rows(ref, grid_ref, g, g * many, times(split(jnp.concatenate(rows, axis=0)), side))
-        return _
-
-    lax.fori_loop(0, spokes // PIECES, step, 0)
-    copies = fetch([(coded_ref, coded_hbm), (sea_ref, sea_hbm)], sems)
+    seat_ref[...] = jnp.concatenate([mask, jnp.zeros((days - mask.shape[0], lons), f32)], axis=0).T
+    for g in range(groups):
+        for copy in loads[g]:
+            copy.wait()
+
+        def step(_, carry, g=g):
+            rows = []
+            for p in range(many):
+                here = g * many + p
+                i = half * lats + here
+                turned = pltpu.roll(seat_ref[...], lax.rem(days - i, days), 1)
+                sea = jnp.broadcast_to(turned[:, :1], (lons, days))
+                sea_ref[here] = sea
+                seen = observed_ref[here] != 0
+                known = jnp.where(seen, sea * anomaly_ref[here], 0.0)
+                coded_ref[here] = jnp.where(seen | (sea == 0.0), known, GAP)
+                rows.append(known)
+            put_rows(ref, grid_ref, g, g * many, times(split(jnp.concatenate(rows, axis=0)), side))
+            return carry
+
+        step(0, 0)
+        near = pl.ds(g * many, many)
+        pairs = [(coded_ref.at[near], shelf_hbm.at[near]), (sea_ref.at[near], shelf_hbm.at[pl.ds(lats + g * many, many)])]
+        stores += fetch(pairs, sems.at[pl.ds(2 + 2 * groups + 2 * g, 2)])
     put_block(half, grid_ref, gram_ref, ref)
-    for copy in copies:
+    for copy in stores:
         copy.wait()
 
 
-def modes_kernel(first, core_ref, weight_ref, here_hbm, there_hbm, days_ref, *refs):
-    coded_hbm, field_hbm, refs = refs[0:2], refs[2:4], refs[4:]
-    spatial_hbm, sums_ref = refs[0:2]
-    around_hbm, refs = refs[2 : (4 if first else 2)], refs[(4 if first else 2) :]
-    pad_ref, rim_ref, wide_ref, spatial_ref = refs[0:4]
-    coded_refs, field_refs, refs = refs[4:6], refs[6:8], refs[8:]
+def modes_kernel(first, core_ref, weight_ref, here_ref, there_ref, days_ref, *refs):
+    shelves, refs = refs[0 : (2 if first else 3)], refs[(2 if first else 3) :]
+    out_hbm, sums_ref, pad_ref, rim_ref, wide_ref, spatial_ref = refs[0:6]
+    coded_refs, field_refs, refs = refs[6:8], refs[8:10], refs[10:]
     around_refs = refs[0:2] if first else field_refs
-    gram_ref, here_ref, there_ref, in_sems, out_sems = refs[-5:]
+    in_sems, out_sems = refs[-2:]
     core = core_ref[0, 0]
     lats, lons, modes = spatial_ref.shape
     deep = lats // 2
@@ -200,15 +201,14 @@
     tiles = 2 if first else 1
     gram_at = cells + 8 * tiles
     halves = (core, 1 - core)
-    loads = fetch(
-        [(here_hbm.at[:, pl.ds(gram_at, 8)], gram_ref), (here_hbm, here_ref), (there_hbm, there_ref)]
-        + list(zip((*field_hbm, *coded_hbm), (*field_refs, *coded_refs))),
-        in_sems,
-    )
-    loads[0].wait()
-    inverse_side = right_side(inverse_spd(add_ridge(gram_ref[...].reshape(modes, modes))))
+    fields = [(shelves[n], deep) if first else (shelves[2], n * deep) for n in range(2)]
+    pairs = [(shelf.at[pl.ds(at, deep)], field_refs[n]) for n, (shelf, at) in enumerate(fields)]
+    pairs += [(shelves[n].at[pl.ds(0, deep)], coded_refs[n]) for n in range(2)]
+    loads = fetch(pairs, in_sems)
+    gram = jnp.concatenate([here_ref[q, gram_at : gram_at + 8, :] for q in range(spokes)], axis=0)
+    inverse_side = right_side(inverse_spd(add_ridge(gram)))
     days_side = right_side(days_ref[...].T)
-    for copy in loads[1:]:
+    for copy in loads:
         copy.wait()
     stores = []
 
@@ -250,7 +250,7 @@
                 return _
 
             lax.fori_loop(0, deep, masks, 0, unroll=2)
-            stores += fetch([(around_ref, around_hbm[n])], out_sems.at[pl.ds(2 + n, 1)])
+            stores += fetch([(around_ref, out_hbm.at[pl.ds(n * deep, deep)])], out_sems.at[pl.ds(2 + n, 1)])
 
     wide_ref[...] = jnp.zeros_like(wide_ref)
     for n, half in enumerate(halves):
@@ -279,7 +279,8 @@
 
         lax.fori_loop(0, deep // GROUP, step, 0)
         part = pl.ds(half * deep, deep)
-        stores += fetch([(spatial_ref.at[part], spatial_hbm.at[part])], out_sems.at[pl.ds(n, 1)])
+        target = pl.ds(half * deep + (lats if first else 0), deep)
+        stores += fetch([(spatial_ref.at[part], out_hbm.at[target])], out_sems.at[pl.ds(n, 1)])
     m = modes
     for part in range(2):
         at = 2 * part * m
@@ -289,12 +290,13 @@
         copy.wait()
 
 
-def days_kernel(mine, core_ref, sums_ref, coded_hbm, spatial_hbm, ref, *refs):
+def days_kernel(mine, core_ref, sums_ref, shelf_hbm, modes_hbm, ref, *refs):
     core = core_ref[0, 0]
     half = core if mine else 1 - core
     grid_ref, gram_ref, coded_ref, spatial_ref, sems = refs[-5:]
     lats, lons, modes = coded_ref.shape
-    loads = fetch([(coded_hbm, coded_ref), (spatial_hbm.at[pl.ds(half * lats, lats)], spatial_ref)], sems)
+    pairs = [(shelf_hbm.at[pl.ds(0, lats)], coded_ref), (modes_hbm.at[pl.ds((2 + half) * lats, lats)], spatial_ref)]
+    loads = fetch(pairs, sems)
     spokes = ref.shape[0]
     many = PIECES * lats // spokes
     if mine:
@@ -352,34 +354,36 @@
     lats, lons, n = anomaly.shape
     block = (spokes, lats * lons // (2 * spokes) + 16, n)
     grid = (lats // 2, lons, n)
-    scratch = [grid, (n, n), grid, pltpu.VMEM(grid, jnp.int32), pltpu.VMEM(mask.shape, jnp.int32), (n, n), grid, grid, copy_sems(4)]
-    outs = [(block, VMEM), (grid, HBM), (grid, HBM)]
-    return call(functools.partial(first_kernel, mine), outs, [SMEM] + [HBM] * 4, scratch, "first_projection", 10**9, 10**7)(
+    scratch = [grid, (n, n), grid, pltpu.VMEM(grid, jnp.int32), pltpu.VMEM(mask.shape, jnp.int32), (n, n), grid, grid]
+    scratch += [(lons, n), copy_sems(2 + 4 * (spokes // PIECES))]
+    outs = [(block, VMEM), ((SHELF, lons, n), HBM)]
+    specs = [SMEM] + [HBM] * 4
+    return call(functools.partial(first_kernel, mine), outs, specs, scratch, "first_projection", 10**9, 10**7, FIRST_ROOM)(
         core, anomaly, observed, mask, days
     )
 
 
-def modes_call(first, core, weight, here, there, days, coded, field):
-    lats, lons, n = coded[0].shape
-    half = (lats, lons, n)
-    grid = (2 * lats, lons, n)
-    outs = [(grid, HBM), ((2 * n, n), VMEM)] + ([(half, HBM)] * 2 if first else [])
-    scratch = [(2 * lats + 2, lons, n), ((8 if first else 4) * lons, n), (4 * n, 2 * n), grid] + [half] * (6 if first else 4)
-    scratch += [(here.shape[0], 8, n), here.shape, here.shape, copy_sems(7), copy_sems(4)]
-    specs = [SMEM, SMEM, HBM, HBM, VMEM] + [HBM] * 4
+def modes_call(first, core, weight, here, there, days, shelves, lats):
+    _, lons, n = shelves[0].shape
+    half = (lats // 2, lons, n)
+    grid = (lats, lons, n)
+    outs = [((SHELF, lons, n) if first else grid, HBM), ((2 * n, n), VMEM)]
+    scratch = [(lats + 2, lons, n), ((8 if first else 4) * lons, n), (4 * n, 2 * n), grid] + [half] * (6 if first else 4)
+    scratch += [copy_sems(4), copy_sems(4)]
+    specs = [SMEM, SMEM] + [VMEM] * 3 + [HBM] * len(shelves)
     return call(functools.partial(modes_kernel, first), outs, specs, scratch, "modes_sweep", 2 * 10**9, 10**7, ROOM)(
-        core, weight, here, there, days, *coded, *field
+        core, weight, here, there, days, *shelves
     )
 
 
-def days_call(mine, core, sums, coded, spatial, spokes):
-    lats, lons, n = coded.shape
-    block = (spokes, lats * lons // spokes + 16, n)
+def days_call(mine, core, sums, shelf, modes, spokes, lats):
+    _, lons, n = shelf.shape
+    block = (spokes, lats * lons // (2 * spokes) + 16, n)
     outs = [(block, VMEM)] if mine else [(block, VMEM), ((sums.shape[0] - n, n), VMEM)]
-    grid = (lats, lons, n)
+    grid = (lats // 2, lons, n)
     scratch = [grid, (n, n), grid, grid, copy_sems(2)]
-    return call(functools.partial(days_kernel, mine), outs, [SMEM, VMEM, HBM, HBM], scratch, "days_sweep", 2 * 10**9, 10**7)(
-        core, sums, coded, spatial
+    return call(functools.partial(days_kernel, mine), outs, [SMEM, VMEM, HBM, HBM], scratch, "days_sweep", 2 * 10**9, 10**7, ROOM)(
+        core, sums, shelf, modes
     )
 
 
@@ -451,9 +455,9 @@
     edge_sea = lax.dynamic_slice_in_dim(edges_of(sea_grid), (core * spokes + spoke) * 8, 8)
     edge_sea = jnp.broadcast_to(edge_sea[:, None], (8, rank_count))
     temporal = start_days
-    coded, field = [None, None], [None, None]
-    other, coded[1], field[1] = first_call(False, core_word, anomaly, observed, ocean_mask, start_days, spokes)
-    mine, coded[0], field[0] = first_call(True, core_word, anomaly, observed, ocean_mask, start_days, spokes)
+    shelves = [None, None]
+    other, shelves[1] = first_call(False, core_word, anomaly, observed, ocean_mask, start_days, spokes)
+    mine, shelves[0] = first_call(True, core_word, anomaly, observed, ocean_mask, start_days, spokes)
     for sweep in range(ITERS):
         half = mine + swap_core(other)
         shard = jnp.sum(lax.all_to_all(half, YZ, 0, 0, tiled=True), axis=0)
@@ -464,13 +468,13 @@
         shard = jnp.concatenate([shard[:cells], halo, shard[cells + 8 :]], axis=0)
         here = gather_all(shard, YZ, spokes)
         there = swap_core(here)
-        out = modes_call(sweep == 0, core_word, weight, here, there, temporal, coded, field)
-        spatial, sums = out[0], sum_cells(out[1])
+        spatial, sums = modes_call(sweep == 0, core_word, weight, here, there, temporal, shelves, rows_lat)
+        sums = sum_cells(sums)
         if sweep == 0:
-            field = out[2:4]
+            shelves.append(spatial)
         if sweep < ITERS - 1:
-            other, temporal = days_call(False, core_word, sums, coded[1], spatial, spokes)
-            (mine,) = days_call(True, core_word, temporal, coded[0], spatial, spokes)
+            other, temporal = days_call(False, core_word, sums, shelves[1], spatial, spokes, rows_lat)
+            (mine,) = days_call(True, core_word, temporal, shelves[0], spatial, spokes, rows_lat)
         else:
             temporal = last_call(sums)
     return (spatial, temporal)

time: 299 us -> 288 us (0.963)
  Pallas kernels: 56.6 us -> 49.7 us
    pallas_call x2, Pallas kernels: 27.2 us -> 23.5 us  [modes_call(): call(functools.partial(modes_kernel, first), outs, specs, scratch, 'modes...]
  transfers between devices with their start and end apart: 7 -> 7, of which waited for: 5 -> 6; matrix products, arithmetic and copies ran while one was open for 0% -> 0% of each run, Pallas kernels for 3% -> 3%
where the time goes in v3:
time: 288 us; the launch traced here: 287 us
  blocking collectives  167 us (58%)
  Pallas kernels  49.7 us (17%)
  waiting for transfers between devices  46.1 us (16%)
  starting transfers between devices  20 us (7%)
    all_to_all x4, blocking collectives, gather_all(): return lax.all_to_all(spread, axes, 0, 0, tiled=True)  94.5 us
    all_to_all x2, blocking collectives, sum_cells(): lax.all_to_all(value.reshape(size, rows // size, -1), LL, 0, 0, tiled=True)  38 us
    all_to_all x1, blocking collectives, on_device(): shard = jnp.sum(lax.all_to_all(half, YZ, 0, 0, tiled=True), axis=0)  34.7 us
    all_to_all x1, waiting for transfers between devices, on_device(): shard = jnp.sum(lax.all_to_all(half, YZ, 0, 0, tiled=True), axis=0)  29.1 us
    pallas_call x2, Pallas kernels, modes_call(): call(functools.partial(modes_kernel, first), outs, specs, scratch, 'modes...  23.5 us
    ppermute x2, waiting for transfers between devices, on_device(): halo = lax.ppermute(send, ALL, pairs)  11.4 us
    pallas_call x2, Pallas kernels, days_call(): call(functools.partial(days_kernel, mine), outs, [SMEM, VMEM, HBM, HBM],...  10.9 us
    all_to_all x1, starting transfers between devices, on_device(): shard = jnp.sum(lax.all_to_all(half, YZ, 0, 0, tiled=True), axis=0)  9.5 us
  transfers between devices with their start and end apart: 7, of which 6 were waited for; matrix products, arithmetic and copies ran while one was open for 0% of the time, Pallas kernels for 3%

profile of v3, /device:TPU:8, one launch (start us, length us, event | category | flops | bytes accessed | tf_op | source)
XLA Modules:
  0.0 287.4 jit_solution(6224966203600777136)
XLA Ops:
  0.6 4.7 %first_projection.3 = (f32[16,144,128]{2,1,0:T(8,128)}, f32[384,64,128]{2,1,0:T(8,128)}) custom-call(s32[1,1]{1,0:T(1,128)} %bitcast.core_ref, f32[64,64,128]{2,1,0:T(8,128)} %anomaly_hbm.3, s32[64,64,128]{2,1,0:T(8,128)} %observed_hbm.3, s32[64,64]{1,0:T(8,128)} %mask_hbm.3, f32[128,128]{1,0:T(8,128)} %days_ref.1), custom_call_target="tpu_custom_call" | custom-call | flops 1000000000 | bytes 10000000 | tf_op jit(solution)/shard_map/first_projection/pallas_call | solution.py:361
  5.4 1.9 collective-permute-start
  7.3 4.6 %first_projection.2 = (f32[16,144,128]{2,1,0:T(8,128)}, f32[384,64,128]{2,1,0:T(8,128)}) custom-call(s32[1,1]{1,0:T(1,128)} %bitcast.core_ref, f32[64,64,128]{2,1,0:T(8,128)} %anomaly_hbm.3, s32[64,64,128]{2,1,0:T(8,128)} %observed_hbm.3, s32[64,64]{1,0:T(8,128)} %mask_hbm.3, f32[128,128]{1,0:T(8,128)} %days_ref.1), custom_call_target="tpu_custom_call" | custom-call | flops 1000000000 | bytes 10000000 | tf_op jit(solution)/shard_map/first_projection/pallas_call | solution.py:361
  11.9 0.0 collective-permute-done
  11.9 2.4 add.60
  14.3 0.0 copy-start.1
  14.3 9.5 %all-to-all-start = ((f32[16,144,128]{2,1,0:T(8,128)}), f32[16,144,128]{2,1,0:T(8,128)S(1)}, u32[]{:S(2)}, u32[]{:S(2)}) async-start(f32[16,144,128]{2,1,0:T(8,128)} %add.60), calls=%async_computation | async-start | bytes 2359296 | tf_op jit(solution)/shard_map/all_to_all | solution.py:463
  23.8 0.0 copy-done.1
  23.9 0.2 slice_reduce_fusion
  24.1 0.1 concatenate.12
  24.2 0.1 dynamic_slice.3
  24.3 0.1 pad.7.clone
  24.3 29.1 %all-to-all-done = f32[16,144,128]{2,1,0:T(8,128)S(1)} async-done(((f32[16,144,128]{2,1,0:T(8,128)}), f32[16,144,128]{2,1,0:T(8,128)S(1)}, u32[]{:S(2)}, u32[]{:S(2)}) %all-to-all-start) | async-done | bytes 1179680 | tf_op jit(solution)/shard_map/all_to_all | solution.py:463
  53.4 0.1 reduce_sum.36
  53.5 0.1 pad_maximum_fusion.2
  53.6 1.3 collective-permute-start.1
  54.9 6.3 %collective-permute-done.1 = f32[16,128]{1,0:T(8,128)S(1)} collective-permute-done((f32[16,128]{1,0:T(8,128)S(1)}, f32[16,128]{1,0:T(8,128)S(1)}, u32[]{:S(2)}, u32[]{:S(2)}) %collective-permute-start.1) | collective-permute-done | bytes 8224 | tf_op jit(solution)/shard_map/ppermute | solution.py:467
  61.2 0.1 broadcast_in_dim.11
  61.3 0.0 copy-start
  61.3 35.4 %all_to_all.40.here_ref = f32[16,152,128]{2,1,0:T(8,128)S(1)} all-to-all(f32[16,152,128]{2,1,0:T(8,128)S(1)} %broadcast_in_dim.11), channel_id=1, replica_groups=mesh['lat'=4,'lon'=4,'zlo'=2,'y'=8,'core'=2] {'zlo','y'}, dimensions={0} | all-to-all | bytes 2490368 | tf_op jit(solution)/shard_map/all_to_all | solution.py:425
  96.7 1.9 collective-permute-start.2
  98.6 0.1 multiply_divide_fusion.weight_ref
  98.7 2.8 collective-permute-done.2.there_ref
  101.5 0.0 copy-done
  101.6 12.4 %modes_sweep.2 = (f32[384,64,128]{2,1,0:T(8,128)}, f32[256,128]{1,0:T(8,128)S(1)}) custom-call(s32[1,1]{1,0:T(1,128)} %bitcast.core_ref, f32[1,64]{1,0:T(1,128)S(1)} %multiply_divide_fusion.weight_ref, f32[16,152,128]{2,1,0:T(8,128)S(1)} %all_to_all.40.here_ref, f32[16,152,128]{2,1,0:T(8,128)S(1)} %collective-permute-done.2.there_ref, ...), custom_call_target="tpu_custom_call" | custom-call | flops 2000000000 | bytes 10000000 | tf_op jit(solution)/shard_map/modes_sweep/pallas_call | solution.py:374
  114.0 22.4 %all_to_all.41 = f32[16,16,128]{2,1,0:T(8,128)S(1)} all-to-all(f32[16,16,128]{2,1,0:T(8,128)S(1)} %bitcast.12), channel_id=1, replica_groups=mesh['lat'=4,'lon'=4,'zlo'=2,'y'=8,'core'=2] {'lat','lon'}, dimensions={0} | all-to-all | bytes 262144 | tf_op jit(solution)/shard_map/all_to_all | solution.py:431
  136.4 13.7 %all_to_all.42 = f32[16,16,128]{2,1,0:T(8,128)S(1)} all-to-all(f32[16,16,128]{2,1,0:T(8,128)S(1)} %broadcast_in_dim.12), channel_id=1, replica_groups=mesh['lat'=4,'lon'=4,'zlo'=2,'y'=8,'core'=2] {'lat','lon'}, dimensions={0} | all-to-all | bytes 262144 | tf_op jit(solution)/shard_map/all_to_all | solution.py:425
  150.1 8.2 %days_sweep.2 = (f32[16,144,128]{2,1,0:T(8,128)S(1)}, f32[128,128]{1,0:T(8,128)S(1)}) custom-call(s32[1,1]{1,0:T(1,128)} %bitcast.core_ref, f32[256,128]{1,0:T(8,128)S(1)} %bitcast.9, f32[384,64,128]{2,1,0:T(8,128)} %get-tuple-element.15.refs_1_.shelf_hbm, f32[384,64,128]{2,1,0:T(8,128)} %get-tuple-element.17.modes_hbm.refs_2_), custom_call_target="tpu_custom_call" | custom-call | flops 2000000000 | bytes 10000000 | tf_op jit(solution)/shard_map/days_sweep/pallas_call | solution.py:385
  158.4 1.9 collective-permute-start.3
  160.3 2.7 days_sweep.3
  163.0 0.1 collective-permute-done.3
  163.1 0.2 add.64
  163.3 34.7 %all_to_all.43 = f32[16,144,128]{2,1,0:T(8,128)S(1)} all-to-all(f32[16,144,128]{2,1,0:T(8,128)S(1)} %add.64), channel_id=1, replica_groups=mesh['lat'=4,'lon'=4,'zlo'=2,'y'=8,'core'=2] {'zlo','y'}, dimensions={0} | all-to-all | bytes 2359296 | tf_op jit(solution)/shard_map/all_to_all | solution.py:463
  198.0 0.1 reduce_sum.38
  198.1 1.3 collective-permute-start.4
  199.4 5.1 %collective-permute-done.4 = f32[8,128]{1,0:T(8,128)S(1)} collective-permute-done((f32[8,128]{1,0:T(8,128)S(1)}, f32[8,128]{1,0:T(8,128)S(1)}, u32[]{:S(2)}, u32[]{:S(2)}) %collective-permute-start.4) | collective-permute-done | bytes 4128 | tf_op jit(solution)/shard_map/ppermute | solution.py:467
  204.5 0.1 broadcast_in_dim.13
  204.6 31.6 %all_to_all.44.here_ref = f32[16,144,128]{2,1,0:T(8,128)S(1)} all-to-all(f32[16,144,128]{2,1,0:T(8,128)S(1)} %broadcast_in_dim.13), channel_id=1, replica_groups=mesh['lat'=4,'lon'=4,'zlo'=2,'y'=8,'core'=2] {'zlo','y'}, dimensions={0} | all-to-all | bytes 2359296 | tf_op jit(solution)/shard_map/all_to_all | solution.py:425
  236.2 2.1 collective-permute-start.5
  238.3 2.6 collective-permute-done.5.there_ref
  240.9 11.1 %modes_sweep.3 = (f32[64,64,128]{2,1,0:T(8,128)}, f32[256,128]{1,0:T(8,128)S(1)}) custom-call(s32[1,1]{1,0:T(1,128)} %bitcast.core_ref, f32[1,64]{1,0:T(1,128)S(1)} %multiply_divide_fusion.weight_ref, f32[16,144,128]{2,1,0:T(8,128)S(1)} %all_to_all.44.here_ref, f32[16,144,128]{2,1,0:T(8,128)S(1)} %collective-permute-done.5.there_ref, ...), custom_call_target="tpu_custom_call" | custom-call | flops 2000000000 | bytes 10000000 | tf_op jit(solution)/shard_map/modes_sweep/pallas_call | solution.py:374
  252.0 15.6 %all_to_all.45 = f32[16,16,128]{2,1,0:T(8,128)S(1)} all-to-all(f32[16,16,128]{2,1,0:T(8,128)S(1)} %bitcast.11), channel_id=1, replica_groups=mesh['lat'=4,'lon'=4,'zlo'=2,'y'=8,'core'=2] {'lat','lon'}, dimensions={0} | all-to-all | bytes 262144 | tf_op jit(solution)/shard_map/all_to_all | solution.py:431
  267.7 13.7 %all_to_all.46 = f32[16,16,128]{2,1,0:T(8,128)S(1)} all-to-all(f32[16,16,128]{2,1,0:T(8,128)S(1)} %broadcast_in_dim.14), channel_id=1, replica_groups=mesh['lat'=4,'lon'=4,'zlo'=2,'y'=8,'core'=2] {'lat','lon'}, dimensions={0} | all-to-all | bytes 262144 | tf_op jit(solution)/shard_map/all_to_all | solution.py:425
  281.4 5.9 %last_days.1 = f32[128,128]{1,0:T(8,128)} custom-call(f32[256,128]{1,0:T(8,128)S(1)} %bitcast.10), custom_call_target="tpu_custom_call" | custom-call | flops 10000000 | bytes 1000000 | tf_op jit(solution)/shard_map/last_days/pallas_call | solution.py:392
  (12 shorter events, 0.1 us)
Async XLA Ops:
  5.4 6.6 %collective-permute-start = (f32[16,144,128]{2,1,0:T(8,128)}, f32[16,144,128]{2,1,0:T(8,128)S(1)}, u32[]{:S(2)}, u32[]{:S(2)}) collective-permute-start(f32[16,144,128]{2,1,0:T(8,128)} %get-tuple-element.13), channel_id=1, source_target_pairs={{0,1},{1,0},{2,3},{3,2},{4,5},{5,4},{6,7},{7,6},{8,9},{9,8},{10,11... | collective-permute-start | bytes 3538952 | tf_op jit(solution)/shard_map/ppermute | solution.py:403
  14.3 9.5 %copy-start.1 = (s32[64,64]{1,0:T(8,128)S(1)}, s32[64,64]{1,0:T(8,128)}, u32[]{:S(2)}) copy-start(s32[64,64]{1,0:T(8,128)} %mask_hbm.3) | copy-start | bytes 49156
  14.3 39.1 %all-to-all-start = ((f32[16,144,128]{2,1,0:T(8,128)}), f32[16,144,128]{2,1,0:T(8,128)S(1)}, u32[]{:S(2)}, u32[]{:S(2)}) async-start(f32[16,144,128]{2,1,0:T(8,128)} %add.60), calls=%async_computation | async-start | bytes 2359296 | tf_op jit(solution)/shard_map/all_to_all | solution.py:463
  53.6 7.7 %collective-permute-start.1 = (f32[16,128]{1,0:T(8,128)S(1)}, f32[16,128]{1,0:T(8,128)S(1)}, u32[]{:S(2)}, u32[]{:S(2)}) collective-permute-start(f32[16,128]{1,0:T(8,128)S(1)} %pad_maximum_fusion.2), channel_id=1, source_target_pairs={{1,129},{3,131},{5,133},{7,135},{9,137},{11,139},{13,141},{15,143}... | collective-permute-start | bytes 24584 | tf_op jit(solution)/shard_map/ppermute | solution.py:467
  61.3 40.3 %copy-start = (f32[128,128]{1,0:T(8,128)S(1)}, f32[128,128]{1,0:T(8,128)}, u32[]{:S(2)}) copy-start(f32[128,128]{1,0:T(8,128)} %days_ref.1) | copy-start | bytes 196612
  96.7 4.8 %collective-permute-start.2 = (f32[16,152,128]{2,1,0:T(8,128)S(1)}, f32[16,152,128]{2,1,0:T(8,128)S(1)}, u32[]{:S(2)}, u32[]{:S(2)}) collective-permute-start(f32[16,152,128]{2,1,0:T(8,128)S(1)} %all_to_all.40.here_ref), channel_id=1, source_target_pairs={{0,1},{1,0},{2,3},{3,2},{4,5},{5,4},{6,7},{7,6},{8,9},{9,8},{10,11... | collective-permute-start | bytes 3735560 | tf_op jit(solution)/shard_map/ppermute | solution.py:403
  158.4 4.7 %collective-permute-start.3 = (f32[16,144,128]{2,1,0:T(8,128)S(1)}, f32[16,144,128]{2,1,0:T(8,128)S(1)}, u32[]{:S(2)}, u32[]{:S(2)}) collective-permute-start(f32[16,144,128]{2,1,0:T(8,128)S(1)} %get-tuple-element.19), channel_id=1, source_target_pairs={{0,1},{1,0},{2,3},{3,2},{4,5},{5,4},{6,7},{7,6},{8,9},{9,8},{10,11... | collective-permute-start | bytes 3538952 | tf_op jit(solution)/shard_map/ppermute | solution.py:403
  198.1 6.4 %collective-permute-start.4 = (f32[8,128]{1,0:T(8,128)S(1)}, f32[8,128]{1,0:T(8,128)S(1)}, u32[]{:S(2)}, u32[]{:S(2)}) collective-permute-start(f32[8,128]{1,0:T(8,128)S(1)} %get-tuple-element.26), channel_id=1, source_target_pairs={{1,129},{3,131},{5,133},{7,135},{9,137},{11,139},{13,141},{15,143}... | collective-permute-start | bytes 12296 | tf_op jit(solution)/shard_map/ppermute | solution.py:467
  236.2 4.7 %collective-permute-start.5 = (f32[16,144,128]{2,1,0:T(8,128)S(1)}, f32[16,144,128]{2,1,0:T(8,128)S(1)}, u32[]{:S(2)}, u32[]{:S(2)}) collective-permute-start(f32[16,144,128]{2,1,0:T(8,128)S(1)} %all_to_all.44.here_ref), channel_id=1, source_target_pairs={{0,1},{1,0},{2,3},{3,2},{4,5},{5,4},{6,7},{7,6},{8,9},{9,8},{10,11... | collective-permute-start | bytes 3538952 | tf_op jit(solution)/shard_map/ppermute | solution.py:403

commit v4 on v3

--- a/solution.py
+++ b/solution.py
@@ -186,7 +186,7 @@
         copy.wait()
 
 
-def modes_kernel(first, core_ref, weight_ref, here_ref, there_ref, days_ref, *refs):
+def modes_kernel(first, core_ref, weight_ref, here_ref, there_ref, here_late_ref, there_late_ref, inverse_ref, days_ref, *refs):
     shelves, refs = refs[0 : (2 if first else 3)], refs[(2 if first else 3) :]
     out_hbm, sums_ref, pad_ref, rim_ref, wide_ref, spatial_ref = refs[0:6]
     coded_refs, field_refs, refs = refs[6:8], refs[8:10], refs[10:]
@@ -196,33 +196,29 @@
     lats, lons, modes = spatial_ref.shape
     deep = lats // 2
     spokes = here_ref.shape[0]
-    per = deep // spokes
-    cells = per * lons
     tiles = 2 if first else 1
-    gram_at = cells + 8 * tiles
     halves = (core, 1 - core)
     fields = [(shelves[n], deep) if first else (shelves[2], n * deep) for n in range(2)]
     pairs = [(shelf.at[pl.ds(at, deep)], field_refs[n]) for n, (shelf, at) in enumerate(fields)]
     pairs += [(shelves[n].at[pl.ds(0, deep)], coded_refs[n]) for n in range(2)]
     loads = fetch(pairs, in_sems)
-    gram = jnp.concatenate([here_ref[q, gram_at : gram_at + 8, :] for q in range(spokes)], axis=0)
-    inverse_side = right_side(inverse_spd(add_ridge(gram)))
+    inverse_side = right_side(inverse_ref[...])
     days_side = right_side(days_ref[...].T)
-    for copy in loads:
-        copy.wait()
     stores = []
-
-    for half, ref in zip(halves, (here_ref, there_ref)):
+    for half, early, late in ((core, here_ref, here_late_ref), (1 - core, there_ref, there_late_ref)):
         for q in range(spokes):
-            for p in range(per):
-                pad_ref[half * deep + q * per + p + 1] = ref[q, p * lons : (p + 1) * lons, :]
+            at = half * deep + q * 2 + 1
+            pad_ref[at] = early[q, 0:lons, :]
+            pad_ref[at + 1] = late[q, 0:lons, :]
             if q < lons // 8:
                 at = half * lons + 8 * q
             else:
                 side, along = divmod(8 * q - lons, deep)
                 at = 2 * lons + side * lats + half * deep + along
             for t in range(tiles):
-                rim_ref[pl.ds(pl.multiple_of(t * 4 * lons + at, 8), 8), :] = ref[q, cells + 8 * t : cells + 8 * t + 8, :]
+                rim_ref[pl.ds(pl.multiple_of(t * 4 * lons + at, 8), 8), :] = late[q, lons + 8 * t : lons + 8 * t + 8, :]
+    for copy in loads:
+        copy.wait()
     pad_ref[0] = rim_ref[lons : 2 * lons, :]
     pad_ref[lats + 1] = rim_ref[0:lons, :]
     row = lax.broadcasted_iota(jnp.int32, (lons, modes), 0)
@@ -323,6 +319,12 @@
     put_block(half, grid_ref, gram_ref, ref)
 
 
+def inverse_kernel(early_ref, inverse_ref):
+    spokes, rows, _ = early_ref.shape
+    gram = jnp.concatenate([early_ref[q, rows - 8 : rows, :] for q in range(spokes)], axis=0)
+    inverse_ref[...] = inverse_spd(add_ridge(gram))
+
+
 def last_kernel(sums_ref, days_ref):
     days = days_ref.shape[0]
     days_ref[...] = full(sums_ref[0:days, :], inverse_spd(add_ridge(sums_ref[days:, :])))
@@ -363,16 +365,16 @@
     )
 
 
-def modes_call(first, core, weight, here, there, days, shelves, lats):
+def modes_call(first, core, weight, pieces, days, shelves, lats):
     _, lons, n = shelves[0].shape
     half = (lats // 2, lons, n)
     grid = (lats, lons, n)
     outs = [((SHELF, lons, n) if first else grid, HBM), ((2 * n, n), VMEM)]
     scratch = [(lats + 2, lons, n), ((8 if first else 4) * lons, n), (4 * n, 2 * n), grid] + [half] * (6 if first else 4)
     scratch += [copy_sems(4), copy_sems(4)]
-    specs = [SMEM, SMEM] + [VMEM] * 3 + [HBM] * len(shelves)
+    specs = [SMEM, SMEM] + [VMEM] * 6 + [HBM] * len(shelves)
     return call(functools.partial(modes_kernel, first), outs, specs, scratch, "modes_sweep", 2 * 10**9, 10**7, ROOM)(
-        core, weight, here, there, days, *shelves
+        core, weight, *pieces, days, *shelves
     )
 
 
@@ -385,6 +387,11 @@
     return call(functools.partial(days_kernel, mine), outs, [SMEM, VMEM, HBM, HBM], scratch, "days_sweep", 2 * 10**9, 10**7, ROOM)(
         core, sums, shelf, modes
     )
+
+
+def inverse_call(early):
+    n = early.shape[2]
+    return call(inverse_kernel, [((n, n), VMEM)], [VMEM], [], "days_inverse", 10**9, 2 * 10**7, 16)(early)[0]
 
 
 def last_call(sums):
@@ -465,10 +472,14 @@
         if sweep == 0:
             send = jnp.concatenate([send, edge_sea], axis=0)
         halo = lax.ppermute(send, ALL, pairs)
-        shard = jnp.concatenate([shard[:cells], halo, shard[cells + 8 :]], axis=0)
-        here = gather_all(shard, YZ, spokes)
-        there = swap_core(here)
-        spatial, sums = modes_call(sweep == 0, core_word, weight, here, there, temporal, shelves, rows_lat)
+        early = gather_all(jnp.concatenate([shard[:cols_lon], shard[cells + 8 :]], axis=0), YZ, spokes)
+        after = jnp.concatenate([shard[cols_lon:cells], halo], axis=0)
+        early, after = lax.optimization_barrier((early, after))
+        late = gather_all(after, YZ, spokes)
+        there, inverse = swap_core(early), inverse_call(early)
+        late, there, inverse = lax.optimization_barrier((late, there, inverse))
+        pieces = (early, there, late, swap_core(late), inverse)
+        spatial, sums = modes_call(sweep == 0, core_word, weight, pieces, temporal, shelves, rows_lat)
         sums = sum_cells(sums)
         if sweep == 0:
             shelves.append(spatial)

time: 288 us -> 288 us (level)
  blocking collectives: 167 us -> 141 us
  starting transfers between devices: 20 us -> 32.4 us
  waiting for transfers between devices: 46.1 us -> 53.6 us
  Pallas kernels: 49.7 us -> 53.5 us
  local copies, waits for them, and re-layouts: 0.67 us -> 3.95 us
    all_to_all x4 -> x2, blocking collectives: 94.5 us -> 27.7 us  [gather_all(): return lax.all_to_all(spread, axes, 0, 0, tiled=True)]
    all_to_all x1 -> x2, blocking collectives: 34.7 us -> 76.1 us  [on_device(): shard = jnp.sum(lax.all_to_all(half, YZ, 0, 0, tiled=True), axis=0)]
    pallas_call x0 -> x2, Pallas kernels: none -> 10.2 us  [inverse_call(): call(inverse_kernel, [((n, n), VMEM)], [VMEM], [], 'days_inverse', 10 **...]
    all_to_all x1 -> x4, waiting for transfers between devices: 29.1 us -> 38.1 us  [gather_all(): return lax.all_to_all(spread, axes, 0, 0, tiled=True)]
    all_to_all x1 -> x4, starting transfers between devices: 9.5 us -> 18 us  [gather_all(): return lax.all_to_all(spread, axes, 0, 0, tiled=True)]
    pallas_call x2, Pallas kernels: 23.5 us -> 17.2 us  [modes_call(): call(functools.partial(modes_kernel, first), outs, specs, scratch, 'modes...]
    ppermute x4 -> x6, starting transfers between devices: 7.88 us -> 11.8 us  [swap_core(): return lax.ppermute(value, 'core', [(0, 1), (1, 0)])]
    broadcast_in_dim x4 -> x6, local copies, waits for them, and re-layouts: 0.18 us -> 3.46 us  [gather_all(): spread = jnp.broadcast_to(value[None], (size,) + value.shape)]
  transfers between devices with their start and end apart: 7 -> 12, of which waited for: 6 -> 9; matrix products, arithmetic and copies ran while one was open for 0% -> 0% of each run, Pallas kernels for 3% -> 6%
where the time goes in v4:
time: 288 us; the launch traced here: 287 us
  blocking collectives  141 us (49%)
  waiting for transfers between devices  53.6 us (19%)
  Pallas kernels  53.5 us (19%)
  starting transfers between devices  32.4 us (11%)
  local copies, waits for them, and re-layouts  3.95 us (1%)
    all_to_all x2, blocking collectives, on_device(): shard = jnp.sum(lax.all_to_all(half, YZ, 0, 0, tiled=True), axis=0)  76.1 us
    all_to_all x4, waiting for transfers between devices, gather_all(): return lax.all_to_all(spread, axes, 0, 0, tiled=True)  38.1 us
    all_to_all x2, blocking collectives, sum_cells(): lax.all_to_all(value.reshape(size, rows // size, -1), LL, 0, 0, tiled=True)  36.7 us
    all_to_all x2, blocking collectives, gather_all(): return lax.all_to_all(spread, axes, 0, 0, tiled=True)  27.7 us
    all_to_all x4, starting transfers between devices, gather_all(): return lax.all_to_all(spread, axes, 0, 0, tiled=True)  18 us
    pallas_call x2, Pallas kernels, modes_call(): call(functools.partial(modes_kernel, first), outs, specs, scratch, 'modes...  17.2 us
    ppermute x6, starting transfers between devices, swap_core(): return lax.ppermute(value, 'core', [(0, 1), (1, 0)])  11.8 us
    ppermute x2, waiting for transfers between devices, on_device(): halo = lax.ppermute(send, ALL, pairs)  11.6 us
  transfers between devices with their start and end apart: 12, of which 9 were waited for; matrix products, arithmetic and copies ran while one was open for 0% of the time, Pallas kernels for 6%

profile of v4, /device:TPU:8, one launch (start us, length us, event | category | flops | bytes accessed | tf_op | source)
XLA Modules:
  0.0 286.9 jit_solution(4008845402342161456)
XLA Ops:
  0.6 4.7 %first_projection.3 = (f32[16,144,128]{2,1,0:T(8,128)}, f32[384,64,128]{2,1,0:T(8,128)}) custom-call(s32[1,1]{1,0:T(1,128)} %bitcast.core_ref, f32[64,64,128]{2,1,0:T(8,128)} %anomaly_hbm.3, s32[64,64,128]{2,1,0:T(8,128)} %observed_hbm.3, s32[64,64]{1,0:T(8,128)} %mask_hbm.3, f32[128,128]{1,0:T(8,128)} %days_ref.1), custom_call_target="tpu_custom_call" | custom-call | flops 1000000000 | bytes 10000000 | tf_op jit(solution)/shard_map/first_projection/pallas_call | solution.py:363
  5.3 1.9 collective-permute-start
  7.3 4.6 %first_projection.2 = (f32[16,144,128]{2,1,0:T(8,128)}, f32[384,64,128]{2,1,0:T(8,128)}) custom-call(s32[1,1]{1,0:T(1,128)} %bitcast.core_ref, f32[64,64,128]{2,1,0:T(8,128)} %anomaly_hbm.3, s32[64,64,128]{2,1,0:T(8,128)} %observed_hbm.3, s32[64,64]{1,0:T(8,128)} %mask_hbm.3, f32[128,128]{1,0:T(8,128)} %days_ref.1), custom_call_target="tpu_custom_call" | custom-call | flops 1000000000 | bytes 10000000 | tf_op jit(solution)/shard_map/first_projection/pallas_call | solution.py:363
  11.8 1.4 add.60
  13.2 40.3 %all_to_all.50 = f32[16,144,128]{2,1,0:T(8,128)S(1)} all-to-all(f32[16,144,128]{2,1,0:T(8,128)S(1)} %add.60), channel_id=1, replica_groups=mesh['lat'=4,'lon'=4,'zlo'=2,'y'=8,'core'=2] {'zlo','y'}, dimensions={0} | all-to-all | bytes 2359296 | tf_op jit(solution)/shard_map/all_to_all | solution.py:470
  53.6 0.9 broadcast_in_dim.14
  54.5 3.8 %all-to-all-start.1 = ((f32[16,72,128]{2,1,0:T(8,128)}), f32[16,72,128]{2,1,0:T(8,128)S(1)}, u32[]{:S(2)}, u32[]{:S(2)}) async-start(f32[16,72,128]{2,1,0:T(8,128)} %broadcast_in_dim.14), calls=%async_computation.1 | async-start | bytes 1179648 | tf_op jit(solution)/shard_map/all_to_all | solution.py:432
  58.4 0.2 slice_reduce_fusion
  58.6 0.1 concatenate.19
  58.7 0.1 dynamic_slice.3
  58.8 0.1 pad.7.clone
  58.8 0.1 pad_maximum_fusion.4
  58.9 1.3 collective-permute-start.1
  60.2 6.5 %collective-permute-done.1 = f32[16,128]{1,0:T(8,128)S(1)} collective-permute-done((f32[16,128]{1,0:T(8,128)S(1)}, f32[16,128]{1,0:T(8,128)S(1)}, u32[]{:S(2)}, u32[]{:S(2)}) %collective-permute-start.1) | collective-permute-done | bytes 8224 | tf_op jit(solution)/shard_map/ppermute | solution.py:474
  66.7 8.3 %all-to-all-done.1.early_ref.here_ref = f32[16,72,128]{2,1,0:T(8,128)S(1)} async-done(((f32[16,72,128]{2,1,0:T(8,128)}), f32[16,72,128]{2,1,0:T(8,128)S(1)}, u32[]{:S(2)}, u32[]{:S(2)}) %all-to-all-start.1) | async-done | bytes 589856 | tf_op jit(solution)/shard_map/all_to_all | solution.py:432
  75.1 0.9 broadcast_in_dim.16
  75.9 5.1 %all-to-all-start.2 = ((f32[16,80,128]{2,1,0:T(8,128)}), f32[16,80,128]{2,1,0:T(8,128)S(1)}, u32[]{:S(2)}, u32[]{:S(2)}) async-start(f32[16,80,128]{2,1,0:T(8,128)} %broadcast_in_dim.16), calls=%async_computation.2 | async-start | bytes 1310720 | tf_op jit(solution)/shard_map/all_to_all | solution.py:432
  81.1 2.1 collective-permute-start.2
  83.1 5.1 %days_inverse.2.inverse_ref = f32[128,128]{1,0:T(8,128)S(1)} custom-call(f32[16,72,128]{2,1,0:T(8,128)S(1)} %all-to-all-done.1.early_ref.here_ref), custom_call_target="tpu_custom_call" | custom-call | flops 1000000000 | bytes 20000000 | tf_op jit(solution)/shard_map/days_inverse/pallas_call | solution.py:394
  88.2 10.6 %all-to-all-done.2.here_late_ref = f32[16,80,128]{2,1,0:T(8,128)S(1)} async-done(((f32[16,80,128]{2,1,0:T(8,128)}), f32[16,80,128]{2,1,0:T(8,128)S(1)}, u32[]{:S(2)}, u32[]{:S(2)}) %all-to-all-start.2) | async-done | bytes 655392 | tf_op jit(solution)/shard_map/all_to_all | solution.py:432
  98.8 1.9 collective-permute-start.3
  100.8 2.0 collective-permute-done.3.there_late_ref
  102.8 9.3 %modes_sweep.2 = (f32[384,64,128]{2,1,0:T(8,128)}, f32[256,128]{1,0:T(8,128)S(1)}) custom-call(s32[1,1]{1,0:T(1,128)} %bitcast.core_ref, f32[1,64]{1,0:T(1,128)S(1)} %multiply_divide_fusion.weight_ref, f32[16,72,128]{2,1,0:T(8,128)S(1)} %all-to-all-done.1.early_ref.here_ref, f32[16,72,128]{2,1,0:T(8,128)S(1)} %collective-permute-done.2.there_ref, ...), custom_call_target="tpu_custom_call" | custom-call | flops 2000000000 | bytes 10000000 | tf_op jit(solution)/shard_map/modes_sweep/pallas_call | solution.py:376
  112.1 22.8 %all_to_all.51 = f32[16,16,128]{2,1,0:T(8,128)S(1)} all-to-all(f32[16,16,128]{2,1,0:T(8,128)S(1)} %bitcast.12), channel_id=1, replica_groups=mesh['lat'=4,'lon'=4,'zlo'=2,'y'=8,'core'=2] {'lat','lon'}, dimensions={0} | all-to-all | bytes 262144 | tf_op jit(solution)/shard_map/all_to_all | solution.py:438
  134.9 13.4 %all_to_all.52 = f32[16,16,128]{2,1,0:T(8,128)S(1)} all-to-all(f32[16,16,128]{2,1,0:T(8,128)S(1)} %broadcast_in_dim.17), channel_id=1, replica_groups=mesh['lat'=4,'lon'=4,'zlo'=2,'y'=8,'core'=2] {'lat','lon'}, dimensions={0} | all-to-all | bytes 262144 | tf_op jit(solution)/shard_map/all_to_all | solution.py:432
  148.3 8.2 %days_sweep.2 = (f32[16,144,128]{2,1,0:T(8,128)S(1)}, f32[128,128]{1,0:T(8,128)S(1)}) custom-call(s32[1,1]{1,0:T(1,128)} %bitcast.core_ref, f32[256,128]{1,0:T(8,128)S(1)} %bitcast.9, f32[384,64,128]{2,1,0:T(8,128)} %get-tuple-element.30.refs_1_.shelf_hbm, f32[384,64,128]{2,1,0:T(8,128)} %get-tuple-element.32.modes_hbm.refs_2_), custom_call_target="tpu_custom_call" | custom-call | flops 2000000000 | bytes 10000000 | tf_op jit(solution)/shard_map/days_sweep/pallas_call | solution.py:387
  156.6 1.9 collective-permute-start.4
  158.5 2.7 days_sweep.3
  161.2 0.1 collective-permute-done.4
  161.3 0.1 add.64
  161.4 35.8 %all_to_all.53 = f32[16,144,128]{2,1,0:T(8,128)S(1)} all-to-all(f32[16,144,128]{2,1,0:T(8,128)S(1)} %add.64), channel_id=1, replica_groups=mesh['lat'=4,'lon'=4,'zlo'=2,'y'=8,'core'=2] {'zlo','y'}, dimensions={0} | all-to-all | bytes 2359296 | tf_op jit(solution)/shard_map/all_to_all | solution.py:470
  197.3 0.1 reduce_sum.38
  197.4 0.9 broadcast_in_dim.18
  198.2 3.8 %all-to-all-start.6 = ((f32[16,72,128]{2,1,0:T(8,128)}), f32[16,72,128]{2,1,0:T(8,128)S(1)}, u32[]{:S(2)}, u32[]{:S(2)}) async-start(f32[16,72,128]{2,1,0:T(8,128)} %broadcast_in_dim.18), calls=%async_computation.6 | async-start | bytes 1179648 | tf_op jit(solution)/shard_map/all_to_all | solution.py:432
  202.1 1.3 collective-permute-start.5
  203.4 5.1 %collective-permute-done.5 = f32[8,128]{1,0:T(8,128)S(1)} collective-permute-done((f32[8,128]{1,0:T(8,128)S(1)}, f32[8,128]{1,0:T(8,128)S(1)}, u32[]{:S(2)}, u32[]{:S(2)}) %collective-permute-start.5) | collective-permute-done | bytes 4128 | tf_op jit(solution)/shard_map/ppermute | solution.py:474
  208.5 10.1 %all-to-all-done.6.early_ref.here_ref = f32[16,72,128]{2,1,0:T(8,128)S(1)} async-done(((f32[16,72,128]{2,1,0:T(8,128)}), f32[16,72,128]{2,1,0:T(8,128)S(1)}, u32[]{:S(2)}, u32[]{:S(2)}) %all-to-all-start.6) | async-done | bytes 589856 | tf_op jit(solution)/shard_map/all_to_all | solution.py:432
  218.6 0.9 broadcast_in_dim.19
  219.4 5.3 %all-to-all-start.7 = ((f32[16,72,128]{2,1,0:T(8,128)}), f32[16,72,128]{2,1,0:T(8,128)S(1)}, u32[]{:S(2)}, u32[]{:S(2)}) async-start(f32[16,72,128]{2,1,0:T(8,128)} %broadcast_in_dim.19), calls=%async_computation.7 | async-start | bytes 1179648 | tf_op jit(solution)/shard_map/all_to_all | solution.py:432
  224.7 1.9 collective-permute-start.6
  226.6 5.1 %days_inverse.3.inverse_ref = f32[128,128]{1,0:T(8,128)S(1)} custom-call(f32[16,72,128]{2,1,0:T(8,128)S(1)} %all-to-all-done.6.early_ref.here_ref), custom_call_target="tpu_custom_call" | custom-call | flops 1000000000 | bytes 20000000 | tf_op jit(solution)/shard_map/days_inverse/pallas_call | solution.py:394
  231.7 9.1 %all-to-all-done.7.here_late_ref = f32[16,72,128]{2,1,0:T(8,128)S(1)} async-done(((f32[16,72,128]{2,1,0:T(8,128)}), f32[16,72,128]{2,1,0:T(8,128)S(1)}, u32[]{:S(2)}, u32[]{:S(2)}) %all-to-all-start.7) | async-done | bytes 589856 | tf_op jit(solution)/shard_map/all_to_all | solution.py:432
  240.8 2.1 collective-permute-start.7
  242.9 1.7 collective-permute-done.7.there_late_ref
  244.6 8.0 %modes_sweep.3 = (f32[64,64,128]{2,1,0:T(8,128)}, f32[256,128]{1,0:T(8,128)S(1)}) custom-call(s32[1,1]{1,0:T(1,128)} %bitcast.core_ref, f32[1,64]{1,0:T(1,128)S(1)} %multiply_divide_fusion.weight_ref, f32[16,72,128]{2,1,0:T(8,128)S(1)} %all-to-all-done.6.early_ref.here_ref, f32[16,72,128]{2,1,0:T(8,128)S(1)} %collective-permute-done.6.there_ref, ...), custom_call_target="tpu_custom_call" | custom-call | flops 2000000000 | bytes 10000000 | tf_op jit(solution)/shard_map/modes_sweep/pallas_call | solution.py:376
  252.6 13.9 %all_to_all.54 = f32[16,16,128]{2,1,0:T(8,128)S(1)} all-to-all(f32[16,16,128]{2,1,0:T(8,128)S(1)} %bitcast.11), channel_id=1, replica_groups=mesh['lat'=4,'lon'=4,'zlo'=2,'y'=8,'core'=2] {'lat','lon'}, dimensions={0} | all-to-all | bytes 262144 | tf_op jit(solution)/shard_map/all_to_all | solution.py:438
  266.6 14.3 %all_to_all.55 = f32[16,16,128]{2,1,0:T(8,128)S(1)} all-to-all(f32[16,16,128]{2,1,0:T(8,128)S(1)} %broadcast_in_dim.20), channel_id=1, replica_groups=mesh['lat'=4,'lon'=4,'zlo'=2,'y'=8,'core'=2] {'lat','lon'}, dimensions={0} | all-to-all | bytes 262144 | tf_op jit(solution)/shard_map/all_to_all | solution.py:432
  280.9 5.9 %last_days.1 = f32[128,128]{1,0:T(8,128)} custom-call(f32[256,128]{1,0:T(8,128)S(1)} %bitcast.10), custom_call_target="tpu_custom_call" | custom-call | flops 10000000 | bytes 1000000 | tf_op jit(solution)/shard_map/last_days/pallas_call | solution.py:399
  (23 shorter events, 0.2 us)
Async XLA Ops:
  5.3 6.5 %collective-permute-start = (f32[16,144,128]{2,1,0:T(8,128)}, f32[16,144,128]{2,1,0:T(8,128)S(1)}, u32[]{:S(2)}, u32[]{:S(2)}) collective-permute-start(f32[16,144,128]{2,1,0:T(8,128)} %get-tuple-element.23), channel_id=1, source_target_pairs={{0,1},{1,0},{2,3},{3,2},{4,5},{5,4},{6,7},{7,6},{8,9},{9,8},{10,11... | collective-permute-start | bytes 3538952 | tf_op jit(solution)/shard_map/ppermute | solution.py:410
  53.6 4.8 %copy-start.1 = (s32[64,64]{1,0:T(8,128)S(1)}, s32[64,64]{1,0:T(8,128)}, u32[]{:S(2)}) copy-start(s32[64,64]{1,0:T(8,128)} %mask_hbm.3) | copy-start | bytes 49156
  54.5 20.6 %all-to-all-start.1 = ((f32[16,72,128]{2,1,0:T(8,128)}), f32[16,72,128]{2,1,0:T(8,128)S(1)}, u32[]{:S(2)}, u32[]{:S(2)}) async-start(f32[16,72,128]{2,1,0:T(8,128)} %broadcast_in_dim.14), calls=%async_computation.1 | async-start | bytes 1179648 | tf_op jit(solution)/shard_map/all_to_all | solution.py:432
  58.9 7.8 %collective-permute-start.1 = (f32[16,128]{1,0:T(8,128)S(1)}, f32[16,128]{1,0:T(8,128)S(1)}, u32[]{:S(2)}, u32[]{:S(2)}) collective-permute-start(f32[16,128]{1,0:T(8,128)S(1)} %pad_maximum_fusion.4), channel_id=1, source_target_pairs={{1,129},{3,131},{5,133},{7,135},{9,137},{11,139},{13,141},{15,143}... | collective-permute-start | bytes 24584 | tf_op jit(solution)/shard_map/ppermute | solution.py:474
  75.9 22.9 %all-to-all-start.2 = ((f32[16,80,128]{2,1,0:T(8,128)}), f32[16,80,128]{2,1,0:T(8,128)S(1)}, u32[]{:S(2)}, u32[]{:S(2)}) async-start(f32[16,80,128]{2,1,0:T(8,128)} %broadcast_in_dim.16), calls=%async_computation.2 | async-start | bytes 1310720 | tf_op jit(solution)/shard_map/all_to_all | solution.py:432
  81.0 21.8 %copy-start = (f32[128,128]{1,0:T(8,128)S(1)}, f32[128,128]{1,0:T(8,128)}, u32[]{:S(2)}) copy-start(f32[128,128]{1,0:T(8,128)} %days_ref.1) | copy-start | bytes 196612
  81.1 7.2 %collective-permute-start.2 = (f32[16,72,128]{2,1,0:T(8,128)S(1)}, f32[16,72,128]{2,1,0:T(8,128)S(1)}, u32[]{:S(2)}, u32[]{:S(2)}) collective-permute-start(f32[16,72,128]{2,1,0:T(8,128)S(1)} %all-to-all-done.1.early_ref.here_ref), channel_id=1, source_target_pairs={{0,1},{1,0},{2,3},{3,2},{4,5},{5,4},{6,7},{7,6},{8,9},{9,8},{10,11... | collective-permute-start | bytes 1769480 | tf_op jit(solution)/shard_map/ppermute | solution.py:410
  98.8 4.0 %collective-permute-start.3 = (f32[16,80,128]{2,1,0:T(8,128)S(1)}, f32[16,80,128]{2,1,0:T(8,128)S(1)}, u32[]{:S(2)}, u32[]{:S(2)}) collective-permute-start(f32[16,80,128]{2,1,0:T(8,128)S(1)} %all-to-all-done.2.here_late_ref), channel_id=1, source_target_pairs={{0,1},{1,0},{2,3},{3,2},{4,5},{5,4},{6,7},{7,6},{8,9},{9,8},{10,11... | collective-permute-start | bytes 1966088 | tf_op jit(solution)/shard_map/ppermute | solution.py:410
  156.6 4.7 %collective-permute-start.4 = (f32[16,144,128]{2,1,0:T(8,128)S(1)}, f32[16,144,128]{2,1,0:T(8,128)S(1)}, u32[]{:S(2)}, u32[]{:S(2)}) collective-permute-start(f32[16,144,128]{2,1,0:T(8,128)S(1)} %get-tuple-element.34), channel_id=1, source_target_pairs={{0,1},{1,0},{2,3},{3,2},{4,5},{5,4},{6,7},{7,6},{8,9},{9,8},{10,11... | collective-permute-start | bytes 3538952 | tf_op jit(solution)/shard_map/ppermute | solution.py:410
  198.2 20.3 %all-to-all-start.6 = ((f32[16,72,128]{2,1,0:T(8,128)}), f32[16,72,128]{2,1,0:T(8,128)S(1)}, u32[]{:S(2)}, u32[]{:S(2)}) async-start(f32[16,72,128]{2,1,0:T(8,128)} %broadcast_in_dim.18), calls=%async_computation.6 | async-start | bytes 1179648 | tf_op jit(solution)/shard_map/all_to_all | solution.py:432
  202.1 6.4 %collective-permute-start.5 = (f32[8,128]{1,0:T(8,128)S(1)}, f32[8,128]{1,0:T(8,128)S(1)}, u32[]{:S(2)}, u32[]{:S(2)}) collective-permute-start(f32[8,128]{1,0:T(8,128)S(1)} %get-tuple-element.48), channel_id=1, source_target_pairs={{1,129},{3,131},{5,133},{7,135},{9,137},{11,139},{13,141},{15,143}... | collective-permute-start | bytes 12296 | tf_op jit(solution)/shard_map/ppermute | solution.py:474
  219.4 21.4 %all-to-all-start.7 = ((f32[16,72,128]{2,1,0:T(8,128)}), f32[16,72,128]{2,1,0:T(8,128)S(1)}, u32[]{:S(2)}, u32[]{:S(2)}) async-start(f32[16,72,128]{2,1,0:T(8,128)} %broadcast_in_dim.19), calls=%async_computation.7 | async-start | bytes 1179648 | tf_op jit(solution)/shard_map/all_to_all | solution.py:432
  224.7 7.0 %collective-permute-start.6 = (f32[16,72,128]{2,1,0:T(8,128)S(1)}, f32[16,72,128]{2,1,0:T(8,128)S(1)}, u32[]{:S(2)}, u32[]{:S(2)}) collective-permute-start(f32[16,72,128]{2,1,0:T(8,128)S(1)} %all-to-all-done.6.early_ref.here_ref), channel_id=1, source_target_pairs={{0,1},{1,0},{2,3},{3,2},{4,5},{5,4},{6,7},{7,6},{8,9},{9,8},{10,11... | collective-permute-start | bytes 1769480 | tf_op jit(solution)/shard_map/ppermute | solution.py:410
  240.8 3.9 %collective-permute-start.7 = (f32[16,72,128]{2,1,0:T(8,128)S(1)}, f32[16,72,128]{2,1,0:T(8,128)S(1)}, u32[]{:S(2)}, u32[]{:S(2)}) collective-permute-start(f32[16,72,128]{2,1,0:T(8,128)S(1)} %all-to-all-done.7.here_late_ref), channel_id=1, source_target_pairs={{0,1},{1,0},{2,3},{3,2},{4,5},{5,4},{6,7},{7,6},{8,9},{9,8},{10,11... | collective-permute-start | bytes 1769480 | tf_op jit(solution)/shard_map/ppermute | solution.py:410

commit v5 on v3

--- a/solution.py
+++ b/solution.py
@@ -18,6 +18,7 @@
 
 GAP = 1e30
 PIECES = 8
+DAYS_PIECES = 16
 GROUP = 16
 FIRST_ROOM = 57
 ROOM = 50
@@ -29,48 +30,65 @@
 f32, bf16 = jnp.float32, jnp.bfloat16
 
 
+def inverse_four(d):
+    a, b, c = d[0][0], d[0][1], d[1][1]
+    r = 1.0 / (a * c - b * b)
+    a00, a01, a11 = c * r, -b * r, a * r
+    b02, b03, b12, b13 = d[0][2], d[0][3], d[1][2], d[1][3]
+    g02, g03 = a00 * b02 + a01 * b12, a00 * b03 + a01 * b13
+    g12, g13 = a01 * b02 + a11 * b12, a01 * b03 + a11 * b13
+    s22 = d[2][2] - (b02 * g02 + b12 * g12)
+    s23 = d[2][3] - (b02 * g03 + b12 * g13)
+    s33 = d[3][3] - (b03 * g03 + b13 * g13)
+    r = 1.0 / (s22 * s33 - s23 * s23)
+    i22, i23, i33 = s33 * r, -s23 * r, s22 * r
+    h02, h03 = g02 * i22 + g03 * i23, g02 * i23 + g03 * i33
+    h12, h13 = g12 * i22 + g13 * i23, g12 * i23 + g13 * i33
+    q00 = a00 + (h02 * g02 + h03 * g03)
+    q01 = a01 + (h02 * g12 + h03 * g13)
+    q11 = a11 + (h12 * g12 + h13 * g13)
+    return [[q00, q01, -h02, -h03], [q01, q11, -h12, -h13], [-h02, -h12, i22, i23], [-h03, -h13, i23, i33]]
+
+
+def tree(terms):
+    while len(terms) > 1:
+        terms = [terms[i] + terms[i + 1] if i + 1 < len(terms) else terms[i] for i in range(0, len(terms), 2)]
+    return terms[0]
+
+
 def inverse_spd(matrix):
     size = matrix.shape[0]
+    four = range(4)
     blocks = [matrix[8 * r : 8 * r + 8] for r in range(size // 8)]
-    lane = lax.broadcasted_iota(jnp.int32, (1, size), 1)
+    lane = lax.broadcasted_iota(jnp.int32, (8, size), 1)
     row = lax.broadcasted_iota(jnp.int32, (8, size), 0)
-    for k in range(0, size, 4):
-        home, off = k // 8, k % 8
-        rows = [blocks[home][off + i : off + i + 1] for i in range(4)]
-        d = [[jnp.broadcast_to(rows[i][:, k + j : k + j + 1], (1, size)) for j in range(4)] for i in range(4)]
-        in_panel = (lane >= k) & (lane < k + 4)
-        a, b, c = d[0][0], d[0][1], d[1][1]
-        r = 1.0 / (a * c - b * b)
-        a00, a01, a11 = c * r, -b * r, a * r
-        b02, b03, b12, b13 = d[0][2], d[0][3], d[1][2], d[1][3]
-        g02, g03 = a00 * b02 + a01 * b12, a00 * b03 + a01 * b13
-        g12, g13 = a01 * b02 + a11 * b12, a01 * b03 + a11 * b13
-        s22 = d[2][2] - (b02 * g02 + b12 * g12)
-        s23 = d[2][3] - (b02 * g03 + b12 * g13)
-        s33 = d[3][3] - (b03 * g03 + b13 * g13)
-        r = 1.0 / (s22 * s33 - s23 * s23)
-        i22, i23, i33 = s33 * r, -s23 * r, s22 * r
-        h02, h03 = g02 * i22 + g03 * i23, g02 * i23 + g03 * i33
-        h12, h13 = g12 * i22 + g13 * i23, g12 * i23 + g13 * i33
-        q00 = a00 + (h02 * g02 + h03 * g03)
-        q01 = a01 + (h02 * g12 + h03 * g13)
-        q11 = a11 + (h12 * g12 + h13 * g13)
-        inv = [[q00, q01, -h02, -h03], [q01, q11, -h12, -h13], [-h02, -h12, i22, i23], [-h03, -h13, i23, i33]]
-        unit = [jnp.where(lane == k + j, 1.0, jnp.where(in_panel, 0.0, rows[j])) for j in range(4)]
-        new = [
-            (inv[i][0] * unit[0] + inv[i][1] * unit[1]) + (inv[i][2] * unit[2] + inv[i][3] * unit[3])
-            for i in range(4)
-        ]
-        out = []
+    for home in range(size // 8):
+        k = 8 * home
+        rows = [blocks[home][i : i + 1] for i in range(8)]
+        d = [[jnp.broadcast_to(rows[min(i, j)][:, k + max(i, j) : k + max(i, j) + 1], (1, size)) for j in range(8)] for i in range(8)]
+        top = inverse_four([[d[i][j] for j in four] for i in four])
+        side = [[d[i][4 + j] for j in four] for i in four]
+        g = [[tree([top[i][m] * side[m][j] for m in four]) for j in four] for i in four]
+        s = [[None] * 4 for _ in four]
+        for i in four:
+            for j in range(i, 4):
+                s[i][j] = s[j][i] = d[4 + i][4 + j] - tree([side[m][i] * g[m][j] for m in four])
+        low = inverse_four(s)
+        h = [[tree([g[i][m] * low[m][j] for m in four]) for j in four] for i in four]
+        q = [[None] * 4 for _ in four]
+        for i in four:
+            for j in range(i, 4):
+                q[i][j] = q[j][i] = top[i][j] + tree([h[i][m] * g[j][m] for m in four])
+        inv = [q[i] + [-h[i][j] for j in four] for i in four] + [[-h[j][i] for j in four] + low[i] for i in four]
+        in_panel = (lane >= k) & (lane < k + 8)
+        unit = jnp.where(in_panel, jnp.where(lane == row + k, 1.0, 0.0), blocks[home])
+        unit = [unit[i : i + 1] for i in range(8)]
+        new = [tree([inv[i][j] * unit[j] for j in range(8)]) for i in range(8)]
         for r8, block in enumerate(blocks):
-            cols = [block[:, k + j : k + j + 1] for j in range(4)]
-            keep = jnp.where(in_panel, 0.0, block)
-            keep = keep - ((cols[0] * new[0] + cols[1] * new[1]) + (cols[2] * new[2] + cols[3] * new[3]))
-            if r8 == home:
-                for j in range(4):
-                    keep = jnp.where(row == off + j, new[j], keep)
-            out.append(keep)
-        blocks = out
+            if r8 != home:
+                keep = jnp.where(in_panel, 0.0, block)
+                blocks[r8] = keep - tree([block[:, k + j : k + j + 1] * new[j] for j in range(8)])
+        blocks[home] = jnp.concatenate(new, axis=0)
     return jnp.concatenate(blocks, axis=0)
 
 
@@ -122,8 +140,9 @@
 def put_rows(ref, grid_ref, g, base, out):
     lons = grid_ref.shape[1]
     cells = ref.shape[1] - 16
-    for p in range(PIECES):
-        ref[g * PIECES + p, 0:cells, :] = out[p * cells : (p + 1) * cells]
+    pieces = out.shape[0] // cells
+    for p in range(pieces):
+        ref[g * pieces + p, 0:cells, :] = out[p * cells : (p + 1) * cells]
     for p in range(out.shape[0] // lons):
         grid_ref[base + p] = out[p * lons : (p + 1) * lons]
 
@@ -298,7 +317,7 @@
     pairs = [(shelf_hbm.at[pl.ds(0, lats)], coded_ref), (modes_hbm.at[pl.ds((2 + half) * lats, lats)], spatial_ref)]
     loads = fetch(pairs, sems)
     spokes = ref.shape[0]
-    many = PIECES * lats // spokes
+    many = DAYS_PIECES * lats // spokes
     if mine:
         temporal = sums_ref[...]
     else:
@@ -319,7 +338,7 @@
         put_rows(ref, grid_ref, g, g * many, times(split(jnp.where(coded == GAP, guess, coded)), side))
         return _
 
-    lax.fori_loop(0, spokes // PIECES, step, 0)
+    lax.fori_loop(0, spokes // DAYS_PIECES, step, 0)
     put_block(half, grid_ref, gram_ref, ref)
 
 

time: 288 us -> 283 us (0.983)
  Pallas kernels: 49.7 us -> 44.5 us
  transfers between devices with their start and end apart: 7 -> 7, of which waited for: 6 -> 6; matrix products, arithmetic and copies ran while one was open for 0% -> 0% of each run, Pallas kernels for 3% -> 2%
where the time goes in v5:
time: 283 us; the launch traced here: 282 us
  blocking collectives  167 us (59%)
  waiting for transfers between devices  46.4 us (16%)
  Pallas kernels  44.5 us (16%)
  starting transfers between devices  20 us (7%)
  other arithmetic  2.86 us (1%)
    all_to_all x4, blocking collectives, gather_all(): return lax.all_to_all(spread, axes, 0, 0, tiled=True)  94.1 us
    all_to_all x2, blocking collectives, sum_cells(): lax.all_to_all(value.reshape(size, rows // size, -1), LL, 0, 0, tiled=True)  38.4 us
    all_to_all x1, blocking collectives, on_device(): shard = jnp.sum(lax.all_to_all(half, YZ, 0, 0, tiled=True), axis=0)  34.6 us
    all_to_all x1, waiting for transfers between devices, on_device(): shard = jnp.sum(lax.all_to_all(half, YZ, 0, 0, tiled=True), axis=0)  29.1 us
    pallas_call x2, Pallas kernels, modes_call(): call(functools.partial(modes_kernel, first), outs, specs, scratch, 'modes...  21.2 us
    ppermute x2, waiting for transfers between devices, on_device(): halo = lax.ppermute(send, ALL, pairs)  11.4 us
    all_to_all x1, starting transfers between devices, on_device(): shard = jnp.sum(lax.all_to_all(half, YZ, 0, 0, tiled=True), axis=0)  9.5 us
    pallas_call x2, Pallas kernels, first_call(): call(functools.partial(first_kernel, mine), outs, specs, scratch, 'first_...  9.34 us
  transfers between devices with their start and end apart: 7, of which 6 were waited for; matrix products, arithmetic and copies ran while one was open for 0% of the time, Pallas kernels for 2%

profile of v5, /device:TPU:8, one launch (start us, length us, event | category | flops | bytes accessed | tf_op | source)
XLA Modules:
  0.0 282.2 jit_solution(5746156922140091143)
XLA Ops:
  0.6 4.7 %first_projection.3 = (f32[16,144,128]{2,1,0:T(8,128)}, f32[384,64,128]{2,1,0:T(8,128)}) custom-call(s32[1,1]{1,0:T(1,128)} %bitcast.core_ref, f32[64,64,128]{2,1,0:T(8,128)} %anomaly_hbm.3, s32[64,64,128]{2,1,0:T(8,128)} %observed_hbm.3, s32[64,64]{1,0:T(8,128)} %mask_hbm.3, f32[128,128]{1,0:T(8,128)} %days_ref.1), custom_call_target="tpu_custom_call" | custom-call | flops 1000000000 | bytes 10000000 | tf_op jit(solution)/shard_map/first_projection/pallas_call | solution.py:380
  5.4 1.9 collective-permute-start
  7.3 4.6 %first_projection.2 = (f32[16,144,128]{2,1,0:T(8,128)}, f32[384,64,128]{2,1,0:T(8,128)}) custom-call(s32[1,1]{1,0:T(1,128)} %bitcast.core_ref, f32[64,64,128]{2,1,0:T(8,128)} %anomaly_hbm.3, s32[64,64,128]{2,1,0:T(8,128)} %observed_hbm.3, s32[64,64]{1,0:T(8,128)} %mask_hbm.3, f32[128,128]{1,0:T(8,128)} %days_ref.1), custom_call_target="tpu_custom_call" | custom-call | flops 1000000000 | bytes 10000000 | tf_op jit(solution)/shard_map/first_projection/pallas_call | solution.py:380
  11.9 0.0 collective-permute-done
  11.9 2.4 add.60
  14.3 0.0 copy-start.1
  14.3 9.5 %all-to-all-start = ((f32[16,144,128]{2,1,0:T(8,128)}), f32[16,144,128]{2,1,0:T(8,128)S(1)}, u32[]{:S(2)}, u32[]{:S(2)}) async-start(f32[16,144,128]{2,1,0:T(8,128)} %add.60), calls=%async_computation | async-start | bytes 2359296 | tf_op jit(solution)/shard_map/all_to_all | solution.py:482
  23.8 0.0 copy-done.1
  23.9 0.2 slice_reduce_fusion
  24.1 0.1 concatenate.12
  24.2 0.1 dynamic_slice.3
  24.3 0.1 pad.7.clone
  24.3 29.1 %all-to-all-done = f32[16,144,128]{2,1,0:T(8,128)S(1)} async-done(((f32[16,144,128]{2,1,0:T(8,128)}), f32[16,144,128]{2,1,0:T(8,128)S(1)}, u32[]{:S(2)}, u32[]{:S(2)}) %all-to-all-start) | async-done | bytes 1179680 | tf_op jit(solution)/shard_map/all_to_all | solution.py:482
  53.4 0.1 reduce_sum.36
  53.5 0.1 pad_maximum_fusion.2
  53.6 1.3 collective-permute-start.1
  54.9 6.3 %collective-permute-done.1 = f32[16,128]{1,0:T(8,128)S(1)} collective-permute-done((f32[16,128]{1,0:T(8,128)S(1)}, f32[16,128]{1,0:T(8,128)S(1)}, u32[]{:S(2)}, u32[]{:S(2)}) %collective-permute-start.1) | collective-permute-done | bytes 8224 | tf_op jit(solution)/shard_map/ppermute | solution.py:486
  61.2 0.1 broadcast_in_dim.11
  61.3 0.0 copy-start
  61.3 35.4 %all_to_all.40.here_ref = f32[16,152,128]{2,1,0:T(8,128)S(1)} all-to-all(f32[16,152,128]{2,1,0:T(8,128)S(1)} %broadcast_in_dim.11), channel_id=1, replica_groups=mesh['lat'=4,'lon'=4,'zlo'=2,'y'=8,'core'=2] {'zlo','y'}, dimensions={0} | all-to-all | bytes 2490368 | tf_op jit(solution)/shard_map/all_to_all | solution.py:444
  96.7 1.9 collective-permute-start.2
  98.6 0.1 multiply_divide_fusion.weight_ref
  98.7 2.8 %collective-permute-done.2.there_ref = f32[16,152,128]{2,1,0:T(8,128)S(1)} collective-permute-done((f32[16,152,128]{2,1,0:T(8,128)S(1)}, f32[16,152,128]{2,1,0:T(8,128)S(1)}, u32[]{:S(2)}, u32[]{:S(2)}) %collective-permute-start.2) | collective-permute-done | bytes 1245216 | tf_op jit(solution)/shard_map/ppermute | solution.py:422
  101.5 0.0 copy-done
  101.6 11.3 %modes_sweep.2 = (f32[384,64,128]{2,1,0:T(8,128)}, f32[256,128]{1,0:T(8,128)S(1)}) custom-call(s32[1,1]{1,0:T(1,128)} %bitcast.core_ref, f32[1,64]{1,0:T(1,128)S(1)} %multiply_divide_fusion.weight_ref, f32[16,152,128]{2,1,0:T(8,128)S(1)} %all_to_all.40.here_ref, f32[16,152,128]{2,1,0:T(8,128)S(1)} %collective-permute-done.2.there_ref, ...), custom_call_target="tpu_custom_call" | custom-call | flops 2000000000 | bytes 10000000 | tf_op jit(solution)/shard_map/modes_sweep/pallas_call | solution.py:393
  112.8 22.4 %all_to_all.41 = f32[16,16,128]{2,1,0:T(8,128)S(1)} all-to-all(f32[16,16,128]{2,1,0:T(8,128)S(1)} %bitcast.12), channel_id=1, replica_groups=mesh['lat'=4,'lon'=4,'zlo'=2,'y'=8,'core'=2] {'lat','lon'}, dimensions={0} | all-to-all | bytes 262144 | tf_op jit(solution)/shard_map/all_to_all | solution.py:450
  135.2 13.7 %all_to_all.42 = f32[16,16,128]{2,1,0:T(8,128)S(1)} all-to-all(f32[16,16,128]{2,1,0:T(8,128)S(1)} %broadcast_in_dim.12), channel_id=1, replica_groups=mesh['lat'=4,'lon'=4,'zlo'=2,'y'=8,'core'=2] {'lat','lon'}, dimensions={0} | all-to-all | bytes 262144 | tf_op jit(solution)/shard_map/all_to_all | solution.py:444
  149.0 6.7 %days_sweep.2 = (f32[16,144,128]{2,1,0:T(8,128)S(1)}, f32[128,128]{1,0:T(8,128)S(1)}) custom-call(s32[1,1]{1,0:T(1,128)} %bitcast.core_ref, f32[256,128]{1,0:T(8,128)S(1)} %bitcast.9, f32[384,64,128]{2,1,0:T(8,128)} %get-tuple-element.15.refs_1_.shelf_hbm, f32[384,64,128]{2,1,0:T(8,128)} %get-tuple-element.17.modes_hbm.refs_2_), custom_call_target="tpu_custom_call" | custom-call | flops 2000000000 | bytes 10000000 | tf_op jit(solution)/shard_map/days_sweep/pallas_call | solution.py:404
  155.7 1.9 collective-permute-start.3
  157.6 2.4 days_sweep.3
  160.0 0.4 collective-permute-done.3
  160.4 0.2 add.64
  160.6 34.6 %all_to_all.43 = f32[16,144,128]{2,1,0:T(8,128)S(1)} all-to-all(f32[16,144,128]{2,1,0:T(8,128)S(1)} %add.64), channel_id=1, replica_groups=mesh['lat'=4,'lon'=4,'zlo'=2,'y'=8,'core'=2] {'zlo','y'}, dimensions={0} | all-to-all | bytes 2359296 | tf_op jit(solution)/shard_map/all_to_all | solution.py:482
  195.1 0.1 reduce_sum.38
  195.2 1.3 collective-permute-start.4
  196.5 5.1 %collective-permute-done.4 = f32[8,128]{1,0:T(8,128)S(1)} collective-permute-done((f32[8,128]{1,0:T(8,128)S(1)}, f32[8,128]{1,0:T(8,128)S(1)}, u32[]{:S(2)}, u32[]{:S(2)}) %collective-permute-start.4) | collective-permute-done | bytes 4128 | tf_op jit(solution)/shard_map/ppermute | solution.py:486
  201.6 0.1 broadcast_in_dim.13
  201.7 31.2 %all_to_all.44.here_ref = f32[16,144,128]{2,1,0:T(8,128)S(1)} all-to-all(f32[16,144,128]{2,1,0:T(8,128)S(1)} %broadcast_in_dim.13), channel_id=1, replica_groups=mesh['lat'=4,'lon'=4,'zlo'=2,'y'=8,'core'=2] {'zlo','y'}, dimensions={0} | all-to-all | bytes 2359296 | tf_op jit(solution)/shard_map/all_to_all | solution.py:444
  232.9 2.1 collective-permute-start.5
  235.0 2.6 collective-permute-done.5.there_ref
  237.6 10.0 %modes_sweep.3 = (f32[64,64,128]{2,1,0:T(8,128)}, f32[256,128]{1,0:T(8,128)S(1)}) custom-call(s32[1,1]{1,0:T(1,128)} %bitcast.core_ref, f32[1,64]{1,0:T(1,128)S(1)} %multiply_divide_fusion.weight_ref, f32[16,144,128]{2,1,0:T(8,128)S(1)} %all_to_all.44.here_ref, f32[16,144,128]{2,1,0:T(8,128)S(1)} %collective-permute-done.5.there_ref, ...), custom_call_target="tpu_custom_call" | custom-call | flops 2000000000 | bytes 10000000 | tf_op jit(solution)/shard_map/modes_sweep/pallas_call | solution.py:393
  247.6 16.0 %all_to_all.45 = f32[16,16,128]{2,1,0:T(8,128)S(1)} all-to-all(f32[16,16,128]{2,1,0:T(8,128)S(1)} %bitcast.11), channel_id=1, replica_groups=mesh['lat'=4,'lon'=4,'zlo'=2,'y'=8,'core'=2] {'lat','lon'}, dimensions={0} | all-to-all | bytes 262144 | tf_op jit(solution)/shard_map/all_to_all | solution.py:450
  263.6 13.7 %all_to_all.46 = f32[16,16,128]{2,1,0:T(8,128)S(1)} all-to-all(f32[16,16,128]{2,1,0:T(8,128)S(1)} %broadcast_in_dim.14), channel_id=1, replica_groups=mesh['lat'=4,'lon'=4,'zlo'=2,'y'=8,'core'=2] {'lat','lon'}, dimensions={0} | all-to-all | bytes 262144 | tf_op jit(solution)/shard_map/all_to_all | solution.py:444
  277.3 4.9 %last_days.1 = f32[128,128]{1,0:T(8,128)} custom-call(f32[256,128]{1,0:T(8,128)S(1)} %bitcast.10), custom_call_target="tpu_custom_call" | custom-call | flops 10000000 | bytes 1000000 | tf_op jit(solution)/shard_map/last_days/pallas_call | solution.py:411
  (12 shorter events, 0.1 us)
Async XLA Ops:
  5.4 6.6 %collective-permute-start = (f32[16,144,128]{2,1,0:T(8,128)}, f32[16,144,128]{2,1,0:T(8,128)S(1)}, u32[]{:S(2)}, u32[]{:S(2)}) collective-permute-start(f32[16,144,128]{2,1,0:T(8,128)} %get-tuple-element.13), channel_id=1, source_target_pairs={{0,1},{1,0},{2,3},{3,2},{4,5},{5,4},{6,7},{7,6},{8,9},{9,8},{10,11... | collective-permute-start | bytes 3538952 | tf_op jit(solution)/shard_map/ppermute | solution.py:422
  14.3 9.5 %copy-start.1 = (s32[64,64]{1,0:T(8,128)S(1)}, s32[64,64]{1,0:T(8,128)}, u32[]{:S(2)}) copy-start(s32[64,64]{1,0:T(8,128)} %mask_hbm.3) | copy-start | bytes 49156
  14.3 39.1 %all-to-all-start = ((f32[16,144,128]{2,1,0:T(8,128)}), f32[16,144,128]{2,1,0:T(8,128)S(1)}, u32[]{:S(2)}, u32[]{:S(2)}) async-start(f32[16,144,128]{2,1,0:T(8,128)} %add.60), calls=%async_computation | async-start | bytes 2359296 | tf_op jit(solution)/shard_map/all_to_all | solution.py:482
  53.6 7.7 %collective-permute-start.1 = (f32[16,128]{1,0:T(8,128)S(1)}, f32[16,128]{1,0:T(8,128)S(1)}, u32[]{:S(2)}, u32[]{:S(2)}) collective-permute-start(f32[16,128]{1,0:T(8,128)S(1)} %pad_maximum_fusion.2), channel_id=1, source_target_pairs={{1,129},{3,131},{5,133},{7,135},{9,137},{11,139},{13,141},{15,143}... | collective-permute-start | bytes 24584 | tf_op jit(solution)/shard_map/ppermute | solution.py:486
  61.3 40.3 %copy-start = (f32[128,128]{1,0:T(8,128)S(1)}, f32[128,128]{1,0:T(8,128)}, u32[]{:S(2)}) copy-start(f32[128,128]{1,0:T(8,128)} %days_ref.1) | copy-start | bytes 196612
  96.7 4.8 %collective-permute-start.2 = (f32[16,152,128]{2,1,0:T(8,128)S(1)}, f32[16,152,128]{2,1,0:T(8,128)S(1)}, u32[]{:S(2)}, u32[]{:S(2)}) collective-permute-start(f32[16,152,128]{2,1,0:T(8,128)S(1)} %all_to_all.40.here_ref), channel_id=1, source_target_pairs={{0,1},{1,0},{2,3},{3,2},{4,5},{5,4},{6,7},{7,6},{8,9},{9,8},{10,11... | collective-permute-start | bytes 3735560 | tf_op jit(solution)/shard_map/ppermute | solution.py:422
  155.7 4.7 %collective-permute-start.3 = (f32[16,144,128]{2,1,0:T(8,128)S(1)}, f32[16,144,128]{2,1,0:T(8,128)S(1)}, u32[]{:S(2)}, u32[]{:S(2)}) collective-permute-start(f32[16,144,128]{2,1,0:T(8,128)S(1)} %get-tuple-element.19), channel_id=1, source_target_pairs={{0,1},{1,0},{2,3},{3,2},{4,5},{5,4},{6,7},{7,6},{8,9},{9,8},{10,11... | collective-permute-start | bytes 3538952 | tf_op jit(solution)/shard_map/ppermute | solution.py:422
  195.2 6.4 %collective-permute-start.4 = (f32[8,128]{1,0:T(8,128)S(1)}, f32[8,128]{1,0:T(8,128)S(1)}, u32[]{:S(2)}, u32[]{:S(2)}) collective-permute-start(f32[8,128]{1,0:T(8,128)S(1)} %get-tuple-element.26), channel_id=1, source_target_pairs={{1,129},{3,131},{5,133},{7,135},{9,137},{11,139},{13,141},{15,143}... | collective-permute-start | bytes 12296 | tf_op jit(solution)/shard_map/ppermute | solution.py:486
  232.9 4.7 %collective-permute-start.5 = (f32[16,144,128]{2,1,0:T(8,128)S(1)}, f32[16,144,128]{2,1,0:T(8,128)S(1)}, u32[]{:S(2)}, u32[]{:S(2)}) collective-permute-start(f32[16,144,128]{2,1,0:T(8,128)S(1)} %all_to_all.44.here_ref), channel_id=1, source_target_pairs={{0,1},{1,0},{2,3},{3,2},{4,5},{5,4},{6,7},{7,6},{8,9},{9,8},{10,11... | collective-permute-start | bytes 3538952 | tf_op jit(solution)/shard_map/ppermute | solution.py:422

commit v6 on v5

--- a/solution.py
+++ b/solution.py
@@ -19,7 +19,7 @@
 GAP = 1e30
 PIECES = 8
 DAYS_PIECES = 16
-GROUP = 16
+GROUP = 32
 FIRST_ROOM = 57
 ROOM = 50
 SHELF = 384

time: 283 us -> 279 us (0.986)
  Pallas kernels: 44.5 us -> 40.7 us
    pallas_call x2, Pallas kernels: 21.2 us -> 17.4 us  [modes_call(): call(functools.partial(modes_kernel, first), outs, specs, scratch, 'modes...]
  transfers between devices with their start and end apart: 7 -> 7, of which waited for: 6 -> 6; matrix products, arithmetic and copies ran while one was open for 0% -> 0% of each run, Pallas kernels for 2% -> 3%
where the time goes in v6:
time: 279 us; the launch traced here: 278 us
  blocking collectives  167 us (60%)
  waiting for transfers between devices  46.4 us (17%)
  Pallas kernels  40.7 us (15%)
  starting transfers between devices  20 us (7%)
  other arithmetic  2.86 us (1%)
    all_to_all x4, blocking collectives, gather_all(): return lax.all_to_all(spread, axes, 0, 0, tiled=True)  94.1 us
    all_to_all x2, blocking collectives, sum_cells(): lax.all_to_all(value.reshape(size, rows // size, -1), LL, 0, 0, tiled=True)  38.3 us
    all_to_all x1, blocking collectives, on_device(): shard = jnp.sum(lax.all_to_all(half, YZ, 0, 0, tiled=True), axis=0)  34.6 us
    all_to_all x1, waiting for transfers between devices, on_device(): shard = jnp.sum(lax.all_to_all(half, YZ, 0, 0, tiled=True), axis=0)  29.1 us
    pallas_call x2, Pallas kernels, modes_call(): call(functools.partial(modes_kernel, first), outs, specs, scratch, 'modes...  17.4 us
    ppermute x2, waiting for transfers between devices, on_device(): halo = lax.ppermute(send, ALL, pairs)  11.4 us
    all_to_all x1, starting transfers between devices, on_device(): shard = jnp.sum(lax.all_to_all(half, YZ, 0, 0, tiled=True), axis=0)  9.5 us
    pallas_call x2, Pallas kernels, first_call(): call(functools.partial(first_kernel, mine), outs, specs, scratch, 'first_...  9.34 us
  transfers between devices with their start and end apart: 7, of which 6 were waited for; matrix products, arithmetic and copies ran while one was open for 0% of the time, Pallas kernels for 3%

profile of v6, /device:TPU:8, one launch (start us, length us, event | category | flops | bytes accessed | tf_op | source)
XLA Modules:
  0.0 278.4 jit_solution(11041018454631940364)
XLA Ops:
  0.6 4.7 %first_projection.3 = (f32[16,144,128]{2,1,0:T(8,128)}, f32[384,64,128]{2,1,0:T(8,128)}) custom-call(s32[1,1]{1,0:T(1,128)} %bitcast.core_ref, f32[64,64,128]{2,1,0:T(8,128)} %anomaly_hbm.3, s32[64,64,128]{2,1,0:T(8,128)} %observed_hbm.3, s32[64,64]{1,0:T(8,128)} %mask_hbm.3, f32[128,128]{1,0:T(8,128)} %days_ref.1), custom_call_target="tpu_custom_call" | custom-call | flops 1000000000 | bytes 10000000 | tf_op jit(solution)/shard_map/first_projection/pallas_call | solution.py:380
  5.4 1.9 collective-permute-start
  7.3 4.6 %first_projection.2 = (f32[16,144,128]{2,1,0:T(8,128)}, f32[384,64,128]{2,1,0:T(8,128)}) custom-call(s32[1,1]{1,0:T(1,128)} %bitcast.core_ref, f32[64,64,128]{2,1,0:T(8,128)} %anomaly_hbm.3, s32[64,64,128]{2,1,0:T(8,128)} %observed_hbm.3, s32[64,64]{1,0:T(8,128)} %mask_hbm.3, f32[128,128]{1,0:T(8,128)} %days_ref.1), custom_call_target="tpu_custom_call" | custom-call | flops 1000000000 | bytes 10000000 | tf_op jit(solution)/shard_map/first_projection/pallas_call | solution.py:380
  11.9 0.0 collective-permute-done
  11.9 2.4 add.60
  14.3 0.0 copy-start.1
  14.3 9.5 %all-to-all-start = ((f32[16,144,128]{2,1,0:T(8,128)}), f32[16,144,128]{2,1,0:T(8,128)S(1)}, u32[]{:S(2)}, u32[]{:S(2)}) async-start(f32[16,144,128]{2,1,0:T(8,128)} %add.60), calls=%async_computation | async-start | bytes 2359296 | tf_op jit(solution)/shard_map/all_to_all | solution.py:482
  23.8 0.0 copy-done.1
  23.9 0.2 slice_reduce_fusion
  24.1 0.1 concatenate.12
  24.2 0.1 dynamic_slice.3
  24.3 0.1 pad.7.clone
  24.3 29.1 %all-to-all-done = f32[16,144,128]{2,1,0:T(8,128)S(1)} async-done(((f32[16,144,128]{2,1,0:T(8,128)}), f32[16,144,128]{2,1,0:T(8,128)S(1)}, u32[]{:S(2)}, u32[]{:S(2)}) %all-to-all-start) | async-done | bytes 1179680 | tf_op jit(solution)/shard_map/all_to_all | solution.py:482
  53.4 0.1 reduce_sum.36
  53.5 0.1 pad_maximum_fusion.2
  53.6 1.3 collective-permute-start.1
  54.9 6.3 %collective-permute-done.1 = f32[16,128]{1,0:T(8,128)S(1)} collective-permute-done((f32[16,128]{1,0:T(8,128)S(1)}, f32[16,128]{1,0:T(8,128)S(1)}, u32[]{:S(2)}, u32[]{:S(2)}) %collective-permute-start.1) | collective-permute-done | bytes 8224 | tf_op jit(solution)/shard_map/ppermute | solution.py:486
  61.2 0.1 broadcast_in_dim.11
  61.3 0.0 copy-start
  61.3 35.4 %all_to_all.40.here_ref = f32[16,152,128]{2,1,0:T(8,128)S(1)} all-to-all(f32[16,152,128]{2,1,0:T(8,128)S(1)} %broadcast_in_dim.11), channel_id=1, replica_groups=mesh['lat'=4,'lon'=4,'zlo'=2,'y'=8,'core'=2] {'zlo','y'}, dimensions={0} | all-to-all | bytes 2490368 | tf_op jit(solution)/shard_map/all_to_all | solution.py:444
  96.7 1.9 collective-permute-start.2
  98.6 0.1 multiply_divide_fusion.weight_ref
  98.7 2.8 %collective-permute-done.2.there_ref = f32[16,152,128]{2,1,0:T(8,128)S(1)} collective-permute-done((f32[16,152,128]{2,1,0:T(8,128)S(1)}, f32[16,152,128]{2,1,0:T(8,128)S(1)}, u32[]{:S(2)}, u32[]{:S(2)}) %collective-permute-start.2) | collective-permute-done | bytes 1245216 | tf_op jit(solution)/shard_map/ppermute | solution.py:422
  101.5 0.0 copy-done
  101.6 9.4 %modes_sweep.2 = (f32[384,64,128]{2,1,0:T(8,128)}, f32[256,128]{1,0:T(8,128)S(1)}) custom-call(s32[1,1]{1,0:T(1,128)} %bitcast.core_ref, f32[1,64]{1,0:T(1,128)S(1)} %multiply_divide_fusion.weight_ref, f32[16,152,128]{2,1,0:T(8,128)S(1)} %all_to_all.40.here_ref, f32[16,152,128]{2,1,0:T(8,128)S(1)} %collective-permute-done.2.there_ref, ...), custom_call_target="tpu_custom_call" | custom-call | flops 2000000000 | bytes 10000000 | tf_op jit(solution)/shard_map/modes_sweep/pallas_call | solution.py:393
  110.9 22.4 %all_to_all.41 = f32[16,16,128]{2,1,0:T(8,128)S(1)} all-to-all(f32[16,16,128]{2,1,0:T(8,128)S(1)} %bitcast.12), channel_id=1, replica_groups=mesh['lat'=4,'lon'=4,'zlo'=2,'y'=8,'core'=2] {'lat','lon'}, dimensions={0} | all-to-all | bytes 262144 | tf_op jit(solution)/shard_map/all_to_all | solution.py:450
  133.3 13.7 %all_to_all.42 = f32[16,16,128]{2,1,0:T(8,128)S(1)} all-to-all(f32[16,16,128]{2,1,0:T(8,128)S(1)} %broadcast_in_dim.12), channel_id=1, replica_groups=mesh['lat'=4,'lon'=4,'zlo'=2,'y'=8,'core'=2] {'lat','lon'}, dimensions={0} | all-to-all | bytes 262144 | tf_op jit(solution)/shard_map/all_to_all | solution.py:444
  147.1 6.7 %days_sweep.2 = (f32[16,144,128]{2,1,0:T(8,128)S(1)}, f32[128,128]{1,0:T(8,128)S(1)}) custom-call(s32[1,1]{1,0:T(1,128)} %bitcast.core_ref, f32[256,128]{1,0:T(8,128)S(1)} %bitcast.9, f32[384,64,128]{2,1,0:T(8,128)} %get-tuple-element.15.refs_1_.shelf_hbm, f32[384,64,128]{2,1,0:T(8,128)} %get-tuple-element.17.modes_hbm.refs_2_), custom_call_target="tpu_custom_call" | custom-call | flops 2000000000 | bytes 10000000 | tf_op jit(solution)/shard_map/days_sweep/pallas_call | solution.py:404
  153.8 1.9 collective-permute-start.3
  155.7 2.4 days_sweep.3
  158.1 0.4 collective-permute-done.3
  158.5 0.2 add.64
  158.7 34.6 %all_to_all.43 = f32[16,144,128]{2,1,0:T(8,128)S(1)} all-to-all(f32[16,144,128]{2,1,0:T(8,128)S(1)} %add.64), channel_id=1, replica_groups=mesh['lat'=4,'lon'=4,'zlo'=2,'y'=8,'core'=2] {'zlo','y'}, dimensions={0} | all-to-all | bytes 2359296 | tf_op jit(solution)/shard_map/all_to_all | solution.py:482
  193.3 0.1 reduce_sum.38
  193.3 1.3 collective-permute-start.4
  194.6 5.1 %collective-permute-done.4 = f32[8,128]{1,0:T(8,128)S(1)} collective-permute-done((f32[8,128]{1,0:T(8,128)S(1)}, f32[8,128]{1,0:T(8,128)S(1)}, u32[]{:S(2)}, u32[]{:S(2)}) %collective-permute-start.4) | collective-permute-done | bytes 4128 | tf_op jit(solution)/shard_map/ppermute | solution.py:486
  199.7 0.1 broadcast_in_dim.13
  199.8 31.2 %all_to_all.44.here_ref = f32[16,144,128]{2,1,0:T(8,128)S(1)} all-to-all(f32[16,144,128]{2,1,0:T(8,128)S(1)} %broadcast_in_dim.13), channel_id=1, replica_groups=mesh['lat'=4,'lon'=4,'zlo'=2,'y'=8,'core'=2] {'zlo','y'}, dimensions={0} | all-to-all | bytes 2359296 | tf_op jit(solution)/shard_map/all_to_all | solution.py:444
  231.0 2.1 collective-permute-start.5
  233.1 2.6 collective-permute-done.5.there_ref
  235.7 8.0 %modes_sweep.3 = (f32[64,64,128]{2,1,0:T(8,128)}, f32[256,128]{1,0:T(8,128)S(1)}) custom-call(s32[1,1]{1,0:T(1,128)} %bitcast.core_ref, f32[1,64]{1,0:T(1,128)S(1)} %multiply_divide_fusion.weight_ref, f32[16,144,128]{2,1,0:T(8,128)S(1)} %all_to_all.44.here_ref, f32[16,144,128]{2,1,0:T(8,128)S(1)} %collective-permute-done.5.there_ref, ...), custom_call_target="tpu_custom_call" | custom-call | flops 2000000000 | bytes 10000000 | tf_op jit(solution)/shard_map/modes_sweep/pallas_call | solution.py:393
  243.8 16.0 %all_to_all.45 = f32[16,16,128]{2,1,0:T(8,128)S(1)} all-to-all(f32[16,16,128]{2,1,0:T(8,128)S(1)} %bitcast.11), channel_id=1, replica_groups=mesh['lat'=4,'lon'=4,'zlo'=2,'y'=8,'core'=2] {'lat','lon'}, dimensions={0} | all-to-all | bytes 262144 | tf_op jit(solution)/shard_map/all_to_all | solution.py:450
  259.8 13.7 %all_to_all.46 = f32[16,16,128]{2,1,0:T(8,128)S(1)} all-to-all(f32[16,16,128]{2,1,0:T(8,128)S(1)} %broadcast_in_dim.14), channel_id=1, replica_groups=mesh['lat'=4,'lon'=4,'zlo'=2,'y'=8,'core'=2] {'lat','lon'}, dimensions={0} | all-to-all | bytes 262144 | tf_op jit(solution)/shard_map/all_to_all | solution.py:444
  273.5 4.9 %last_days.1 = f32[128,128]{1,0:T(8,128)} custom-call(f32[256,128]{1,0:T(8,128)S(1)} %bitcast.10), custom_call_target="tpu_custom_call" | custom-call | flops 10000000 | bytes 1000000 | tf_op jit(solution)/shard_map/last_days/pallas_call | solution.py:411
  (12 shorter events, 0.1 us)
Async XLA Ops:
  5.4 6.6 %collective-permute-start = (f32[16,144,128]{2,1,0:T(8,128)}, f32[16,144,128]{2,1,0:T(8,128)S(1)}, u32[]{:S(2)}, u32[]{:S(2)}) collective-permute-start(f32[16,144,128]{2,1,0:T(8,128)} %get-tuple-element.13), channel_id=1, source_target_pairs={{0,1},{1,0},{2,3},{3,2},{4,5},{5,4},{6,7},{7,6},{8,9},{9,8},{10,11... | collective-permute-start | bytes 3538952 | tf_op jit(solution)/shard_map/ppermute | solution.py:422
  14.3 9.5 %copy-start.1 = (s32[64,64]{1,0:T(8,128)S(1)}, s32[64,64]{1,0:T(8,128)}, u32[]{:S(2)}) copy-start(s32[64,64]{1,0:T(8,128)} %mask_hbm.3) | copy-start | bytes 49156
  14.3 39.1 %all-to-all-start = ((f32[16,144,128]{2,1,0:T(8,128)}), f32[16,144,128]{2,1,0:T(8,128)S(1)}, u32[]{:S(2)}, u32[]{:S(2)}) async-start(f32[16,144,128]{2,1,0:T(8,128)} %add.60), calls=%async_computation | async-start | bytes 2359296 | tf_op jit(solution)/shard_map/all_to_all | solution.py:482
  53.6 7.7 %collective-permute-start.1 = (f32[16,128]{1,0:T(8,128)S(1)}, f32[16,128]{1,0:T(8,128)S(1)}, u32[]{:S(2)}, u32[]{:S(2)}) collective-permute-start(f32[16,128]{1,0:T(8,128)S(1)} %pad_maximum_fusion.2), channel_id=1, source_target_pairs={{1,129},{3,131},{5,133},{7,135},{9,137},{11,139},{13,141},{15,143}... | collective-permute-start | bytes 24584 | tf_op jit(solution)/shard_map/ppermute | solution.py:486
  61.3 40.3 %copy-start = (f32[128,128]{1,0:T(8,128)S(1)}, f32[128,128]{1,0:T(8,128)}, u32[]{:S(2)}) copy-start(f32[128,128]{1,0:T(8,128)} %days_ref.1) | copy-start | bytes 196612
  96.7 4.8 %collective-permute-start.2 = (f32[16,152,128]{2,1,0:T(8,128)S(1)}, f32[16,152,128]{2,1,0:T(8,128)S(1)}, u32[]{:S(2)}, u32[]{:S(2)}) collective-permute-start(f32[16,152,128]{2,1,0:T(8,128)S(1)} %all_to_all.40.here_ref), channel_id=1, source_target_pairs={{0,1},{1,0},{2,3},{3,2},{4,5},{5,4},{6,7},{7,6},{8,9},{9,8},{10,11... | collective-permute-start | bytes 3735560 | tf_op jit(solution)/shard_map/ppermute | solution.py:422
  153.8 4.7 %collective-permute-start.3 = (f32[16,144,128]{2,1,0:T(8,128)S(1)}, f32[16,144,128]{2,1,0:T(8,128)S(1)}, u32[]{:S(2)}, u32[]{:S(2)}) collective-permute-start(f32[16,144,128]{2,1,0:T(8,128)S(1)} %get-tuple-element.19), channel_id=1, source_target_pairs={{0,1},{1,0},{2,3},{3,2},{4,5},{5,4},{6,7},{7,6},{8,9},{9,8},{10,11... | collective-permute-start | bytes 3538952 | tf_op jit(solution)/shard_map/ppermute | solution.py:422
  193.3 6.4 %collective-permute-start.4 = (f32[8,128]{1,0:T(8,128)S(1)}, f32[8,128]{1,0:T(8,128)S(1)}, u32[]{:S(2)}, u32[]{:S(2)}) collective-permute-start(f32[8,128]{1,0:T(8,128)S(1)} %get-tuple-element.26), channel_id=1, source_target_pairs={{1,129},{3,131},{5,133},{7,135},{9,137},{11,139},{13,141},{15,143}... | collective-permute-start | bytes 12296 | tf_op jit(solution)/shard_map/ppermute | solution.py:486
  231.0 4.7 %collective-permute-start.5 = (f32[16,144,128]{2,1,0:T(8,128)S(1)}, f32[16,144,128]{2,1,0:T(8,128)S(1)}, u32[]{:S(2)}, u32[]{:S(2)}) collective-permute-start(f32[16,144,128]{2,1,0:T(8,128)S(1)} %all_to_all.44.here_ref), channel_id=1, source_target_pairs={{0,1},{1,0},{2,3},{3,2},{4,5},{5,4},{6,7},{7,6},{8,9},{9,8},{10,11... | collective-permute-start | bytes 3538952 | tf_op jit(solution)/shard_map/ppermute | solution.py:422
